TPU v7x, 128 devices: a whole 4x4x4 slice. The times are simulated.
128 devices in a mesh: ctx: 16 (over y, z_lo, core), fsdp: 8 (over z_hi, x).
Axes of the slice: x: 4, y: 4, z: 4 (z_hi: 2, z_lo: 2; z = z_hi * 2 + z_lo), core: 2. Of those that a mesh axis runs over, the one named last changes fastest.
Arguments:
- tokens: bfloat16 [8, 4096, 576], P('fsdp', 'ctx'), may hold values from -6 to 6
- block_order: int32 [32], replicated, may hold values from 0 to 31, as said below
- doc_ids: int32 [8, 4096], P('fsdp'), may hold values from 0 to 4, as said below
- norm_gains: bfloat16 [2, 2, 576], P(None, None, 'fsdp'), may hold values from 0.5 to 1.5
- w_qkv: bfloat16 [2, 576, 960], P(None, 'fsdp'), may hold values from -0.25 to 0.25
- w_out: bfloat16 [2, 576, 576], P(None, 'fsdp'), may hold values from -3 to 3
- w_gate_up: bfloat16 [2, 576, 3072], P(None, 'fsdp'), may hold values from -0.25 to 0.25
- w_down: bfloat16 [2, 1536, 576], P(None, 'fsdp'), may hold values from -0.15625 to 0.15625
- cotangent: bfloat16 [8, 4096, 576], P('fsdp', 'ctx'), may hold values from -6 to 6
Outputs:
- output: bfloat16 [8, 4096, 576], P('fsdp', 'ctx')
- input_grad: float32 [8, 4096, 576], P('fsdp', 'ctx')
- gain_grad: float32 [2, 2, 576], P(None, None, 'fsdp')
- qkv_grad: float32 [2, 576, 960], P(None, 'fsdp')
- out_proj_grad: float32 [2, 576, 576], P(None, 'fsdp')
- gate_up_grad: float32 [2, 576, 3072], P(None, 'fsdp')
- down_grad: float32 [2, 1536, 576], P(None, 'fsdp')
Inputs may be any that keep to these rules, and one draw needn't show every extreme that they name: `block_order`: entries 2 c and 2 c + 1 add up to 31, and every block number appears once. `doc_ids`: non-decreasing along each sequence; document 0 covers at least the first 2176 positions; the last position has id 4.
All inputs are finite; a program needn't handle non-finite values.
Results may differ from a plain program's by a relative error of at most 0.025.
Values may be sent and summed in bfloat16 or wider, within the bound.
No kernel may reach another device: no remote copies, remote signals or barrier semaphores. Data moves between devices by JAX's collectives and lax.ppermute only.
A program may use at most 192 MiB of HBM per device.

v0:
```python
import functools

import jax
import jax.numpy as jnp
from jax import lax
from jax.experimental import pallas as pl
from jax.experimental.pallas import tpu as pltpu
from jax.sharding import PartitionSpec as P

D = 576
HEADS = 9
KV_HEADS = 3
GROUP = 3
HEAD_DIM = 64
FF = 1536
LAYERS = 2
BLK = 128
NBLK = 32
EPS = 1e-05
THETA = 100000.0
NEG = -1e30
F32 = jnp.float32
BF16 = jnp.bfloat16
LANES = GROUP * BLK
CTX = 16
FSDP = 8
SHARD = D // FSDP
HALF = FF // 2
Q_ROWS = HEADS * HEAD_DIM
KV_ROWS = 2 * KV_HEADS * HEAD_DIM

PARTNER = [(i, i ^ 1) for i in range(CTX)]
SAME_CORE = [[2 * chip + core for chip in range(CTX // 2)] for core in range(2)]


def to_partner(x):
    return lax.ppermute(x, "ctx", PARTNER)


def over_chips(x):
    return lax.all_to_all(x, "ctx", 0, 0, axis_index_groups=SAME_CORE, tiled=True)


def over_fsdp(x):
    return lax.all_to_all(x, "fsdp", 0, 0, tiled=True)


def gather_fsdp(x):
    return over_fsdp(jnp.broadcast_to(x[None], (FSDP,) + x.shape)).reshape(-1, x.shape[1])


def scatter_fsdp(x):
    parts = over_fsdp(x.reshape(FSDP, -1, x.shape[1]))
    return jnp.sum(parts.astype(F32), 0).astype(BF16)


def sum_pair(a, b):
    return (a.astype(F32) + b.astype(F32)).astype(BF16)


def sum_chips(x):
    for bit in (2, 4, 8):
        x = sum_pair(x, lax.ppermute(x, "ctx", [(i, i ^ bit) for i in range(CTX)]))
    return x


def dot_tn(a, b):
    return lax.dot_general(a, b, (((0,), (0,)), ((), ())), preferred_element_type=F32)


def dot_nt(a, b):
    return lax.dot_general(a, b, (((1,), (1,)), ((), ())), preferred_element_type=F32)


UNROLL_F = 9
UNROLL_B = 3
CHUNK = 4
KEYS = CHUNK * BLK
CHUNKS = NBLK // CHUNK


def fill_keys(sc, own_ref, other_ref, kv_s):
    core = sc[2]
    for chip in range(CTX // 2):
        for half in range(2):
            lanes = slice(half * BLK, (half + 1) * BLK)
            block = sc[7 + 2 * (2 * chip + core) + half]
            kv_s[block] = own_ref[chip, :, 0, :, lanes]
            block = sc[7 + 2 * (2 * chip + 1 - core) + half]
            kv_s[block] = other_ref[chip, :, 0, :, lanes]


def fill_queries(sc, src_ref, dst):
    for half in range(2):
        lanes = slice(half * BLK, (half + 1) * BLK)
        which = jnp.bitwise_xor(half, sc[1])
        dst[which] = jnp.concatenate([src_ref[j, :, lanes] for j in range(GROUP)], axis=1)


def query_rows(sc, which):
    block = jnp.where(which == 0, sc[0], NBLK - 1 - sc[0])
    lane = lax.broadcasted_iota(jnp.int32, (1, LANES), 1)
    pos = block * BLK + jnp.bitwise_and(lane, BLK - 1)
    start = jnp.zeros((1, LANES), jnp.int32)
    for d in range(4):
        start = jnp.where(pos >= sc[3 + d], jnp.maximum(start, sc[3 + d]), start)
    return pos, start


def chunk_of(sc, t):
    high = (NBLK - sc[0] + CHUNK - 1) // CHUNK
    which = (t < high).astype(jnp.int32)
    return which, jnp.where(t < high, t, t - high)


def keys_of(kv_s, chunk, kind):
    return jnp.concatenate([kv_s[chunk * CHUNK + j, kind] for j in range(CHUNK)], axis=1)


def seen(pos_s, which, chunk):
    at = lax.broadcasted_iota(jnp.int32, (KEYS, LANES), 0)
    base = chunk * KEYS
    return (at >= pos_s[which, 1:2] - base) & (at <= pos_s[which, 0:1] - base)


def fill_rows(sc, pos_s):
    for which in range(2):
        pos, start = query_rows(sc, which)
        pos_s[which, 0:1] = pos
        pos_s[which, 1:2] = start


def forward_kernel(sc, q_ref, own_ref, other_ref, o_ref, lse_ref, kv_s, q_s, acc_s, m_s, l_s, pos_s):
    fill_keys(sc, own_ref, other_ref, kv_s)
    fill_queries(sc, q_ref, q_s)
    fill_rows(sc, pos_s)
    acc_s[...] = jnp.zeros_like(acc_s)
    m_s[...] = jnp.full_like(m_s, NEG)
    l_s[...] = jnp.zeros_like(l_s)

    def step(t, carry):
        which, chunk = chunk_of(sc, t)
        scores = dot_tn(keys_of(kv_s, chunk, 0), q_s[which])
        scores = jnp.where(seen(pos_s, which, chunk), scores, NEG)
        old = m_s[which]
        new = jnp.maximum(old, jnp.max(scores, axis=0, keepdims=True))
        prob = jnp.exp(scores - new)
        shrink = jnp.exp(old - new)
        m_s[which] = new
        l_s[which] = l_s[which] * shrink + jnp.sum(prob, axis=0, keepdims=True)
        acc_s[which] = acc_s[which] * shrink + jnp.dot(
            keys_of(kv_s, chunk, 1), prob.astype(BF16), preferred_element_type=F32
        )
        return carry

    lax.fori_loop(0, CHUNKS + 1, step, 0, unroll=UNROLL_F)
    for which in range(2):
        acc_s[which] = acc_s[which] / l_s[which]
        lse_ref[0, which] = m_s[which] + jnp.log(l_s[which])
    for half in range(2):
        mine = acc_s[jnp.bitwise_xor(half, sc[1])]
        for j in range(GROUP):
            o_ref[j, :, half * BLK : (half + 1) * BLK] = mine[:, j * BLK : (j + 1) * BLK]


def backward_kernel(
    sc, q_ref, own_ref, other_ref, o_ref, do_ref, lse_ref,
    dq_ref, down_ref, dother_ref,
    kv_s, q_s, do_s, dq_s, dkv_s, delta_s, pos_s,
):
    fill_keys(sc, own_ref, other_ref, kv_s)
    fill_queries(sc, q_ref, q_s)
    fill_queries(sc, do_ref, do_s)
    fill_queries(sc, o_ref, dq_s)
    fill_rows(sc, pos_s)
    for which in range(2):
        delta_s[which] = jnp.sum(dq_s[which] * do_s[which].astype(F32), axis=0, keepdims=True)
    dq_s[...] = jnp.zeros_like(dq_s)
    dkv_s[...] = jnp.zeros_like(dkv_s)

    def step(t, carry):
        which, chunk = chunk_of(sc, t)
        key_t, val_t, q_t, do_t = keys_of(kv_s, chunk, 0), keys_of(kv_s, chunk, 1), q_s[which], do_s[which]
        scores = dot_tn(key_t, q_t)
        prob = jnp.where(seen(pos_s, which, chunk), jnp.exp(scores - lse_ref[0, which]), 0.0)
        d_prob = dot_tn(val_t, do_t)
        d_score = (prob * (d_prob - delta_s[which])).astype(BF16)
        d_val = dot_nt(do_t, prob.astype(BF16))
        d_key = dot_nt(q_t, d_score)
        dq_s[which] = dq_s[which] + jnp.dot(key_t, d_score, preferred_element_type=F32)
        for j in range(CHUNK):
            lanes = slice(j * BLK, (j + 1) * BLK)
            dkv_s[chunk * CHUNK + j, 0] = dkv_s[chunk * CHUNK + j, 0] + d_key[:, lanes]
            dkv_s[chunk * CHUNK + j, 1] = dkv_s[chunk * CHUNK + j, 1] + d_val[:, lanes]
        return carry

    lax.fori_loop(0, CHUNKS + 1, step, 0, unroll=UNROLL_B)
    core = sc[2]
    scale = HEAD_DIM**-0.5
    for half in range(2):
        lanes = slice(half * BLK, (half + 1) * BLK)
        mine = dq_s[jnp.bitwise_xor(half, sc[1])] * scale
        for j in range(GROUP):
            dq_ref[j, :, lanes] = mine[:, j * BLK : (j + 1) * BLK]
        for chip in range(CTX // 2):
            block = sc[7 + 2 * (2 * chip + core) + half]
            down_ref[chip, :, 0, :, lanes] = dkv_s[block].astype(BF16)
            block = sc[7 + 2 * (2 * chip + 1 - core) + half]
            dother_ref[chip, :, 0, :, lanes] = dkv_s[block].astype(BF16)


ROWS = 2 * BLK
HEAD_SPEC = pl.BlockSpec((GROUP, HEAD_DIM, ROWS), lambda g, sc: (g, 0, 0))
KV_SPEC = pl.BlockSpec((CTX // 2, 2, 1, HEAD_DIM, ROWS), lambda g, sc: (0, 0, g, 0, 0))
LSE_SPEC = pl.BlockSpec((1, 2, 1, LANES), lambda g, sc: (g, 0, 0, 0))
HEAD_SHAPE = jax.ShapeDtypeStruct((HEADS, HEAD_DIM, ROWS), F32)
KV_SHAPE = jax.ShapeDtypeStruct((CTX // 2, 2, KV_HEADS, HEAD_DIM, ROWS), BF16)
LSE_SHAPE = jax.ShapeDtypeStruct((KV_HEADS, 2, 1, LANES), F32)
KERNEL_PARAMS = pltpu.CompilerParams(
    dimension_semantics=("arbitrary",), vmem_limit_bytes=40 * 2**20
)


def attention(scalars, q_t, own, other):
    return pl.pallas_call(
        forward_kernel,
        grid_spec=pltpu.PrefetchScalarGridSpec(
            num_scalar_prefetch=1,
            grid=(KV_HEADS,),
            in_specs=[HEAD_SPEC, KV_SPEC, KV_SPEC],
            out_specs=[HEAD_SPEC, LSE_SPEC],
            scratch_shapes=[
                pltpu.VMEM((NBLK, 2, HEAD_DIM, BLK), BF16),
                pltpu.VMEM((2, HEAD_DIM, LANES), BF16),
                pltpu.VMEM((2, HEAD_DIM, LANES), F32),
                pltpu.VMEM((2, 1, LANES), F32),
                pltpu.VMEM((2, 1, LANES), F32),
                pltpu.VMEM((2, 8, LANES), jnp.int32),
            ],
        ),
        out_shape=[HEAD_SHAPE, LSE_SHAPE],
        compiler_params=KERNEL_PARAMS,
        name="attention",
    )(scalars, q_t, own, other)


def attention_back(scalars, q_t, own, other, o_t, do_t, lse):
    return pl.pallas_call(
        backward_kernel,
        grid_spec=pltpu.PrefetchScalarGridSpec(
            num_scalar_prefetch=1,
            grid=(KV_HEADS,),
            in_specs=[HEAD_SPEC, KV_SPEC, KV_SPEC, HEAD_SPEC, HEAD_SPEC, LSE_SPEC],
            out_specs=[HEAD_SPEC, KV_SPEC, KV_SPEC],
            scratch_shapes=[
                pltpu.VMEM((NBLK, 2, HEAD_DIM, BLK), BF16),
                pltpu.VMEM((2, HEAD_DIM, LANES), BF16),
                pltpu.VMEM((2, HEAD_DIM, LANES), BF16),
                pltpu.VMEM((2, HEAD_DIM, LANES), F32),
                pltpu.VMEM((NBLK, 2, HEAD_DIM, BLK), F32),
                pltpu.VMEM((2, 1, LANES), F32),
                pltpu.VMEM((2, 8, LANES), jnp.int32),
            ],
        ),
        out_shape=[HEAD_SHAPE, KV_SHAPE, KV_SHAPE],
        compiler_params=KERNEL_PARAMS,
        name="attention_back",
    )(scalars, q_t, own, other, o_t, do_t, lse)


VMEM_SPEC = pl.BlockSpec(memory_space=pltpu.VMEM)


UNITS = FF // FSDP // 2


def unpack_kernel(sc, *refs):
    mlp0, mlp0_p, qkv0, qkv0_p, all1, all1_p, qkv_ref, out_ref, gu_ref = refs

    def layer_out(layer, halves, qkv_halves, qkv_at, wout_at):
        for half in range(2):
            mlp = halves[half]
            for k in range(2):
                for i in range(FSDP):
                    src = k * HALF + i * UNITS
                    dst = k * FF + i * 2 * UNITS + half * UNITS
                    gu_ref[layer, :, dst : dst + UNITS] = mlp[:, src : src + UNITS].astype(F32)
            cut = (Q_ROWS + KV_ROWS) // 2
            qkv_ref[layer, :, half * cut : (half + 1) * cut] = (
                qkv_halves[half][:, qkv_at : qkv_at + cut].astype(F32)
            )
            cut = D // 2
            out_ref[layer, :, half * cut : (half + 1) * cut] = (
                mlp[:, wout_at : wout_at + cut].astype(F32)
            )

    def both(order):
        m0, q0, a1 = [mlp0, mlp0_p][::order], [qkv0, qkv0_p][::order], [all1, all1_p][::order]
        layer_out(0, m0, q0, 0, FF + HALF)
        layer_out(1, a1, a1, FF + HALF + D // 2, FF + HALF)

    @pl.when(sc[0] == 0)
    def _():
        both(1)

    @pl.when(sc[0] != 0)
    def _():
        both(-1)


def unpack(core, mlp0, mlp0_p, qkv0, qkv0_p, all1, all1_p):
    return pl.pallas_call(
        unpack_kernel,
        grid_spec=pltpu.PrefetchScalarGridSpec(
            num_scalar_prefetch=1,
            grid=(),
            in_specs=[VMEM_SPEC] * 6,
            out_specs=[VMEM_SPEC] * 3,
        ),
        out_shape=[
            jax.ShapeDtypeStruct((LAYERS, SHARD, Q_ROWS + KV_ROWS), F32),
            jax.ShapeDtypeStruct((LAYERS, SHARD, D), F32),
            jax.ShapeDtypeStruct((LAYERS, SHARD, 2 * FF), F32),
        ],
        compiler_params=pltpu.CompilerParams(vmem_limit_bytes=40 * 2**20),
        name="unpack",
    )(core, mlp0, mlp0_p, qkv0, qkv0_p, all1, all1_p)


def rotate(x, cosine, sine):
    half = HEAD_DIM // 2
    first, second = x[:, :half], x[:, half:]
    return jnp.concatenate([first * cosine - second * sine, second * cosine + first * sine], 1)


def normed(hidden):
    inv_rms = lax.rsqrt(jnp.mean(hidden * hidden, -1, keepdims=True) + EPS)
    return hidden * inv_rms, inv_rms


def norm_back(d_unit, unit, inv_rms):
    return inv_rms * (d_unit - unit * jnp.mean(d_unit * unit, -1, keepdims=True))


def mm(a, b):
    return jnp.dot(a, b, preferred_element_type=F32)


def ein(spec, a, b):
    return jnp.einsum(spec, a, b, preferred_element_type=F32)


def local(tokens, block_order, doc_ids, norm_gains, w_qkv, w_out, w_gate_up, w_down, cotangent):
    place = lax.axis_index("ctx")
    core = jnp.bitwise_and(place, 1)
    first_core = core == 0

    def my_half(left, right):
        return jnp.where(first_core, left, right)

    def in_order(own, other):
        return my_half(own, other), my_half(other, own)

    gain_cols = jnp.transpose(norm_gains.reshape(2 * LAYERS, SHARD))
    cut = (Q_ROWS + KV_ROWS + D) // 2

    def mlp_pack(layer):
        wgu = w_gate_up[layer].reshape(SHARD, 2, FSDP, 2, UNITS)
        wgu = my_half(wgu[..., 0, :], wgu[..., 1, :]).reshape(SHARD, FF)
        wdown = my_half(w_down[layer, :UNITS], w_down[layer, UNITS:]).reshape(SHARD, HALF)
        return jnp.concatenate([wgu, wdown], 1)

    def proj_pack(layer):
        proj = jnp.concatenate([w_qkv[layer], w_out[layer]], 1)
        return my_half(proj[:, :cut], proj[:, cut:])

    pack0, first = lax.optimization_barrier(
        (mlp_pack(0), jnp.concatenate([proj_pack(0), gain_cols], 1))
    )
    pack0 = lax.all_gather(pack0, "fsdp", axis=0, tiled=True)
    first = gather_fsdp(first)
    pack1 = lax.all_gather(mlp_pack(1), "fsdp", axis=0, tiled=True)
    gains = jnp.transpose(first[:, cut:].astype(F32)).reshape(LAYERS, 2, D)

    def whole_proj(own):
        return jnp.concatenate(in_order(own, to_partner(own)), 1)

    def mlp_halves(pack):
        wgu, wdown = pack[:, :FF], pack[:, FF:].reshape(HALF, D)
        return [(wgu, wdown), (to_partner(wgu), to_partner(wdown))]

    projs, mlps = [whole_proj(first[:, :cut])], []

    first_block = lax.dynamic_index_in_dim(block_order, 2 * place, 0, keepdims=False)
    low = jnp.minimum(first_block, NBLK - 1 - first_block)
    low_half = (first_block != low).astype(jnp.int32)
    starts = jnp.sum(
        (doc_ids[0][None, :] < jnp.arange(1, 5, dtype=jnp.int32)[:, None]).astype(jnp.int32), 1
    )
    scalars = jnp.concatenate([jnp.stack([low, low_half, core]), starts, block_order])
    lane = jnp.arange(ROWS, dtype=jnp.int32)
    pos = jnp.where(lane < BLK, first_block, NBLK - 2 - first_block) * BLK + lane
    inv_freq = THETA ** (-jnp.arange(HEAD_DIM // 2, dtype=F32) / (HEAD_DIM // 2))
    angles = pos.astype(F32)[None, :] * inv_freq[:, None]
    cosine, sine = jnp.cos(angles), jnp.sin(angles)

    hidden = tokens[0].astype(F32)
    saved = []
    for layer in range(LAYERS):
        wqkv, wout = projs[layer][:, : Q_ROWS + KV_ROWS], projs[layer][:, Q_ROWS + KV_ROWS :]
        unit_a, rms_a = normed(hidden)
        attn_in = (unit_a * gains[layer, 0]).astype(BF16)
        qkv_t = ein("de,td->et", wqkv, attn_in).reshape(-1, HEAD_DIM, ROWS)
        turned = rotate(qkv_t[: HEADS + KV_HEADS], cosine, sine)
        q_t = (turned[:HEADS] * HEAD_DIM**-0.5).astype(BF16)
        kv_t = jnp.concatenate([turned[HEADS:], qkv_t[HEADS + KV_HEADS :]], 0).astype(BF16)
        kv_t = kv_t.reshape(1, 2, KV_HEADS, HEAD_DIM, ROWS)
        kv_own = over_chips(jnp.broadcast_to(kv_t, (CTX // 2,) + kv_t.shape[1:]))
        if layer == 0:
            kv_own, late = lax.optimization_barrier((kv_own, proj_pack(1)))
            late = gather_fsdp(late)
        else:
            mlps.append(mlp_halves(pack1))
        kv_other = to_partner(kv_own)
        o_t, lse = attention(scalars, q_t, kv_own, kv_other)
        if layer == 0:
            o_t, pack0, late = lax.optimization_barrier((o_t, pack0, late))
            mlps.append(mlp_halves(pack0))
            projs.append(whole_proj(late))
        attn_out = o_t.astype(BF16).reshape(Q_ROWS, ROWS)
        mid = hidden + ein("at,ad->td", attn_out, wout)
        unit_m, rms_m = normed(mid)
        mlp_in = (unit_m * gains[layer, 1]).astype(BF16)
        hidden = mid
        halves = []
        for wgu, wdown in mlps[layer]:
            gate_up = mm(mlp_in, wgu)
            inner = (jax.nn.silu(gate_up[:, :HALF]) * gate_up[:, HALF:]).astype(BF16)
            hidden = hidden + mm(inner, wdown)
            halves.append((wgu, wdown, gate_up, inner))
        saved.append(
            (wqkv, wout, unit_a, rms_a, attn_in, q_t, kv_own, kv_other, o_t, lse, attn_out,
             unit_m, rms_m, mlp_in, halves)
        )
    output = hidden.astype(BF16).reshape(1, ROWS, D)

    d_hidden = cotangent[0].astype(F32)
    gain_grads = [None] * LAYERS
    for layer in reversed(range(LAYERS)):
        (wqkv, wout, unit_a, rms_a, attn_in, q_t, kv_own, kv_other, o_t, lse, attn_out,
         unit_m, rms_m, mlp_in, halves) = saved[layer]
        grad_b = d_hidden.astype(BF16)
        d_norm = 0.0
        wgu_parts, wd_parts = [], []
        for wgu, wdown, gate_up, inner in halves:
            d_inner = ein("td,fd->tf", grad_b, wdown)
            gate, up = gate_up[:, :HALF], gate_up[:, HALF:]
            sig = jax.nn.sigmoid(gate)
            d_gate = d_inner * up * sig * (1.0 + gate * (1.0 - sig))
            d_up = d_inner * (gate * sig)
            d_gu = jnp.concatenate([d_gate, d_up], 1).astype(BF16)
            d_norm = d_norm + ein("tf,df->td", d_gu, wgu)
            wd_parts.append(ein("tf,td->fd", inner, grad_b).astype(BF16))
            wgu_parts.append(ein("td,tf->df", mlp_in, d_gu).astype(BF16))
        d_gain_m = jnp.sum(d_norm * unit_m, 0)
        d_hidden = d_hidden + norm_back(d_norm * gains[layer, 1], unit_m, rms_m)
        grad_b = d_hidden.astype(BF16)
        d_wout = mm(attn_out, grad_b)
        do_t = ein("ad,td->at", wout, grad_b).astype(BF16).reshape(HEADS, HEAD_DIM, ROWS)
        if layer == 0:
            do_t, wgu_parts, wd_parts, late = lax.optimization_barrier(
                (do_t, wgu_parts, wd_parts, late)
            )
            late = scatter_fsdp(late)
        wout_half = D // 2
        d_wout = d_wout.astype(BF16)
        wout_mine = my_half(d_wout[:, :wout_half], d_wout[:, wout_half:])
        wout_theirs = my_half(d_wout[:, wout_half:], d_wout[:, :wout_half])
        d_mlp = [
            sum_pair(wgu_parts[0], to_partner(wgu_parts[1])),
            sum_pair(wd_parts[0], to_partner(wd_parts[1])).reshape(D, HALF),
            sum_pair(wout_mine, to_partner(wout_theirs)),
        ]
        share = lax.psum_scatter(
            jnp.concatenate(d_mlp, 1), "fsdp", scatter_dimension=0, tiled=True
        )
        if layer == 1:
            share1 = share
        else:
            share0 = share
        dq_t, dkv_own, dkv_other = attention_back(scalars, q_t, kv_own, kv_other, o_t, do_t, lse)
        dkv = (dkv_own.astype(F32) + to_partner(dkv_other).astype(F32)).astype(BF16)
        if layer == 0:
            dkv, late = lax.optimization_barrier((dkv, late))
            share1 = lax.optimization_barrier((share1, late, dkv))[0]
            share1 = sum_chips(jnp.concatenate([share1, late], 1))
        dkv = jnp.sum(over_chips(dkv).astype(F32), 0)
        turned = jnp.concatenate([dq_t, dkv[0]], 0)
        d_qkv = jnp.concatenate([rotate(turned, cosine, -sine), dkv[1]], 0)
        d_qkv = d_qkv.astype(BF16).reshape(Q_ROWS + KV_ROWS, ROWS)
        d_wqkv = ein("td,et->de", attn_in, d_qkv)
        d_norm = ein("et,de->td", d_qkv, wqkv)
        d_gain_a = jnp.sum(d_norm * unit_a, 0)
        d_hidden = d_hidden + norm_back(d_norm * gains[layer, 0], unit_a, rms_a)
        gain_grads[layer] = jnp.stack([d_gain_a, d_gain_m])
        d_wqkv = d_wqkv.astype(BF16)
        half = (Q_ROWS + KV_ROWS) // 2
        mine = my_half(d_wqkv[:, :half], d_wqkv[:, half:])
        theirs = my_half(d_wqkv[:, half:], d_wqkv[:, :half])
        d_wqkv = sum_pair(mine, to_partner(theirs))
        if layer == 0:
            d_gains = jnp.transpose(jnp.stack(gain_grads).reshape(2 * LAYERS, D)).astype(BF16)
            share_qkv = sum_chips(scatter_fsdp(jnp.concatenate([d_wqkv, d_gains], 1)))
        else:
            late = d_wqkv
    input_grad = d_hidden.reshape(1, ROWS, D)

    share0 = sum_chips(share0)
    mlp0, mlp0_p, qkv0, qkv0_p = share0, to_partner(share0), share_qkv, to_partner(share_qkv)
    all1, all1_p = share1, to_partner(share1)
    d_gain = qkv0[:, half:].astype(F32) + qkv0_p[:, half:].astype(F32)
    gain_grad = jnp.transpose(d_gain).reshape(LAYERS, 2, SHARD)
    qkv_grad, out_proj_grad, gate_up_grad = unpack(
        core.reshape(1), mlp0, mlp0_p, qkv0, qkv0_p, all1, all1_p
    )
    down_grad = []
    for own, theirs in ((mlp0, mlp0_p), (all1, all1_p)):
        rows = [x[:, FF : FF + HALF].reshape(UNITS, D) for x in in_order(own, theirs)]
        down_grad.append(jnp.concatenate(rows, 0))
    down_grad = jnp.stack(down_grad).astype(F32)
    return (output, input_grad, gain_grad, qkv_grad, out_proj_grad, gate_up_grad, down_grad)


def solution(mesh):
    in_specs = (
        P("fsdp", "ctx", None),
        P(),
        P("fsdp", None),
        P(None, None, "fsdp"),
        P(None, "fsdp", None),
        P(None, "fsdp", None),
        P(None, "fsdp", None),
        P(None, "fsdp", None),
        P("fsdp", "ctx", None),
    )
    out_specs = (
        P("fsdp", "ctx", None),
        P("fsdp", "ctx", None),
        P(None, None, "fsdp"),
        P(None, "fsdp", None),
        P(None, "fsdp", None),
        P(None, "fsdp", None),
        P(None, "fsdp", None),
    )
    return jax.shard_map(local, mesh=mesh, in_specs=in_specs, out_specs=out_specs, check_vma=False)
```

profile of v0, /device:TPU:1, one launch (start us, length us, event | category | flops | bytes accessed | tf_op | source)
XLA Modules:
  0.0 507.0 jit_solution(7278679058069742855)
XLA Ops:
  16.4 8.2 %all-to-all-start = ((bf16[8,72,772]{2,1,0:T(8,128)(2,1)}), bf16[8,72,772]{2,1,0:T(8,128)(2,1)S(1)}, u32[]{:S(2)}, u32[]{:S(2)}) async-start(bf16[8,72,772]{2,1,0:T(8,128)(2,1)} %broadcast_in_dim.16), calls=%async_computation | async-start | bytes 2064384 | tf_op jit(solution)/shard_map/all_to_all | solution.py:45
  27.3 14.4 %all-to-all-done = bf16[8,72,772]{2,1,0:T(8,128)(2,1)S(1)} async-done(((bf16[8,72,772]{2,1,0:T(8,128)(2,1)}), bf16[8,72,772]{2,1,0:T(8,128)(2,1)S(1)}, u32[]{:S(2)}, u32[]{:S(2)}) %all-to-all-start) | async-done | bytes 889376 | tf_op jit(solution)/shard_map/all_to_all | solution.py:45
  49.8 4.6 all-to-all-start.1
  55.2 22.7 %all-to-all-done.1.own_ref = bf16[8,2,3,64,256]{4,3,2,1,0:T(8,128)(2,1)S(1)} async-done(((bf16[8,2,3,64,256]{4,3,2,1,0:T(8,128)(2,1)}), bf16[8,2,3,64,256]{4,3,2,1,0:T(8,128)(2,1)S(1)}, u32[]{:S(2)}, u32[]{:S(2)}) %all-to-all-start.1) | async-done | bytes 1572896 | tf_op jit(solution)/shard_map/all_to_all | solution.py:41
  81.1 4.4 all-to-all-start.2
  93.6 15.5 %attention.2 = (f32[9,64,256]{2,1,0:T(8,128)S(1)}, f32[3,2,1,384]{3,2,1,0:T(1,128)S(1)}) custom-call(s32[39]{0:T(128)S(1)} %concatenate.92.sc, bf16[9,64,256]{2,1,0:T(8,128)(2,1)S(1)} %fusion.29.q_ref, bf16[8,2,3,64,256]{4,3,2,1,0:T(8,128)(2,1)S(1)} %all-to-all-done.1.own_ref, bf16[8,2,3,64,256]{4,3,2,1,0:T(8,128)(2,1)S(1)} %collective-permute-done.1.other_ref), custom_call_target="tpu_custom_call" | custom-call | tf_op jit(solution)/shard_map/attention/pallas_call | solution.py:225
  110.0 2.9 slice.286
  114.9 2.4 slice.289
  117.3 2.7 reshape.315
  123.1 2.4 fusion.79
  128.4 2.9 fusion.85
  134.5 25.2 %all_to_all.40.own_ref = bf16[8,2,3,64,256]{4,3,2,1,0:T(8,128)(2,1)S(1)} all-to-all(bf16[8,2,3,64,256]{4,3,2,1,0:T(8,128)(2,1)S(1)} %broadcast_in_dim.21), channel_id=1, replica_groups={{0,16,32,48,64,80,96,112},{8,24,40,56,72,88,104,120},{1,17,33,49,65,81,..., dimensions={0} | all-to-all | bytes 3145728 | tf_op jit(solution)/shard_map/all_to_all | solution.py:41
  159.8 2.5 collective-permute-start.5
  162.2 20.3 %all-gather.5.cloned.1.call-done = bf16[576,2304]{1,0:T(8,128)(2,1)} async-done(((bf16[72,2304]{1,0:T(8,128)(2,1)}), bf16[576,2304]{1,0:T(8,128)(2,1)}) %all-gather.5.cloned.1.call-update) | async-done | bytes 2654224 | tf_op jit(solution)/shard_map/all_gather | solution.py:382
  184.7 3.4 reshape.317
  188.1 2.8 slice.367
  191.7 2.2 copy.76
  195.5 16.4 %attention.3 = (f32[9,64,256]{2,1,0:T(8,128)S(1)}, f32[3,2,1,384]{3,2,1,0:T(1,128)S(1)}) custom-call(s32[39]{0:T(128)S(1)} %concatenate.92.sc, bf16[9,64,256]{2,1,0:T(8,128)(2,1)S(1)} %fusion.26.q_ref, bf16[8,2,3,64,256]{4,3,2,1,0:T(8,128)(2,1)S(1)} %all_to_all.40.own_ref, bf16[8,2,3,64,256]{4,3,2,1,0:T(8,128)(2,1)} %collective-permute-done.5.other_ref), custom_call_target="tpu_custom_call" | custom-call | tf_op jit(solution)/shard_map/attention/pallas_call | solution.py:225
  217.6 2.3 fusion.86
  220.8 2.4 multiply_reduce_fusion
  223.8 22.9 %attention_back.2 = (f32[9,64,256]{2,1,0:T(8,128)S(1)}, bf16[8,2,3,64,256]{4,3,2,1,0:T(8,128)(2,1)S(1)}, bf16[8,2,3,64,256]{4,3,2,1,0:T(8,128)(2,1)S(1)}) custom-call(s32[39]{0:T(128)S(1)} %concatenate.92.sc, bf16[9,64,256]{2,1,0:T(8,128)(2,1)S(1)} %fusion.26.q_ref, bf16[8,2,3,64,256]{4,3,2,1,0:T(8,128)(2,1)S(1)} %all_to_all.40.own_ref, ...), custom_call_target="tpu_custom_call" | custom-call | tf_op jit(solution)/shard_map/attention_back/pallas_call | solution.py:248
  254.3 4.4 all-to-all-start.4
  260.9 2.5 add_convert_fusion.4
  265.0 2.2 reshape.326
  267.2 2.4 add_convert_fusion
  271.5 10.6 %all-to-all-done.4 = bf16[8,2,3,64,256]{4,3,2,1,0:T(8,128)(2,1)} async-done(((bf16[8,2,3,64,256]{4,3,2,1,0:T(8,128)(2,1)}), bf16[8,2,3,64,256]{4,3,2,1,0:T(8,128)(2,1)}, u32[]{:S(2)}, u32[]{:S(2)}) %all-to-all-start.4) | async-done | bytes 1572896 | tf_op jit(solution)/shard_map/all_to_all | solution.py:41
  292.8 2.3 multiply_reduce_fusion.2
  303.4 22.7 %attention_back.3 = (f32[9,64,256]{2,1,0:T(8,128)S(1)}, bf16[8,2,3,64,256]{4,3,2,1,0:T(8,128)(2,1)S(1)}, bf16[8,2,3,64,256]{4,3,2,1,0:T(8,128)(2,1)}) custom-call(s32[39]{0:T(128)S(1)} %concatenate.92.sc, bf16[9,64,256]{2,1,0:T(8,128)(2,1)S(1)} %fusion.29.q_ref, bf16[8,2,3,64,256]{4,3,2,1,0:T(8,128)(2,1)S(1)} %all-to-all-done.1.own_ref, ...), custom_call_target="tpu_custom_call" | custom-call | tf_op jit(solution)/shard_map/attention_back/pallas_call | solution.py:248
  329.8 4.5 all-to-all-start.5
  336.4 11.8 %all-to-all-done.5 = bf16[8,72,480]{2,1,0:T(8,128)(2,1)S(1)} async-done(((bf16[8,72,480]{2,1,0:T(8,128)(2,1)}), bf16[8,72,480]{2,1,0:T(8,128)(2,1)S(1)}, u32[]{:S(2)}, u32[]{:S(2)}) %all-to-all-start.5) | async-done | bytes 552992 | tf_op jit(solution)/shard_map/all_to_all | solution.py:45
  348.9 2.3 add_convert_fusion.5
  352.9 2.2 reshape.325
  355.1 3.1 add_convert_fusion.2
  358.3 4.4 all-to-all-start.6
  366.7 19.1 %all-to-all-done.6 = bf16[8,2,3,64,256]{4,3,2,1,0:T(8,128)(2,1)} async-done(((bf16[8,2,3,64,256]{4,3,2,1,0:T(8,128)(2,1)}), bf16[8,2,3,64,256]{4,3,2,1,0:T(8,128)(2,1)}, u32[]{:S(2)}, u32[]{:S(2)}) %all-to-all-start.6) | async-done | bytes 1572896 | tf_op jit(solution)/shard_map/all_to_all | solution.py:41
  394.0 3.5 all-to-all-start.7
  398.1 13.6 %all-to-all-done.7 = bf16[8,72,484]{2,1,0:T(8,128)(2,1)S(1)} async-done(((bf16[8,72,484]{2,1,0:T(8,128)(2,1)}), bf16[8,72,484]{2,1,0:T(8,128)(2,1)S(1)}, u32[]{:S(2)}, u32[]{:S(2)}) %all-to-all-start.7) | async-done | bytes 557600 | tf_op jit(solution)/shard_map/all_to_all | solution.py:45
  412.4 2.4 fusion.38
  416.6 3.0 collective-permute-done.13
  424.5 3.7 collective-permute-start.15
  428.2 25.4 %reduce-scatter.7.cloned.1.call-done = bf16[72,2592]{1,0:T(8,128)(2,1)} async-done(((bf16[576,2592]{1,0:T(8,128)(2,1)}), bf16[72,2592]{1,0:T(8,128)(2,1)}) %reduce-scatter.7.cloned.1.call-update) | async-done | bytes 373264
  455.4 6.4 %collective-permute-done.19 = bf16[72,2592]{1,0:T(8,128)(2,1)S(1)} collective-permute-done((bf16[72,2592]{1,0:T(8,128)(2,1)}, bf16[72,2592]{1,0:T(8,128)(2,1)S(1)}, u32[]{:S(2)}, u32[]{:S(2)}) %collective-permute-start.19) | collective-permute-done | bytes 373280 | tf_op jit(solution)/shard_map/ppermute | solution.py:63
  464.2 2.6 collective-permute-start.28
  466.8 4.6 collective-permute-done.20
  471.5 2.8 collective-permute-start.21
  474.3 8.7 %collective-permute-done.28 = bf16[72,3072]{1,0:T(8,128)(2,1)S(1)} collective-permute-done((bf16[72,3072]{1,0:T(8,128)(2,1)S(1)}, bf16[72,3072]{1,0:T(8,128)(2,1)S(1)}, u32[]{:S(2)}, u32[]{:S(2)}) %collective-permute-start.28) | collective-permute-done | bytes 442400 | tf_op jit(solution)/shard_map/ppermute | solution.py:63
  483.1 7.1 %collective-permute-start.29 = (bf16[72,3072]{1,0:T(8,128)(2,1)S(1)}, bf16[72,3072]{1,0:T(8,128)(2,1)S(1)}, u32[]{:S(2)}, u32[]{:S(2)}) collective-permute-start(bf16[72,3072]{1,0:T(8,128)(2,1)S(1)} %add_convert_fusion.8.refs_4_), channel_id=1, source_target_pairs={{0,8},{8,0},{16,24},{24,16},{32,40},{40,32},{48,56},{56,48},{64,72... | collective-permute-start | bytes 1327112 | tf_op jit(solution)/shard_map/ppermute | solution.py:37
  491.4 3.8 collective-permute-start.22
  (405 shorter events, 123.0 us)
Async XLA Ops:
  16.4 25.3 %all-to-all-start = ((bf16[8,72,772]{2,1,0:T(8,128)(2,1)}), bf16[8,72,772]{2,1,0:T(8,128)(2,1)S(1)}, u32[]{:S(2)}, u32[]{:S(2)}) async-start(bf16[8,72,772]{2,1,0:T(8,128)(2,1)} %broadcast_in_dim.16), calls=%async_computation | async-start | bytes 2064384 | tf_op jit(solution)/shard_map/all_to_all | solution.py:45
  24.6 85.3 %all-gather.3.cloned.1.call-start = ((), (), s32[]{:S(2)}) async-start(), calls=%async_computation.10 | async-start | bytes 2985984 | tf_op jit(solution)/shard_map/all_gather | solution.py:380
  41.8 3.1 collective-permute-start
  49.8 28.1 %all-to-all-start.1 = ((bf16[8,2,3,64,256]{4,3,2,1,0:T(8,128)(2,1)}), bf16[8,2,3,64,256]{4,3,2,1,0:T(8,128)(2,1)S(1)}, u32[]{:S(2)}, u32[]{:S(2)}) async-start(bf16[8,2,3,64,256]{4,3,2,1,0:T(8,128)(2,1)} %broadcast_in_dim.19), calls=%async_computation.1 | async-start | bytes 3145728 | tf_op jit(solution)/shard_map/all_to_all | solution.py:41
  54.4 31.3 %copy-start.63 = (bf16[72,2,8,1,96]{4,2,1,0,3:T(8,128)(2,1)S(1)}, bf16[72,2,8,1,96]{4,2,1,0,3:T(8,128)(2,1)}, u32[]{:S(2)}) copy-start(bf16[72,2,8,1,96]{4,2,1,0,3:T(8,128)(2,1)} %get-tuple-element.137) | copy-start | bytes 663556
  77.9 15.7 %collective-permute-start.1 = (bf16[8,2,3,64,256]{4,3,2,1,0:T(8,128)(2,1)S(1)}, bf16[8,2,3,64,256]{4,3,2,1,0:T(8,128)(2,1)S(1)}, u32[]{:S(2)}, u32[]{:S(2)}) collective-permute-start(bf16[8,2,3,64,256]{4,3,2,1,0:T(8,128)(2,1)S(1)} %all-to-all-done.1.own_ref), channel_id=1, source_target_pairs={{0,8},{8,0},{16,24},{24,16},{32,40},{40,32},{48,56},{56,48},{64,72... | collective-permute-start | bytes 4718600 | tf_op jit(solution)/shard_map/ppermute | solution.py:37
  81.1 28.8 %all-to-all-start.2 = ((bf16[8,72,768]{2,1,0:T(8,128)(2,1)}), bf16[8,72,768]{2,1,0:T(8,128)(2,1)}, u32[]{:S(2)}, u32[]{:S(2)}) async-start(bf16[8,72,768]{2,1,0:T(8,128)(2,1)} %broadcast_in_dim.20), calls=%async_computation.2 | async-start | bytes 1769472 | tf_op jit(solution)/shard_map/all_to_all | solution.py:45
  85.5 97.0 %all-gather.5.cloned.1.call-start = ((), (), s32[]{:S(2)}) async-start(), calls=%async_computation.11 | async-start | bytes 2985984 | tf_op jit(solution)/shard_map/all_gather | solution.py:382
  109.9 16.9 %collective-permute-start.4 = (bf16[576,768]{1,0:T(8,128)(2,1)}, bf16[576,768]{1,0:T(8,128)(2,1)}, u32[]{:S(2)}, u32[]{:S(2)}) collective-permute-start(bf16[576,768]{1,0:T(8,128)(2,1)} %bitcast.17), channel_id=1, source_target_pairs={{0,8},{8,0},{16,24},{24,16},{32,40},{40,32},{48,56},{56,48},{64,72... | collective-permute-start | bytes 2654216 | tf_op jit(solution)/shard_map/ppermute | solution.py:37
  112.9 15.5 %collective-permute-start.2 = (bf16[576,1536]{1,0:T(8,128)(2,1)}, bf16[576,1536]{1,0:T(8,128)(2,1)}, u32[]{:S(2)}, u32[]{:S(2)}) collective-permute-start(bf16[576,1536]{1,0:T(8,128)(2,1)} %slice.286), channel_id=1, source_target_pairs={{0,8},{8,0},{16,24},{24,16},{32,40},{40,32},{48,56},{56,48},{64,72... | collective-permute-start | bytes 5308424 | tf_op jit(solution)/shard_map/ppermute | solution.py:37
  121.2 10.3 %collective-permute-start.3 = (bf16[768,576]{0,1:T(8,128)(2,1)}, bf16[768,576]{0,1:T(8,128)(2,1)S(1)}, u32[]{:S(2)}, u32[]{:S(2)}) collective-permute-start(bf16[768,576]{0,1:T(8,128)(2,1)} %copy.73), channel_id=1, source_target_pairs={{0,8},{8,0},{16,24},{24,16},{32,40},{40,32},{48,56},{56,48},{64,72... | collective-permute-start | bytes 2654216 | tf_op jit(solution)/shard_map/ppermute | solution.py:37
  159.8 35.8 %collective-permute-start.5 = (bf16[8,2,3,64,256]{4,3,2,1,0:T(8,128)(2,1)S(1)}, bf16[8,2,3,64,256]{4,3,2,1,0:T(8,128)(2,1)}, u32[]{:S(2)}, u32[]{:S(2)}) collective-permute-start(bf16[8,2,3,64,256]{4,3,2,1,0:T(8,128)(2,1)S(1)} %all_to_all.40.own_ref), channel_id=1, source_target_pairs={{0,8},{8,0},{16,24},{24,16},{32,40},{40,32},{48,56},{56,48},{64,72... | collective-permute-start | bytes 4718600 | tf_op jit(solution)/shard_map/ppermute | solution.py:37
  190.9 26.7 %collective-permute-start.6 = (bf16[576,1536]{1,0:T(8,128)(2,1)}, bf16[576,1536]{1,0:T(8,128)(2,1)}, u32[]{:S(2)}, u32[]{:S(2)}) collective-permute-start(bf16[576,1536]{1,0:T(8,128)(2,1)} %slice.367), channel_id=1, source_target_pairs={{0,8},{8,0},{16,24},{24,16},{32,40},{40,32},{48,56},{56,48},{64,72... | collective-permute-start | bytes 5308424 | tf_op jit(solution)/shard_map/ppermute | solution.py:37
  193.9 25.9 %collective-permute-start.7 = (bf16[768,576]{0,1:T(8,128)(2,1)}, bf16[768,576]{0,1:T(8,128)(2,1)S(1)}, u32[]{:S(2)}, u32[]{:S(2)}) collective-permute-start(bf16[768,576]{0,1:T(8,128)(2,1)} %copy.76), channel_id=1, source_target_pairs={{0,8},{8,0},{16,24},{24,16},{32,40},{40,32},{48,56},{56,48},{64,72... | collective-permute-start | bytes 2654216 | tf_op jit(solution)/shard_map/ppermute | solution.py:37
  213.7 33.7 %copy-start.12 = (bf16[256,576]{0,1:T(8,128)(2,1)}, bf16[256,576]{0,1:T(8,128)(2,1)S(1)}, u32[]{:S(2)}) copy-start(bf16[256,576]{0,1:T(8,128)(2,1)S(1)} %multiply_convert_fusion.12) | copy-start | bytes 884740
  220.8 28.5 %copy-start.61 = (bf16[256,768]{1,0:T(8,128)(2,1)}, bf16[256,768]{1,0:T(8,128)(2,1)S(1)}, u32[]{:S(2)}) copy-start(bf16[256,768]{1,0:T(8,128)(2,1)S(1)} %get-tuple-element.100) | copy-start | bytes 1179652
  223.4 27.7 %copy-start.16 = (f32[256,576]{0,1:T(8,128)}, f32[256,576]{0,1:T(8,128)S(1)}, u32[]{:S(2)}) copy-start(f32[256,576]{0,1:T(8,128)S(1)} %multiply_add_fusion.2) | copy-start | bytes 1769476
  246.7 5.8 %collective-permute-start.8 = (bf16[8,2,3,64,256]{4,3,2,1,0:T(8,128)(2,1)S(1)}, bf16[8,2,3,64,256]{4,3,2,1,0:T(8,128)(2,1)S(1)}, u32[]{:S(2)}, u32[]{:S(2)}) collective-permute-start(bf16[8,2,3,64,256]{4,3,2,1,0:T(8,128)(2,1)S(1)} %get-tuple-element.48), channel_id=1, source_target_pairs={{0,8},{8,0},{16,24},{24,16},{32,40},{40,32},{48,56},{56,48},{64,72... | collective-permute-start | bytes 4718600 | tf_op jit(solution)/shard_map/ppermute | solution.py:37
  249.3 17.9 %collective-permute-start.23 = (bf16[576,1536]{1,0:T(8,128)(2,1)}, bf16[576,1536]{1,0:T(8,128)(2,1)}, u32[]{:S(2)}, u32[]{:S(2)}) collective-permute-start(bf16[576,1536]{1,0:T(8,128)(2,1)} %convolution_convert_fusion), channel_id=1, source_target_pairs={{0,8},{8,0},{16,24},{24,16},{32,40},{40,32},{48,56},{56,48},{64,72... | collective-permute-start | bytes 5308424 | tf_op jit(solution)/shard_map/ppermute | solution.py:37
  250.6 10.3 %collective-permute-start.24 = (bf16[768,576]{0,1:T(8,128)(2,1)}, bf16[768,576]{0,1:T(8,128)(2,1)}, u32[]{:S(2)}, u32[]{:S(2)}) collective-permute-start(bf16[768,576]{0,1:T(8,128)(2,1)} %convolution_convert_fusion.6), channel_id=1, source_target_pairs={{0,8},{8,0},{16,24},{24,16},{32,40},{40,32},{48,56},{56,48},{64,72... | collective-permute-start | bytes 2654216 | tf_op jit(solution)/shard_map/ppermute | solution.py:37
  252.5 6.3 %collective-permute-start.25 = (bf16[576,288]{1,0:T(8,128)(2,1)}, bf16[576,288]{1,0:T(8,128)(2,1)}, u32[]{:S(2)}, u32[]{:S(2)}) collective-permute-start(bf16[576,288]{1,0:T(8,128)(2,1)} %broadcast_select_fusion.6), channel_id=1, source_target_pairs={{0,8},{8,0},{16,24},{24,16},{32,40},{40,32},{48,56},{56,48},{64,72... | collective-permute-start | bytes 995336 | tf_op jit(solution)/shard_map/ppermute | solution.py:37
  254.3 27.8 %all-to-all-start.4 = ((bf16[8,2,3,64,256]{4,3,2,1,0:T(8,128)(2,1)}), bf16[8,2,3,64,256]{4,3,2,1,0:T(8,128)(2,1)}, u32[]{:S(2)}, u32[]{:S(2)}) async-start(bf16[8,2,3,64,256]{4,3,2,1,0:T(8,128)(2,1)} %add_convert_fusion.3), calls=%async_computation.4 | async-start | bytes 3145728 | tf_op jit(solution)/shard_map/all_to_all | solution.py:41
  258.8 162.2 %reduce-scatter.9.cloned.1.call-start = ((), (), s32[]{:S(2)}) async-start(), calls=%async_computation.13 | async-start | bytes 3483648
  286.3 15.3 %collective-permute-start.9 = (bf16[576,480]{1,0:T(8,128)(2,1)S(1)}, bf16[576,480]{1,0:T(8,128)(2,1)S(1)}, u32[]{:S(2)}, u32[]{:S(2)}) collective-permute-start(bf16[576,480]{1,0:T(8,128)(2,1)S(1)} %broadcast_select_fusion.5), channel_id=1, source_target_pairs={{0,8},{8,0},{16,24},{24,16},{32,40},{40,32},{48,56},{56,48},{64,72... | collective-permute-start | bytes 1658888 | tf_op jit(solution)/shard_map/ppermute | solution.py:37
  296.6 32.4 %copy-start.14 = (f32[256,576]{0,1:T(8,128)}, f32[256,576]{0,1:T(8,128)S(1)}, u32[]{:S(2)}) copy-start(f32[256,576]{0,1:T(8,128)S(1)} %multiply_add_fusion) | copy-start | bytes 1769476
  303.4 25.7 %copy-start.65 = (bf16[9,64,256]{2,1,0:T(8,128)(2,1)S(1)}, bf16[9,64,256]{2,1,0:T(8,128)(2,1)}, u32[]{:S(2)}) copy-start(bf16[9,64,256]{2,1,0:T(8,128)(2,1)} %copy-done.64) | copy-start | bytes 884740
  327.3 27.8 %collective-permute-start.10 = (bf16[8,2,3,64,256]{4,3,2,1,0:T(8,128)(2,1)}, bf16[8,2,3,64,256]{4,3,2,1,0:T(8,128)(2,1)}, u32[]{:S(2)}, u32[]{:S(2)}) collective-permute-start(bf16[8,2,3,64,256]{4,3,2,1,0:T(8,128)(2,1)} %get-tuple-element.53), channel_id=1, source_target_pairs={{0,8},{8,0},{16,24},{24,16},{32,40},{40,32},{48,56},{56,48},{64,72... | collective-permute-start | bytes 4718600 | tf_op jit(solution)/shard_map/ppermute | solution.py:37
  328.5 34.3 %collective-permute-start.16 = (bf16[576,1536]{1,0:T(8,128)(2,1)}, bf16[576,1536]{1,0:T(8,128)(2,1)}, u32[]{:S(2)}, u32[]{:S(2)}) collective-permute-start(bf16[576,1536]{1,0:T(8,128)(2,1)} %convolution_convert_fusion.2), channel_id=1, source_target_pairs={{0,8},{8,0},{16,24},{24,16},{32,40},{40,32},{48,56},{56,48},{64,72... | collective-permute-start | bytes 5308424 | tf_op jit(solution)/shard_map/ppermute | solution.py:37
  328.5 20.4 %collective-permute-start.17 = (bf16[768,576]{0,1:T(8,128)(2,1)}, bf16[768,576]{0,1:T(8,128)(2,1)}, u32[]{:S(2)}, u32[]{:S(2)}) collective-permute-start(bf16[768,576]{0,1:T(8,128)(2,1)} %convolution_convert_fusion.8), channel_id=1, source_target_pairs={{0,8},{8,0},{16,24},{24,16},{32,40},{40,32},{48,56},{56,48},{64,72... | collective-permute-start | bytes 2654216 | tf_op jit(solution)/shard_map/ppermute | solution.py:37
  329.7 4.6 collective-permute-start.18
  329.8 18.4 %all-to-all-start.5 = ((bf16[8,72,480]{2,1,0:T(8,128)(2,1)}), bf16[8,72,480]{2,1,0:T(8,128)(2,1)S(1)}, u32[]{:S(2)}, u32[]{:S(2)}) async-start(bf16[8,72,480]{2,1,0:T(8,128)(2,1)} %bitcast.32), calls=%async_computation.5 | async-start | bytes 1179648 | tf_op jit(solution)/shard_map/all_to_all | solution.py:45
  358.3 27.5 %all-to-all-start.6 = ((bf16[8,2,3,64,256]{4,3,2,1,0:T(8,128)(2,1)}), bf16[8,2,3,64,256]{4,3,2,1,0:T(8,128)(2,1)}, u32[]{:S(2)}, u32[]{:S(2)}) async-start(bf16[8,2,3,64,256]{4,3,2,1,0:T(8,128)(2,1)} %add_convert_fusion.2), calls=%async_computation.6 | async-start | bytes 3145728 | tf_op jit(solution)/shard_map/all_to_all | solution.py:41
  362.7 90.8 %reduce-scatter.7.cloned.1.call-start = ((), (), s32[]{:S(2)}) async-start(), calls=%async_computation.12 | async-start | bytes 3483648
  389.3 3.3 collective-permute-start.11
  394.0 17.7 %all-to-all-start.7 = ((bf16[8,72,484]{2,1,0:T(8,128)(2,1)}), bf16[8,72,484]{2,1,0:T(8,128)(2,1)S(1)}, u32[]{:S(2)}, u32[]{:S(2)}) async-start(bf16[8,72,484]{2,1,0:T(8,128)(2,1)} %bitcast.41), calls=%async_computation.7 | async-start | bytes 1179648 | tf_op jit(solution)/shard_map/all_to_all | solution.py:45
  411.8 4.5 collective-permute-start.12
  416.4 3.3 collective-permute-start.13
  419.7 4.8 collective-permute-start.14
  421.0 33.0 %copy-start.62 = (bf16[72,2592]{1,0:T(8,128)(2,1)S(1)}, bf16[72,2592]{1,0:T(8,128)(2,1)}, u32[]{:S(2)}) copy-start(bf16[72,2592]{1,0:T(8,128)(2,1)} %reduce-scatter.9.cloned.1.call-done) | copy-start | bytes 1119748
  422.1 31.8 %collective-permute-start.26 = (bf16[72,3072]{1,0:T(8,128)(2,1)S(1)}, bf16[72,3072]{1,0:T(8,128)(2,1)S(1)}, u32[]{:S(2)}, u32[]{:S(2)}) collective-permute-start(bf16[72,3072]{1,0:T(8,128)(2,1)S(1)} %pad_maximum_fusion.22), channel_id=1, source_target_pairs={{0,16},{8,24},{16,0},{24,8},{32,48},{40,56},{48,32},{56,40},{64,80... | collective-permute-start | bytes 1327112 | tf_op jit(solution)/shard_map/ppermute | solution.py:63
  424.5 70.6 %collective-permute-start.15 = (bf16[72,484]{1,0:T(8,128)(2,1)S(1)}, bf16[72,484]{1,0:T(8,128)(2,1)S(1)}, u32[]{:S(2)}, u32[]{:S(2)}) collective-permute-start(bf16[72,484]{1,0:T(8,128)(2,1)S(1)} %add_convert_fusion.18.refs_2_), channel_id=1, source_target_pairs={{0,8},{8,0},{16,24},{24,16},{32,40},{40,32},{48,56},{56,48},{64,72... | collective-permute-start | bytes 209096 | tf_op jit(solution)/shard_map/ppermute | solution.py:37
  453.6 8.2 %collective-permute-start.19 = (bf16[72,2592]{1,0:T(8,128)(2,1)}, bf16[72,2592]{1,0:T(8,128)(2,1)S(1)}, u32[]{:S(2)}, u32[]{:S(2)}) collective-permute-start(bf16[72,2592]{1,0:T(8,128)(2,1)} %reduce-scatter.7.cloned.1.call-done), channel_id=1, source_target_pairs={{0,16},{8,24},{16,0},{24,8},{32,48},{40,56},{48,32},{56,40},{64,80... | collective-permute-start | bytes 1119752 | tf_op jit(solution)/shard_map/ppermute | solution.py:63
  454.1 10.0 %collective-permute-start.27 = (bf16[72,3072]{1,0:T(8,128)(2,1)S(1)}, bf16[72,3072]{1,0:T(8,128)(2,1)S(1)}, u32[]{:S(2)}, u32[]{:S(2)}) collective-permute-start(bf16[72,3072]{1,0:T(8,128)(2,1)S(1)} %add_convert_fusion.10), channel_id=1, source_target_pairs={{0,32},{8,40},{16,48},{24,56},{32,0},{40,8},{48,16},{56,24},{64,96... | collective-permute-start | bytes 1327112 | tf_op jit(solution)/shard_map/ppermute | solution.py:63
  462.8 8.6 %collective-permute-start.20 = (bf16[72,2592]{1,0:T(8,128)(2,1)S(1)}, bf16[72,2592]{1,0:T(8,128)(2,1)S(1)}, u32[]{:S(2)}, u32[]{:S(2)}) collective-permute-start(bf16[72,2592]{1,0:T(8,128)(2,1)S(1)} %add_convert_fusion.15), channel_id=1, source_target_pairs={{0,32},{8,40},{16,48},{24,56},{32,0},{40,8},{48,16},{56,24},{64,96... | collective-permute-start | bytes 1119752 | tf_op jit(solution)/shard_map/ppermute | solution.py:63
  464.2 18.8 %collective-permute-start.28 = (bf16[72,3072]{1,0:T(8,128)(2,1)S(1)}, bf16[72,3072]{1,0:T(8,128)(2,1)S(1)}, u32[]{:S(2)}, u32[]{:S(2)}) collective-permute-start(bf16[72,3072]{1,0:T(8,128)(2,1)S(1)} %add_convert_fusion.9), channel_id=1, source_target_pairs={{0,64},{8,72},{16,80},{24,88},{32,96},{40,104},{48,112},{56,120},{... | collective-permute-start | bytes 1327112 | tf_op jit(solution)/shard_map/ppermute | solution.py:63
  471.5 19.7 %collective-permute-start.21 = (bf16[72,2592]{1,0:T(8,128)(2,1)S(1)}, bf16[72,2592]{1,0:T(8,128)(2,1)S(1)}, u32[]{:S(2)}, u32[]{:S(2)}) collective-permute-start(bf16[72,2592]{1,0:T(8,128)(2,1)S(1)} %add_convert_fusion.14), channel_id=1, source_target_pairs={{0,64},{8,72},{16,80},{24,88},{32,96},{40,104},{48,112},{56,120},{... | collective-permute-start | bytes 1119752 | tf_op jit(solution)/shard_map/ppermute | solution.py:63
  483.1 12.8 %collective-permute-start.29 = (bf16[72,3072]{1,0:T(8,128)(2,1)S(1)}, bf16[72,3072]{1,0:T(8,128)(2,1)S(1)}, u32[]{:S(2)}, u32[]{:S(2)}) collective-permute-start(bf16[72,3072]{1,0:T(8,128)(2,1)S(1)} %add_convert_fusion.8.refs_4_), channel_id=1, source_target_pairs={{0,8},{8,0},{16,24},{24,16},{32,40},{40,32},{48,56},{56,48},{64,72... | collective-permute-start | bytes 1327112 | tf_op jit(solution)/shard_map/ppermute | solution.py:37
  491.4 5.1 %collective-permute-start.22 = (bf16[72,2592]{1,0:T(8,128)(2,1)S(1)}, bf16[72,2592]{1,0:T(8,128)(2,1)S(1)}, u32[]{:S(2)}, u32[]{:S(2)}) collective-permute-start(bf16[72,2592]{1,0:T(8,128)(2,1)S(1)} %add_convert_fusion.13.refs_0_), channel_id=1, source_target_pairs={{0,8},{8,0},{16,24},{24,16},{32,40},{40,32},{48,56},{56,48},{64,72... | collective-permute-start | bytes 1119752 | tf_op jit(solution)/shard_map/ppermute | solution.py:37
  (87 other events, 320.4 us)
Sparse Core Ops, SparseCore 0:
  28.3 75.4 all-gather.2
  106.1 76.4 all-gather.4
  271.6 83.0 reduce-scatter.8
  367.2 86.3 reduce-scatter.6
where the time goes:
time: 514 us; the launch traced here: 507 us
  waiting for transfers between devices  166 us (32%)
  Pallas kernels  79.5 us (15%)
  starting transfers between devices  73.2 us (14%)
  local copies, waits for them, and re-layouts  55.5 us (11%)
  other arithmetic  44.9 us (9%)
  matrix products  44 us (9%)
  blocking collectives  25.2 us (5%)
  between operations  18.5 us (4%)
    all_to_all x3, waiting for transfers between devices, over_chips(): lax.all_to_all(x, 'ctx', 0, 0, axis_index_groups=SAME_CORE, tiled=True)  52.5 us
    pallas_call x2, Pallas kernels, attention_back(): pl.pallas_call(backward_kernel, grid_spec=pltpu.PrefetchScalarGridSpec(nu...  45.5 us
    all_to_all x4, waiting for transfers between devices, over_fsdp(): return lax.all_to_all(x, 'fsdp', 0, 0, tiled=True)  39.8 us
    pallas_call x2, Pallas kernels, attention(): pl.pallas_call(forward_kernel, grid_spec=pltpu.PrefetchScalarGridSpec(num...  31.9 us
    dot_general x26, matrix products, ein(): return jnp.einsum(spec, a, b, preferred_element_type=F32)  30.9 us
    ppermute x21, starting transfers between devices, to_partner(): return lax.ppermute(x, 'ctx', PARTNER)  27.9 us
    ppermute x9, waiting for transfers between devices, sum_chips(): x = sum_pair(x, lax.ppermute(x, 'ctx', [(i, i ^ bit) for i in range(CTX)]))  26.3 us
    unnamed x5, waiting for transfers between devices  26.1 us
  transfers between devices with their start and end apart: 41, of which 17 were waited for; matrix products, arithmetic and copies ran while one was open for 23% of the time, Pallas kernels for 11%

commit v1 on v0

--- a/solution.py
+++ b/solution.py
@@ -240,6 +240,9 @@
         ),
         out_shape=[HEAD_SHAPE, LSE_SHAPE],
         compiler_params=KERNEL_PARAMS,
+        cost_estimate=pl.CostEstimate(
+            flops=4 * 36 * BLK * HEADS * BLK * 256, transcendentals=36 * BLK * HEADS * BLK, bytes_accessed=50 * 10**6
+        ),
         name="attention",
     )(scalars, q_t, own, other)
 
@@ -264,6 +267,9 @@
         ),
         out_shape=[HEAD_SHAPE, KV_SHAPE, KV_SHAPE],
         compiler_params=KERNEL_PARAMS,
+        cost_estimate=pl.CostEstimate(
+            flops=10 * 36 * BLK * HEADS * BLK * 256, transcendentals=36 * BLK * HEADS * BLK, bytes_accessed=75 * 10**6
+        ),
         name="attention_back",
     )(scalars, q_t, own, other, o_t, do_t, lse)
 
@@ -419,14 +425,15 @@
         if layer == 0:
             kv_own, late = lax.optimization_barrier((kv_own, proj_pack(1)))
             late = gather_fsdp(late)
-        else:
-            mlps.append(mlp_halves(pack1))
         kv_other = to_partner(kv_own)
         o_t, lse = attention(scalars, q_t, kv_own, kv_other)
         if layer == 0:
             o_t, pack0, late = lax.optimization_barrier((o_t, pack0, late))
             mlps.append(mlp_halves(pack0))
             projs.append(whole_proj(late))
+        else:
+            o_t, pack1 = lax.optimization_barrier((o_t, pack1))
+            mlps.append(mlp_halves(pack1))
         attn_out = o_t.astype(BF16).reshape(Q_ROWS, ROWS)
         mid = hidden + ein("at,ad->td", attn_out, wout)
         unit_m, rms_m = normed(mid)
@@ -481,6 +488,8 @@
             sum_pair(wd_parts[0], to_partner(wd_parts[1])).reshape(D, HALF),
             sum_pair(wout_mine, to_partner(wout_theirs)),
         ]
+        if layer == 1:
+            do_t, d_mlp = lax.optimization_barrier((do_t, d_mlp))
         share = lax.psum_scatter(
             jnp.concatenate(d_mlp, 1), "fsdp", scatter_dimension=0, tiled=True
         )

time: 514 us -> 510 us (level)
  blocking collectives: 25.2 us -> 46.4 us
  waiting for transfers between devices: 166 us -> 147 us
  local copies, waits for them, and re-layouts: 55.5 us -> 64.5 us
  starting transfers between devices: 73.2 us -> 64.8 us
    all_to_all x4 -> x3, waiting for transfers between devices: 39.8 us -> 14.4 us  [over_fsdp(): return lax.all_to_all(x, 'fsdp', 0, 0, tiled=True)]
    all_gather x1, waiting for transfers between devices: 20.3 us -> 0.01 us  [local(): pack1 = lax.all_gather(mlp_pack(1), 'fsdp', axis=0, tiled=True)]
    all_to_all x0 -> x1, blocking collectives: none -> 19.8 us  [over_fsdp(): return lax.all_to_all(x, 'fsdp', 0, 0, tiled=True)]
    all_to_all x3, waiting for transfers between devices: 52.5 us -> 64.8 us  [over_chips(): lax.all_to_all(x, 'ctx', 0, 0, axis_index_groups=SAME_CORE, tiled=True)]
    unnamed x188, local copies, waits for them, and re-layouts: 11.9 us -> 19.7 us
    ppermute x21, waiting for transfers between devices: 1.34 us -> 8.12 us  [to_partner(): return lax.ppermute(x, 'ctx', PARTNER)]
    all_to_all x4 -> x3, starting transfers between devices: 20.6 us -> 16.3 us  [over_fsdp(): return lax.all_to_all(x, 'fsdp', 0, 0, tiled=True)]
  transfers between devices with their start and end apart: 41 -> 40, of which waited for: 17 -> 14; matrix products, arithmetic and copies ran while one was open for 23% -> 21% of each run, Pallas kernels for 11% -> 11%
where the time goes in v1:
time: 510 us; the launch traced here: 502 us
  waiting for transfers between devices  147 us (29%)
  Pallas kernels  77.7 us (15%)
  starting transfers between devices  64.8 us (13%)
  local copies, waits for them, and re-layouts  64.5 us (13%)
  blocking collectives  46.4 us (9%)
  other arithmetic  42 us (8%)
  matrix products  41.7 us (8%)
  between operations  18.4 us (4%)
    all_to_all x3, waiting for transfers between devices, over_chips(): lax.all_to_all(x, 'ctx', 0, 0, axis_index_groups=SAME_CORE, tiled=True)  64.8 us
    pallas_call x2, Pallas kernels, attention_back(): pl.pallas_call(backward_kernel, grid_spec=pltpu.PrefetchScalarGridSpec(nu...  44.7 us
    ppermute x9, waiting for transfers between devices, sum_chips(): x = sum_pair(x, lax.ppermute(x, 'ctx', [(i, i ^ bit) for i in range(CTX)]))  31 us
    pallas_call x2, Pallas kernels, attention(): pl.pallas_call(forward_kernel, grid_spec=pltpu.PrefetchScalarGridSpec(num...  30.9 us
    dot_general x26, matrix products, ein(): return jnp.einsum(spec, a, b, preferred_element_type=F32)  30 us
    unnamed x5, waiting for transfers between devices  28.2 us
    all_to_all x1, blocking collectives, over_chips(): lax.all_to_all(x, 'ctx', 0, 0, axis_index_groups=SAME_CORE, tiled=True)  26.5 us
    ppermute x21, starting transfers between devices, to_partner(): return lax.ppermute(x, 'ctx', PARTNER)  25.1 us
  transfers between devices with their start and end apart: 40, of which 14 were waited for; matrix products, arithmetic and copies ran while one was open for 21% of the time, Pallas kernels for 11%

profile of v1, /device:TPU:1, one launch (start us, length us, event | category | flops | bytes accessed | tf_op | source)
XLA Modules:
  0.0 501.9 jit_solution(11727726655534900989)
XLA Ops:
  18.6 8.2 %all-to-all-start = ((bf16[8,72,772]{2,1,0:T(8,128)(2,1)}), bf16[8,72,772]{2,1,0:T(8,128)(2,1)S(1)}, u32[]{:S(2)}, u32[]{:S(2)}) async-start(bf16[8,72,772]{2,1,0:T(8,128)(2,1)} %broadcast_in_dim.16), calls=%async_computation | async-start | bytes 2064384 | tf_op jit(solution)/shard_map/all_to_all | solution.py:45
  29.5 14.4 %all-to-all-done = bf16[8,72,772]{2,1,0:T(8,128)(2,1)S(1)} async-done(((bf16[8,72,772]{2,1,0:T(8,128)(2,1)}), bf16[8,72,772]{2,1,0:T(8,128)(2,1)S(1)}, u32[]{:S(2)}, u32[]{:S(2)}) %all-to-all-start) | async-done | bytes 889376 | tf_op jit(solution)/shard_map/all_to_all | solution.py:45
  51.5 4.8 all-to-all-start.1
  57.1 23.2 %all-to-all-done.1.own_ref = bf16[8,2,3,64,256]{4,3,2,1,0:T(8,128)(2,1)S(1)} async-done(((bf16[8,2,3,64,256]{4,3,2,1,0:T(8,128)(2,1)}), bf16[8,2,3,64,256]{4,3,2,1,0:T(8,128)(2,1)S(1)}, u32[]{:S(2)}, u32[]{:S(2)}) %all-to-all-start.1) | async-done | bytes 1572896 | tf_op jit(solution)/shard_map/all_to_all | solution.py:41
  83.2 2.0 select_n.165
  88.9 4.4 all-to-all-start.2
  101.0 15.5 %attention.2 = (f32[9,64,256]{2,1,0:T(8,128)S(1)}, f32[3,2,1,384]{3,2,1,0:T(1,128)S(1)}) custom-call(s32[39]{0:T(128)S(1)} %concatenate.92.sc, bf16[9,64,256]{2,1,0:T(8,128)(2,1)S(1)} %fusion.29.q_ref, bf16[8,2,3,64,256]{4,3,2,1,0:T(8,128)(2,1)S(1)} %all-to-all-done.1.own_ref, bf16[8,2,3,64,256]{4,3,2,1,0:T(8,128)(2,1)S(1)} %copy-done.14), custom_call_target="tpu_custom_call" | custom-call | flops 5435817984 | bytes 50000000 | tf_op jit(solution)/shard_map/attention/pallas_call | solution.py:225
  117.3 3.1 slice.286
  125.6 2.4 fusion.79
  130.7 2.9 fusion.85
  136.6 26.5 %all_to_all.40.own_ref = bf16[8,2,3,64,256]{4,3,2,1,0:T(8,128)(2,1)S(1)} all-to-all(bf16[8,2,3,64,256]{4,3,2,1,0:T(8,128)(2,1)S(1)} %broadcast_in_dim.21), channel_id=1, replica_groups={{0,16,32,48,64,80,96,112},{8,24,40,56,72,88,104,120},{1,17,33,49,65,81,..., dimensions={0} | all-to-all | bytes 3145728 | tf_op jit(solution)/shard_map/all_to_all | solution.py:41
  163.2 2.0 collective-permute-start.5
  165.2 3.0 collective-permute-done.5.other_ref
  168.2 15.5 %attention.3 = (f32[9,64,256]{2,1,0:T(8,128)S(1)}, f32[3,2,1,384]{3,2,1,0:T(1,128)S(1)}) custom-call(s32[39]{0:T(128)S(1)} %concatenate.92.sc, bf16[9,64,256]{2,1,0:T(8,128)(2,1)S(1)} %fusion.26.q_ref, bf16[8,2,3,64,256]{4,3,2,1,0:T(8,128)(2,1)S(1)} %all_to_all.40.own_ref, bf16[8,2,3,64,256]{4,3,2,1,0:T(8,128)(2,1)S(1)} %collective-permute-done.5.other_ref), custom_call_target="tpu_custom_call" | custom-call | flops 5435817984 | bytes 50000000 | tf_op jit(solution)/shard_map/attention/pallas_call | solution.py:225
  186.4 2.8 slice.309
  189.6 2.2 slice.312
  191.8 3.4 reshape.317
  195.2 2.2 copy.76
  197.6 2.4 multiply_reduce_fusion.6
  203.3 2.3 fusion.86
  209.2 2.2 multiply_reduce_fusion
  217.1 2.2 copy.79
  219.3 3.3 reshape.320
  222.6 3.8 add_convert_fusion.1
  226.4 22.0 %attention_back.2 = (f32[9,64,256]{2,1,0:T(8,128)S(1)}, bf16[8,2,3,64,256]{4,3,2,1,0:T(8,128)(2,1)S(1)}, bf16[8,2,3,64,256]{4,3,2,1,0:T(8,128)(2,1)S(1)}) custom-call(s32[39]{0:T(128)S(1)} %concatenate.92.sc, bf16[9,64,256]{2,1,0:T(8,128)(2,1)S(1)} %copy-done.12, bf16[8,2,3,64,256]{4,3,2,1,0:T(8,128)(2,1)S(1)} %all_to_all.40.own_ref, ...), custom_call_target="tpu_custom_call" | custom-call | flops 13589544960 | bytes 75000000 | tf_op jit(solution)/shard_map/attention_back/pallas_call | solution.py:251
  249.4 3.2 collective-permute-done.11
  254.5 4.4 all-to-all-start.4
  259.0 2.9 pad_maximum_fusion.1
  262.0 21.3 %all-to-all-done.4 = bf16[8,2,3,64,256]{4,3,2,1,0:T(8,128)(2,1)} async-done(((bf16[8,2,3,64,256]{4,3,2,1,0:T(8,128)(2,1)}), bf16[8,2,3,64,256]{4,3,2,1,0:T(8,128)(2,1)}, u32[]{:S(2)}, u32[]{:S(2)}) %all-to-all-start.4) | async-done | bytes 1572896 | tf_op jit(solution)/shard_map/all_to_all | solution.py:41
  294.3 2.4 multiply_reduce_fusion.2
  307.3 22.7 %attention_back.3 = (f32[9,64,256]{2,1,0:T(8,128)S(1)}, bf16[8,2,3,64,256]{4,3,2,1,0:T(8,128)(2,1)S(1)}, bf16[8,2,3,64,256]{4,3,2,1,0:T(8,128)(2,1)}) custom-call(s32[39]{0:T(128)S(1)} %concatenate.92.sc, bf16[9,64,256]{2,1,0:T(8,128)(2,1)S(1)} %copy-done.10, bf16[8,2,3,64,256]{4,3,2,1,0:T(8,128)(2,1)S(1)} %all-to-all-done.1.own_ref, ...), custom_call_target="tpu_custom_call" | custom-call | flops 13589544960 | bytes 75000000 | tf_op jit(solution)/shard_map/attention_back/pallas_call | solution.py:251
  333.6 2.3 reshape.326
  335.9 2.6 add_convert_fusion
  341.4 19.8 %all_to_all.41 = bf16[8,72,480]{2,1,0:T(8,128)(2,1)S(1)} all-to-all(bf16[8,72,480]{2,1,0:T(8,128)(2,1)S(1)} %bitcast.170), channel_id=1, replica_groups=mesh['ctx'=16,'fsdp'=8] {'fsdp'}, dimensions={0} | all-to-all | bytes 1105920 | tf_op jit(solution)/shard_map/all_to_all | solution.py:45
  361.9 3.2 add_convert_fusion.2
  365.2 3.7 all-to-all-start.6
  371.5 20.3 %all-to-all-done.6 = bf16[8,2,3,64,256]{4,3,2,1,0:T(8,128)(2,1)S(1)} async-done(((bf16[8,2,3,64,256]{4,3,2,1,0:T(8,128)(2,1)}), bf16[8,2,3,64,256]{4,3,2,1,0:T(8,128)(2,1)S(1)}, u32[]{:S(2)}, u32[]{:S(2)}) %all-to-all-start.6) | async-done | bytes 1572896 | tf_op jit(solution)/shard_map/all_to_all | solution.py:41
  400.6 3.7 all-to-all-start.7
  404.3 13.9 %collective-permute-done.26 = bf16[72,3072]{1,0:T(8,128)(2,1)} collective-permute-done((bf16[72,3072]{1,0:T(8,128)(2,1)S(1)}, bf16[72,3072]{1,0:T(8,128)(2,1)}, u32[]{:S(2)}, u32[]{:S(2)}) %collective-permute-start.26) | collective-permute-done | bytes 442400 | tf_op jit(solution)/shard_map/ppermute | solution.py:63
  421.0 27.5 %reduce-scatter.7.cloned.1.call-done = bf16[72,2592]{1,0:T(8,128)(2,1)} async-done(((bf16[576,2592]{1,0:T(8,128)(2,1)}), bf16[72,2592]{1,0:T(8,128)(2,1)}) %reduce-scatter.7.cloned.1.call-update) | async-done | bytes 373264
  451.1 5.5 %collective-permute-done.22 = bf16[72,2592]{1,0:T(8,128)(2,1)S(1)} collective-permute-done((bf16[72,2592]{1,0:T(8,128)(2,1)}, bf16[72,2592]{1,0:T(8,128)(2,1)S(1)}, u32[]{:S(2)}, u32[]{:S(2)}) %collective-permute-start.22) | collective-permute-done | bytes 373280 | tf_op jit(solution)/shard_map/ppermute | solution.py:63
  458.1 2.6 collective-permute-start.28
  461.3 2.7 collective-permute-done.23
  464.0 2.7 collective-permute-start.24
  466.7 8.9 %collective-permute-done.28 = bf16[72,3072]{1,0:T(8,128)(2,1)S(1)} collective-permute-done((bf16[72,3072]{1,0:T(8,128)(2,1)S(1)}, bf16[72,3072]{1,0:T(8,128)(2,1)S(1)}, u32[]{:S(2)}, u32[]{:S(2)}) %collective-permute-start.28) | collective-permute-done | bytes 442400 | tf_op jit(solution)/shard_map/ppermute | solution.py:63
  475.7 8.3 %collective-permute-start.29 = (bf16[72,3072]{1,0:T(8,128)(2,1)S(1)}, bf16[72,3072]{1,0:T(8,128)(2,1)S(1)}, u32[]{:S(2)}, u32[]{:S(2)}) collective-permute-start(bf16[72,3072]{1,0:T(8,128)(2,1)S(1)} %add_convert_fusion.8.refs_4_), channel_id=1, source_target_pairs={{0,8},{8,0},{16,24},{24,16},{32,40},{40,32},{48,56},{56,48},{64,72... | collective-permute-start | bytes 1327112 | tf_op jit(solution)/shard_map/ppermute | solution.py:37
  485.7 4.3 collective-permute-start.25
  492.9 2.1 unpack.1
  (405 shorter events, 115.9 us)
Async XLA Ops:
  18.6 25.3 %all-to-all-start = ((bf16[8,72,772]{2,1,0:T(8,128)(2,1)}), bf16[8,72,772]{2,1,0:T(8,128)(2,1)S(1)}, u32[]{:S(2)}, u32[]{:S(2)}) async-start(bf16[8,72,772]{2,1,0:T(8,128)(2,1)} %broadcast_in_dim.16), calls=%async_computation | async-start | bytes 2064384 | tf_op jit(solution)/shard_map/all_to_all | solution.py:45
  26.8 90.5 %all-gather.3.cloned.1.call-start = ((), (), s32[]{:S(2)}) async-start(), calls=%async_computation.10 | async-start | bytes 2985984 | tf_op jit(solution)/shard_map/all_gather | solution.py:386
  44.0 3.2 collective-permute-start
  51.5 28.8 %all-to-all-start.1 = ((bf16[8,2,3,64,256]{4,3,2,1,0:T(8,128)(2,1)}), bf16[8,2,3,64,256]{4,3,2,1,0:T(8,128)(2,1)S(1)}, u32[]{:S(2)}, u32[]{:S(2)}) async-start(bf16[8,2,3,64,256]{4,3,2,1,0:T(8,128)(2,1)} %broadcast_in_dim.19), calls=%async_computation.1 | async-start | bytes 3145728 | tf_op jit(solution)/shard_map/all_to_all | solution.py:41
  56.3 130.0 %all-gather.5.cloned.1.call-start = ((), (), s32[]{:S(2)}) async-start(), calls=%async_computation.11 | async-start | bytes 2985984 | tf_op jit(solution)/shard_map/all_gather | solution.py:388
  80.4 18.1 %collective-permute-start.1 = (bf16[8,2,3,64,256]{4,3,2,1,0:T(8,128)(2,1)S(1)}, bf16[8,2,3,64,256]{4,3,2,1,0:T(8,128)(2,1)S(1)}, u32[]{:S(2)}, u32[]{:S(2)}) collective-permute-start(bf16[8,2,3,64,256]{4,3,2,1,0:T(8,128)(2,1)S(1)} %all-to-all-done.1.own_ref), channel_id=1, source_target_pairs={{0,8},{8,0},{16,24},{24,16},{32,40},{40,32},{48,56},{56,48},{64,72... | collective-permute-start | bytes 4718600 | tf_op jit(solution)/shard_map/ppermute | solution.py:37
  88.9 28.4 %all-to-all-start.2 = ((bf16[8,72,768]{2,1,0:T(8,128)(2,1)}), bf16[8,72,768]{2,1,0:T(8,128)(2,1)}, u32[]{:S(2)}, u32[]{:S(2)}) async-start(bf16[8,72,768]{2,1,0:T(8,128)(2,1)} %broadcast_in_dim.20), calls=%async_computation.2 | async-start | bytes 1769472 | tf_op jit(solution)/shard_map/all_to_all | solution.py:45
  120.4 10.3 %collective-permute-start.2 = (bf16[576,1536]{1,0:T(8,128)(2,1)}, bf16[576,1536]{1,0:T(8,128)(2,1)}, u32[]{:S(2)}, u32[]{:S(2)}) collective-permute-start(bf16[576,1536]{1,0:T(8,128)(2,1)} %slice.286), channel_id=1, source_target_pairs={{0,8},{8,0},{16,24},{24,16},{32,40},{40,32},{48,56},{56,48},{64,72... | collective-permute-start | bytes 5308424 | tf_op jit(solution)/shard_map/ppermute | solution.py:37
  125.0 8.8 %collective-permute-start.3 = (bf16[768,576]{0,1:T(8,128)(2,1)}, bf16[768,576]{0,1:T(8,128)(2,1)S(1)}, u32[]{:S(2)}, u32[]{:S(2)}) collective-permute-start(bf16[768,576]{0,1:T(8,128)(2,1)} %copy.73), channel_id=1, source_target_pairs={{0,8},{8,0},{16,24},{24,16},{32,40},{40,32},{48,56},{56,48},{64,72... | collective-permute-start | bytes 2654216 | tf_op jit(solution)/shard_map/ppermute | solution.py:37
  125.4 3.9 collective-permute-start.4
  163.2 5.0 %collective-permute-start.5 = (bf16[8,2,3,64,256]{4,3,2,1,0:T(8,128)(2,1)S(1)}, bf16[8,2,3,64,256]{4,3,2,1,0:T(8,128)(2,1)S(1)}, u32[]{:S(2)}, u32[]{:S(2)}) collective-permute-start(bf16[8,2,3,64,256]{4,3,2,1,0:T(8,128)(2,1)S(1)} %all_to_all.40.own_ref), channel_id=1, source_target_pairs={{0,8},{8,0},{16,24},{24,16},{32,40},{40,32},{48,56},{56,48},{64,72... | collective-permute-start | bytes 4718600 | tf_op jit(solution)/shard_map/ppermute | solution.py:37
  189.2 14.1 %collective-permute-start.6 = (bf16[576,1536]{1,0:T(8,128)(2,1)}, bf16[576,1536]{1,0:T(8,128)(2,1)}, u32[]{:S(2)}, u32[]{:S(2)}) collective-permute-start(bf16[576,1536]{1,0:T(8,128)(2,1)} %slice.309), channel_id=1, source_target_pairs={{0,8},{8,0},{16,24},{24,16},{32,40},{40,32},{48,56},{56,48},{64,72... | collective-permute-start | bytes 5308424 | tf_op jit(solution)/shard_map/ppermute | solution.py:37
  197.4 8.1 %collective-permute-start.7 = (bf16[768,576]{0,1:T(8,128)(2,1)}, bf16[768,576]{0,1:T(8,128)(2,1)S(1)}, u32[]{:S(2)}, u32[]{:S(2)}) collective-permute-start(bf16[768,576]{0,1:T(8,128)(2,1)} %copy.76), channel_id=1, source_target_pairs={{0,8},{8,0},{16,24},{24,16},{32,40},{40,32},{48,56},{56,48},{64,72... | collective-permute-start | bytes 2654216 | tf_op jit(solution)/shard_map/ppermute | solution.py:37
  200.0 11.7 %copy-start.25 = (f32[256,576]{0,1:T(8,128)}, f32[256,576]{0,1:T(8,128)S(1)}, u32[]{:S(2)}) copy-start(f32[256,576]{0,1:T(8,128)S(1)} %get-tuple-element.144) | copy-start | bytes 1769476
  202.4 13.3 %copy-start.61 = (bf16[256,768]{1,0:T(8,128)(2,1)}, bf16[256,768]{1,0:T(8,128)(2,1)S(1)}, u32[]{:S(2)}) copy-start(bf16[256,768]{1,0:T(8,128)(2,1)S(1)} %get-tuple-element.113) | copy-start | bytes 1179652
  208.7 13.9 %collective-permute-start.8 = (bf16[576,1536]{1,0:T(8,128)(2,1)}, bf16[576,1536]{1,0:T(8,128)(2,1)}, u32[]{:S(2)}, u32[]{:S(2)}) collective-permute-start(bf16[576,1536]{1,0:T(8,128)(2,1)} %convolution_convert_fusion.2), channel_id=1, source_target_pairs={{0,8},{8,0},{16,24},{24,16},{32,40},{40,32},{48,56},{56,48},{64,72... | collective-permute-start | bytes 5308424 | tf_op jit(solution)/shard_map/ppermute | solution.py:37
  211.5 4.2 collective-permute-start.9
  212.5 2.1 collective-permute-start.10
  249.2 3.4 collective-permute-start.11
  254.5 28.8 %all-to-all-start.4 = ((bf16[8,2,3,64,256]{4,3,2,1,0:T(8,128)(2,1)}), bf16[8,2,3,64,256]{4,3,2,1,0:T(8,128)(2,1)}, u32[]{:S(2)}, u32[]{:S(2)}) async-start(bf16[8,2,3,64,256]{4,3,2,1,0:T(8,128)(2,1)} %add_convert_fusion.3), calls=%async_computation.4 | async-start | bytes 3145728 | tf_op jit(solution)/shard_map/all_to_all | solution.py:41
  259.0 112.5 %reduce-scatter.9.cloned.1.call-start = ((), (), s32[]{:S(2)}) async-start(), calls=%async_computation.13 | async-start | bytes 3483648
  262.0 23.1 %copy-start.8 = (f32[9,64,256]{2,1,0:T(8,128)S(1)}, f32[9,64,256]{2,1,0:T(8,128)}, u32[]{:S(2)}) copy-start(f32[9,64,256]{2,1,0:T(8,128)} %copy-done.7) | copy-start | bytes 1769476
  262.0 23.1 %copy-start.85 = (f32[32,256]{1,0:T(8,128)S(1)}, f32[32,256]{1,0:T(8,128)}, u32[]{:S(2)}) copy-start(f32[32,256]{1,0:T(8,128)} %get-tuple-element.138) | copy-start | bytes 98308
  262.0 186.5 %reduce-scatter.7.cloned.1.call-start = ((), (), s32[]{:S(2)}) async-start(), calls=%async_computation.12 | async-start | bytes 3483648
  291.0 13.4 %collective-permute-start.12 = (bf16[576,480]{1,0:T(8,128)(2,1)S(1)}, bf16[576,480]{1,0:T(8,128)(2,1)S(1)}, u32[]{:S(2)}, u32[]{:S(2)}) collective-permute-start(bf16[576,480]{1,0:T(8,128)(2,1)S(1)} %broadcast_select_fusion.5), channel_id=1, source_target_pairs={{0,8},{8,0},{16,24},{24,16},{32,40},{40,32},{48,56},{56,48},{64,72... | collective-permute-start | bytes 1658888 | tf_op jit(solution)/shard_map/ppermute | solution.py:37
  301.2 4.6 collective-permute-start.21
  305.7 30.2 %collective-permute-start.19 = (bf16[576,1536]{1,0:T(8,128)(2,1)}, bf16[576,1536]{1,0:T(8,128)(2,1)}, u32[]{:S(2)}, u32[]{:S(2)}) collective-permute-start(bf16[576,1536]{1,0:T(8,128)(2,1)} %convolution_convert_fusion), channel_id=1, source_target_pairs={{0,8},{8,0},{16,24},{24,16},{32,40},{40,32},{48,56},{56,48},{64,72... | collective-permute-start | bytes 5308424 | tf_op jit(solution)/shard_map/ppermute | solution.py:37
  306.8 24.1 %collective-permute-start.20 = (bf16[768,576]{0,1:T(8,128)(2,1)S(1)}, bf16[768,576]{0,1:T(8,128)(2,1)S(1)}, u32[]{:S(2)}, u32[]{:S(2)}) collective-permute-start(bf16[768,576]{0,1:T(8,128)(2,1)S(1)} %convolution_convert_fusion.6), channel_id=1, source_target_pairs={{0,8},{8,0},{16,24},{24,16},{32,40},{40,32},{48,56},{56,48},{64,72... | collective-permute-start | bytes 2654216 | tf_op jit(solution)/shard_map/ppermute | solution.py:37
  330.9 31.1 %collective-permute-start.13 = (bf16[8,2,3,64,256]{4,3,2,1,0:T(8,128)(2,1)}, bf16[8,2,3,64,256]{4,3,2,1,0:T(8,128)(2,1)}, u32[]{:S(2)}, u32[]{:S(2)}) collective-permute-start(bf16[8,2,3,64,256]{4,3,2,1,0:T(8,128)(2,1)} %get-tuple-element.62), channel_id=1, source_target_pairs={{0,8},{8,0},{16,24},{24,16},{32,40},{40,32},{48,56},{56,48},{64,72... | collective-permute-start | bytes 4718600 | tf_op jit(solution)/shard_map/ppermute | solution.py:37
  365.2 26.6 %all-to-all-start.6 = ((bf16[8,2,3,64,256]{4,3,2,1,0:T(8,128)(2,1)}), bf16[8,2,3,64,256]{4,3,2,1,0:T(8,128)(2,1)S(1)}, u32[]{:S(2)}, u32[]{:S(2)}) async-start(bf16[8,2,3,64,256]{4,3,2,1,0:T(8,128)(2,1)} %add_convert_fusion.2), calls=%async_computation.6 | async-start | bytes 3145728 | tf_op jit(solution)/shard_map/all_to_all | solution.py:41
  371.4 20.7 %copy-start.6 = (f32[9,64,256]{2,1,0:T(8,128)S(1)}, f32[9,64,256]{2,1,0:T(8,128)}, u32[]{:S(2)}) copy-start(f32[9,64,256]{2,1,0:T(8,128)} %copy-done.5) | copy-start | bytes 1769476
  371.4 20.7 %copy-start.79 = (f32[32,256]{1,0:T(8,128)S(1)}, f32[32,256]{1,0:T(8,128)}, u32[]{:S(2)}) copy-start(f32[32,256]{1,0:T(8,128)} %get-tuple-element.140) | copy-start | bytes 98308
  371.4 20.7 %copy-start.86 = (f32[32,256]{1,0:T(8,128)S(1)}, f32[32,256]{1,0:T(8,128)}, u32[]{:S(2)}) copy-start(f32[32,256]{1,0:T(8,128)} %get-tuple-element.138) | copy-start | bytes 98308
  394.5 3.6 collective-permute-start.14
  396.3 21.9 %collective-permute-start.26 = (bf16[72,3072]{1,0:T(8,128)(2,1)S(1)}, bf16[72,3072]{1,0:T(8,128)(2,1)}, u32[]{:S(2)}, u32[]{:S(2)}) collective-permute-start(bf16[72,3072]{1,0:T(8,128)(2,1)S(1)} %pad_maximum_fusion.22), channel_id=1, source_target_pairs={{0,16},{8,24},{16,0},{24,8},{32,48},{40,56},{48,32},{56,40},{64,80... | collective-permute-start | bytes 1327112 | tf_op jit(solution)/shard_map/ppermute | solution.py:63
  400.6 48.3 %copy-start.22 = (f32[256,576]{0,1:T(8,128)S(1)}, f32[256,576]{0,1:T(8,128)}, u32[]{:S(2)}) copy-start(f32[256,576]{0,1:T(8,128)} %copy-done.21) | copy-start | bytes 1769476
  400.6 19.9 %all-to-all-start.7 = ((bf16[8,72,484]{2,1,0:T(8,128)(2,1)}), bf16[8,72,484]{2,1,0:T(8,128)(2,1)S(1)}, u32[]{:S(2)}, u32[]{:S(2)}) async-start(bf16[8,72,484]{2,1,0:T(8,128)(2,1)} %bitcast.41), calls=%async_computation.7 | async-start | bytes 1179648 | tf_op jit(solution)/shard_map/all_to_all | solution.py:45
  419.3 38.7 %collective-permute-start.27 = (bf16[72,3072]{1,0:T(8,128)(2,1)S(1)}, bf16[72,3072]{1,0:T(8,128)(2,1)S(1)}, u32[]{:S(2)}, u32[]{:S(2)}) collective-permute-start(bf16[72,3072]{1,0:T(8,128)(2,1)S(1)} %add_convert_fusion.10), channel_id=1, source_target_pairs={{0,32},{8,40},{16,48},{24,56},{32,0},{40,8},{48,16},{56,24},{64,96... | collective-permute-start | bytes 1327112 | tf_op jit(solution)/shard_map/ppermute | solution.py:63
  420.6 29.3 %collective-permute-start.15 = (bf16[72,484]{1,0:T(8,128)(2,1)S(1)}, bf16[72,484]{1,0:T(8,128)(2,1)S(1)}, u32[]{:S(2)}, u32[]{:S(2)}) collective-permute-start(bf16[72,484]{1,0:T(8,128)(2,1)S(1)} %reduce_sum.175), channel_id=1, source_target_pairs={{0,16},{8,24},{16,0},{24,8},{32,48},{40,56},{48,32},{56,40},{64,80... | collective-permute-start | bytes 209096 | tf_op jit(solution)/shard_map/ppermute | solution.py:63
  448.5 8.2 %collective-permute-start.22 = (bf16[72,2592]{1,0:T(8,128)(2,1)}, bf16[72,2592]{1,0:T(8,128)(2,1)S(1)}, u32[]{:S(2)}, u32[]{:S(2)}) collective-permute-start(bf16[72,2592]{1,0:T(8,128)(2,1)} %reduce-scatter.7.cloned.1.call-done), channel_id=1, source_target_pairs={{0,16},{8,24},{16,0},{24,8},{32,48},{40,56},{48,32},{56,40},{64,80... | collective-permute-start | bytes 1119752 | tf_op jit(solution)/shard_map/ppermute | solution.py:63
  449.9 10.8 %collective-permute-start.16 = (bf16[72,484]{1,0:T(8,128)(2,1)S(1)}, bf16[72,484]{1,0:T(8,128)(2,1)S(1)}, u32[]{:S(2)}, u32[]{:S(2)}) collective-permute-start(bf16[72,484]{1,0:T(8,128)(2,1)S(1)} %add_convert_fusion.20), channel_id=1, source_target_pairs={{0,32},{8,40},{16,48},{24,56},{32,0},{40,8},{48,16},{56,24},{64,96... | collective-permute-start | bytes 209096 | tf_op jit(solution)/shard_map/ppermute | solution.py:63
  456.8 7.1 %collective-permute-start.23 = (bf16[72,2592]{1,0:T(8,128)(2,1)S(1)}, bf16[72,2592]{1,0:T(8,128)(2,1)S(1)}, u32[]{:S(2)}, u32[]{:S(2)}) collective-permute-start(bf16[72,2592]{1,0:T(8,128)(2,1)S(1)} %add_convert_fusion.15), channel_id=1, source_target_pairs={{0,32},{8,40},{16,48},{24,56},{32,0},{40,8},{48,16},{56,24},{64,96... | collective-permute-start | bytes 1119752 | tf_op jit(solution)/shard_map/ppermute | solution.py:63
  458.1 17.5 %collective-permute-start.28 = (bf16[72,3072]{1,0:T(8,128)(2,1)S(1)}, bf16[72,3072]{1,0:T(8,128)(2,1)S(1)}, u32[]{:S(2)}, u32[]{:S(2)}) collective-permute-start(bf16[72,3072]{1,0:T(8,128)(2,1)S(1)} %add_convert_fusion.9), channel_id=1, source_target_pairs={{0,64},{8,72},{16,80},{24,88},{32,96},{40,104},{48,112},{56,120},{... | collective-permute-start | bytes 1327112 | tf_op jit(solution)/shard_map/ppermute | solution.py:63
  460.8 23.3 %collective-permute-start.17 = (bf16[72,484]{1,0:T(8,128)(2,1)S(1)}, bf16[72,484]{1,0:T(8,128)(2,1)S(1)}, u32[]{:S(2)}, u32[]{:S(2)}) collective-permute-start(bf16[72,484]{1,0:T(8,128)(2,1)S(1)} %add_convert_fusion.19), channel_id=1, source_target_pairs={{0,64},{8,72},{16,80},{24,88},{32,96},{40,104},{48,112},{56,120},{... | collective-permute-start | bytes 209096 | tf_op jit(solution)/shard_map/ppermute | solution.py:63
  464.0 21.5 %collective-permute-start.24 = (bf16[72,2592]{1,0:T(8,128)(2,1)S(1)}, bf16[72,2592]{1,0:T(8,128)(2,1)S(1)}, u32[]{:S(2)}, u32[]{:S(2)}) collective-permute-start(bf16[72,2592]{1,0:T(8,128)(2,1)S(1)} %add_convert_fusion.14), channel_id=1, source_target_pairs={{0,64},{8,72},{16,80},{24,88},{32,96},{40,104},{48,112},{56,120},{... | collective-permute-start | bytes 1119752 | tf_op jit(solution)/shard_map/ppermute | solution.py:63
  475.7 14.3 %collective-permute-start.29 = (bf16[72,3072]{1,0:T(8,128)(2,1)S(1)}, bf16[72,3072]{1,0:T(8,128)(2,1)S(1)}, u32[]{:S(2)}, u32[]{:S(2)}) collective-permute-start(bf16[72,3072]{1,0:T(8,128)(2,1)S(1)} %add_convert_fusion.8.refs_4_), channel_id=1, source_target_pairs={{0,8},{8,0},{16,24},{24,16},{32,40},{40,32},{48,56},{56,48},{64,72... | collective-permute-start | bytes 1327112 | tf_op jit(solution)/shard_map/ppermute | solution.py:37
  484.1 6.4 %collective-permute-start.18 = (bf16[72,484]{1,0:T(8,128)(2,1)S(1)}, bf16[72,484]{1,0:T(8,128)(2,1)S(1)}, u32[]{:S(2)}, u32[]{:S(2)}) collective-permute-start(bf16[72,484]{1,0:T(8,128)(2,1)S(1)} %add_convert_fusion.18.refs_2_), channel_id=1, source_target_pairs={{0,8},{8,0},{16,24},{24,16},{32,40},{40,32},{48,56},{56,48},{64,72... | collective-permute-start | bytes 209096 | tf_op jit(solution)/shard_map/ppermute | solution.py:37
  485.7 5.7 %collective-permute-start.25 = (bf16[72,2592]{1,0:T(8,128)(2,1)S(1)}, bf16[72,2592]{1,0:T(8,128)(2,1)S(1)}, u32[]{:S(2)}, u32[]{:S(2)}) collective-permute-start(bf16[72,2592]{1,0:T(8,128)(2,1)S(1)} %add_convert_fusion.13.refs_0_), channel_id=1, source_target_pairs={{0,8},{8,0},{16,24},{24,16},{32,40},{40,32},{48,56},{56,48},{64,72... | collective-permute-start | bytes 1119752 | tf_op jit(solution)/shard_map/ppermute | solution.py:37
  (87 other events, 209.7 us)
Sparse Core Ops, SparseCore 0:
  30.5 66.5 all-gather.2
  99.4 82.2 all-gather.4
  263.7 81.8 reduce-scatter.8
  349.4 99.0 reduce-scatter.6

commit v2 on v1

--- a/solution.py
+++ b/solution.py
@@ -281,40 +281,33 @@
 
 
 def unpack_kernel(sc, *refs):
-    mlp0, mlp0_p, qkv0, qkv0_p, all1, all1_p, qkv_ref, out_ref, gu_ref = refs
-
-    def layer_out(layer, halves, qkv_halves, qkv_at, wout_at):
-        for half in range(2):
-            mlp = halves[half]
-            for k in range(2):
-                for i in range(FSDP):
-                    src = k * HALF + i * UNITS
-                    dst = k * FF + i * 2 * UNITS + half * UNITS
-                    gu_ref[layer, :, dst : dst + UNITS] = mlp[:, src : src + UNITS].astype(F32)
-            cut = (Q_ROWS + KV_ROWS) // 2
-            qkv_ref[layer, :, half * cut : (half + 1) * cut] = (
-                qkv_halves[half][:, qkv_at : qkv_at + cut].astype(F32)
-            )
-            cut = D // 2
-            out_ref[layer, :, half * cut : (half + 1) * cut] = (
-                mlp[:, wout_at : wout_at + cut].astype(F32)
-            )
-
-    def both(order):
-        m0, q0, a1 = [mlp0, mlp0_p][::order], [qkv0, qkv0_p][::order], [all1, all1_p][::order]
-        layer_out(0, m0, q0, 0, FF + HALF)
-        layer_out(1, a1, a1, FF + HALF + D // 2, FF + HALF)
+    mlp0, mlp0_p, mlp1, mlp1_p, qkv, qkv_p, qkv_ref, out_ref, gu_ref = refs
+
+    def write(order):
+        for layer, pair in enumerate(((mlp0, mlp0_p), (mlp1, mlp1_p))):
+            for half, mlp in enumerate(pair[::order]):
+                for k in range(2):
+                    for i in range(FSDP):
+                        src = k * HALF + i * UNITS
+                        dst = k * FF + i * 2 * UNITS + half * UNITS
+                        gu_ref[layer, :, dst : dst + UNITS] = mlp[:, src : src + UNITS].astype(F32)
+                cut = D // 2
+                out_ref[layer, :, half * cut : (half + 1) * cut] = (
+                    mlp[:, FF + HALF : FF + HALF + cut].astype(F32)
+                )
+        for layer, src in enumerate((qkv, qkv_p)[::order]):
+            qkv_ref[layer] = src[:, : Q_ROWS + KV_ROWS].astype(F32)
 
     @pl.when(sc[0] == 0)
     def _():
-        both(1)
+        write(1)
 
     @pl.when(sc[0] != 0)
     def _():
-        both(-1)
-
-
-def unpack(core, mlp0, mlp0_p, qkv0, qkv0_p, all1, all1_p):
+        write(-1)
+
+
+def unpack(core, *shares):
     return pl.pallas_call(
         unpack_kernel,
         grid_spec=pltpu.PrefetchScalarGridSpec(
@@ -330,7 +323,7 @@
         ],
         compiler_params=pltpu.CompilerParams(vmem_limit_bytes=40 * 2**20),
         name="unpack",
-    )(core, mlp0, mlp0_p, qkv0, qkv0_p, all1, all1_p)
+    )(core, *shares)
 
 
 def rotate(x, cosine, sine):
@@ -380,20 +373,19 @@
         proj = jnp.concatenate([w_qkv[layer], w_out[layer]], 1)
         return my_half(proj[:, :cut], proj[:, cut:])
 
-    pack0, first = lax.optimization_barrier(
-        (mlp_pack(0), jnp.concatenate([proj_pack(0), gain_cols], 1))
-    )
-    pack0 = lax.all_gather(pack0, "fsdp", axis=0, tiled=True)
-    first = gather_fsdp(first)
+    first = jnp.concatenate([proj_pack(0), gain_cols], 1)
+    first = jnp.broadcast_to(first[None], (FSDP,) + first.shape)
+    first, w_gate_up, w_down = lax.optimization_barrier((first, w_gate_up, w_down))
+    first = over_fsdp(first).reshape(D, -1)
+    pack0 = lax.all_gather(mlp_pack(0), "fsdp", axis=0, tiled=True)
     pack1 = lax.all_gather(mlp_pack(1), "fsdp", axis=0, tiled=True)
     gains = jnp.transpose(first[:, cut:].astype(F32)).reshape(LAYERS, 2, D)
 
     def whole_proj(own):
         return jnp.concatenate(in_order(own, to_partner(own)), 1)
 
-    def mlp_halves(pack):
-        wgu, wdown = pack[:, :FF], pack[:, FF:].reshape(HALF, D)
-        return [(wgu, wdown), (to_partner(wgu), to_partner(wdown))]
+    def mlp_weights(pack):
+        return pack[:, :FF], pack[:, FF:].reshape(HALF, D)
 
     projs, mlps = [whole_proj(first[:, :cut])], []
 
@@ -429,70 +421,56 @@
         o_t, lse = attention(scalars, q_t, kv_own, kv_other)
         if layer == 0:
             o_t, pack0, late = lax.optimization_barrier((o_t, pack0, late))
-            mlps.append(mlp_halves(pack0))
+            mlps.append(mlp_weights(pack0))
             projs.append(whole_proj(late))
         else:
             o_t, pack1 = lax.optimization_barrier((o_t, pack1))
-            mlps.append(mlp_halves(pack1))
+            mlps.append(mlp_weights(pack1))
         attn_out = o_t.astype(BF16).reshape(Q_ROWS, ROWS)
         mid = hidden + ein("at,ad->td", attn_out, wout)
         unit_m, rms_m = normed(mid)
         mlp_in = (unit_m * gains[layer, 1]).astype(BF16)
-        hidden = mid
-        halves = []
-        for wgu, wdown in mlps[layer]:
-            gate_up = mm(mlp_in, wgu)
-            inner = (jax.nn.silu(gate_up[:, :HALF]) * gate_up[:, HALF:]).astype(BF16)
-            hidden = hidden + mm(inner, wdown)
-            halves.append((wgu, wdown, gate_up, inner))
+        wgu, wdown = mlps[layer]
+        both_in = jnp.concatenate([mlp_in, to_partner(mlp_in)], 0)
+        gate_up = mm(both_in, wgu)
+        inner = (jax.nn.silu(gate_up[:, :HALF]) * gate_up[:, HALF:]).astype(BF16)
+        part = mm(inner, wdown)
+        hidden = mid + part[:ROWS] + to_partner(part[ROWS:].astype(BF16)).astype(F32)
         saved.append(
             (wqkv, wout, unit_a, rms_a, attn_in, q_t, kv_own, kv_other, o_t, lse, attn_out,
-             unit_m, rms_m, mlp_in, halves)
+             unit_m, rms_m, both_in, gate_up, inner, wgu, wdown)
         )
     output = hidden.astype(BF16).reshape(1, ROWS, D)
 
     d_hidden = cotangent[0].astype(F32)
-    gain_grads = [None] * LAYERS
+    gain_grads, qkv_grads = [None] * LAYERS, [None] * LAYERS
     for layer in reversed(range(LAYERS)):
         (wqkv, wout, unit_a, rms_a, attn_in, q_t, kv_own, kv_other, o_t, lse, attn_out,
-         unit_m, rms_m, mlp_in, halves) = saved[layer]
+         unit_m, rms_m, both_in, gate_up, inner, wgu, wdown) = saved[layer]
         grad_b = d_hidden.astype(BF16)
-        d_norm = 0.0
-        wgu_parts, wd_parts = [], []
-        for wgu, wdown, gate_up, inner in halves:
-            d_inner = ein("td,fd->tf", grad_b, wdown)
-            gate, up = gate_up[:, :HALF], gate_up[:, HALF:]
-            sig = jax.nn.sigmoid(gate)
-            d_gate = d_inner * up * sig * (1.0 + gate * (1.0 - sig))
-            d_up = d_inner * (gate * sig)
-            d_gu = jnp.concatenate([d_gate, d_up], 1).astype(BF16)
-            d_norm = d_norm + ein("tf,df->td", d_gu, wgu)
-            wd_parts.append(ein("tf,td->fd", inner, grad_b).astype(BF16))
-            wgu_parts.append(ein("td,tf->df", mlp_in, d_gu).astype(BF16))
+        both_grad = jnp.concatenate([grad_b, to_partner(grad_b)], 0)
+        d_inner = ein("td,fd->tf", both_grad, wdown)
+        gate, up = gate_up[:, :HALF], gate_up[:, HALF:]
+        sig = jax.nn.sigmoid(gate)
+        d_gate = d_inner * up * sig * (1.0 + gate * (1.0 - sig))
+        d_up = d_inner * (gate * sig)
+        d_gu = jnp.concatenate([d_gate, d_up], 1).astype(BF16)
+        part = ein("tf,df->td", d_gu, wgu)
+        d_norm = part[:ROWS] + to_partner(part[ROWS:].astype(BF16)).astype(F32)
+        d_wdown = ein("tf,td->fd", inner, both_grad).astype(BF16)
+        d_wgu = ein("td,tf->df", both_in, d_gu).astype(BF16)
         d_gain_m = jnp.sum(d_norm * unit_m, 0)
         d_hidden = d_hidden + norm_back(d_norm * gains[layer, 1], unit_m, rms_m)
         grad_b = d_hidden.astype(BF16)
         d_wout = mm(attn_out, grad_b)
         do_t = ein("ad,td->at", wout, grad_b).astype(BF16).reshape(HEADS, HEAD_DIM, ROWS)
-        if layer == 0:
-            do_t, wgu_parts, wd_parts, late = lax.optimization_barrier(
-                (do_t, wgu_parts, wd_parts, late)
-            )
-            late = scatter_fsdp(late)
         wout_half = D // 2
         d_wout = d_wout.astype(BF16)
         wout_mine = my_half(d_wout[:, :wout_half], d_wout[:, wout_half:])
         wout_theirs = my_half(d_wout[:, wout_half:], d_wout[:, :wout_half])
-        d_mlp = [
-            sum_pair(wgu_parts[0], to_partner(wgu_parts[1])),
-            sum_pair(wd_parts[0], to_partner(wd_parts[1])).reshape(D, HALF),
-            sum_pair(wout_mine, to_partner(wout_theirs)),
-        ]
-        if layer == 1:
-            do_t, d_mlp = lax.optimization_barrier((do_t, d_mlp))
-        share = lax.psum_scatter(
-            jnp.concatenate(d_mlp, 1), "fsdp", scatter_dimension=0, tiled=True
-        )
+        d_mlp = [d_wgu, d_wdown.reshape(D, HALF), sum_pair(wout_mine, to_partner(wout_theirs))]
+        do_t, d_mlp = lax.optimization_barrier((do_t, jnp.concatenate(d_mlp, 1)))
+        share = lax.psum_scatter(d_mlp, "fsdp", scatter_dimension=0, tiled=True)
         if layer == 1:
             share1 = share
         else:
@@ -500,9 +478,7 @@
         dq_t, dkv_own, dkv_other = attention_back(scalars, q_t, kv_own, kv_other, o_t, do_t, lse)
         dkv = (dkv_own.astype(F32) + to_partner(dkv_other).astype(F32)).astype(BF16)
         if layer == 0:
-            dkv, late = lax.optimization_barrier((dkv, late))
-            share1 = lax.optimization_barrier((share1, late, dkv))[0]
-            share1 = sum_chips(jnp.concatenate([share1, late], 1))
+            share1 = sum_chips(lax.optimization_barrier((share1, dkv))[0])
         dkv = jnp.sum(over_chips(dkv).astype(F32), 0)
         turned = jnp.concatenate([dq_t, dkv[0]], 0)
         d_qkv = jnp.concatenate([rotate(turned, cosine, -sine), dkv[1]], 0)
@@ -512,28 +488,25 @@
         d_gain_a = jnp.sum(d_norm * unit_a, 0)
         d_hidden = d_hidden + norm_back(d_norm * gains[layer, 0], unit_a, rms_a)
         gain_grads[layer] = jnp.stack([d_gain_a, d_gain_m])
-        d_wqkv = d_wqkv.astype(BF16)
-        half = (Q_ROWS + KV_ROWS) // 2
-        mine = my_half(d_wqkv[:, :half], d_wqkv[:, half:])
-        theirs = my_half(d_wqkv[:, half:], d_wqkv[:, :half])
-        d_wqkv = sum_pair(mine, to_partner(theirs))
-        if layer == 0:
-            d_gains = jnp.transpose(jnp.stack(gain_grads).reshape(2 * LAYERS, D)).astype(BF16)
-            share_qkv = sum_chips(scatter_fsdp(jnp.concatenate([d_wqkv, d_gains], 1)))
-        else:
-            late = d_wqkv
+        qkv_grads[layer] = d_wqkv.astype(BF16)
     input_grad = d_hidden.reshape(1, ROWS, D)
 
+    mine, theirs = in_order(*qkv_grads)
+    d_gains = jnp.transpose(jnp.stack(gain_grads).reshape(2 * LAYERS, D)).astype(BF16)
+    d_wqkv = jnp.concatenate([sum_pair(mine, to_partner(theirs)), d_gains], 1)
+    qkv = sum_chips(scatter_fsdp(d_wqkv))
+    qkv_p = to_partner(qkv)
+
     share0 = sum_chips(share0)
-    mlp0, mlp0_p, qkv0, qkv0_p = share0, to_partner(share0), share_qkv, to_partner(share_qkv)
-    all1, all1_p = share1, to_partner(share1)
-    d_gain = qkv0[:, half:].astype(F32) + qkv0_p[:, half:].astype(F32)
+    mlp0, mlp0_p, mlp1, mlp1_p = share0, to_partner(share0), share1, to_partner(share1)
+    half = Q_ROWS + KV_ROWS
+    d_gain = qkv[:, half:].astype(F32) + qkv_p[:, half:].astype(F32)
     gain_grad = jnp.transpose(d_gain).reshape(LAYERS, 2, SHARD)
     qkv_grad, out_proj_grad, gate_up_grad = unpack(
-        core.reshape(1), mlp0, mlp0_p, qkv0, qkv0_p, all1, all1_p
+        core.reshape(1), mlp0, mlp0_p, mlp1, mlp1_p, qkv, qkv_p
     )
     down_grad = []
-    for own, theirs in ((mlp0, mlp0_p), (all1, all1_p)):
+    for own, theirs in ((mlp0, mlp0_p), (mlp1, mlp1_p)):
         rows = [x[:, FF : FF + HALF].reshape(UNITS, D) for x in in_order(own, theirs)]
         down_grad.append(jnp.concatenate(rows, 0))
     down_grad = jnp.stack(down_grad).astype(F32)

time: 510 us -> 532 us (1.043)
  waiting for transfers between devices: 147 us -> 166 us
    all_to_all x3 -> x2, waiting for transfers between devices: 64.8 us -> 22.7 us  [over_chips(): lax.all_to_all(x, 'ctx', 0, 0, axis_index_groups=SAME_CORE, tiled=True)]
    optimization_barrier x1, waiting for transfers between devices: 0.02 us -> 29.6 us  [local(): share1 = sum_chips(lax.optimization_barrier((share1, dkv))[0])]
    all_to_all x1 -> x2, blocking collectives: 26.5 us -> 48.6 us  [over_chips(): lax.all_to_all(x, 'ctx', 0, 0, axis_index_groups=SAME_CORE, tiled=True)]
    ppermute x9, waiting for transfers between devices: 31 us -> 11 us  [sum_chips(): x = sum_pair(x, lax.ppermute(x, 'ctx', [(i, i ^ bit) for i in range(CTX)]))]
    all_to_all x1 -> x0, blocking collectives: 19.8 us -> none  [over_fsdp(): return lax.all_to_all(x, 'fsdp', 0, 0, tiled=True)]
    all_gather x1, waiting for transfers between devices: 0.01 us -> 18.5 us  [local(): pack1 = lax.all_gather(mlp_pack(1), 'fsdp', axis=0, tiled=True)]
    unnamed x5, waiting for transfers between devices: 28.2 us -> 44.9 us
    all_to_all x3, waiting for transfers between devices: 14.4 us -> 27.8 us  [over_fsdp(): return lax.all_to_all(x, 'fsdp', 0, 0, tiled=True)]
  transfers between devices with their start and end apart: 40 -> 38, of which waited for: 14 -> 16; matrix products, arithmetic and copies ran while one was open for 21% -> 19% of each run, Pallas kernels for 11% -> 10%
where the time goes in v2:
time: 532 us; the launch traced here: 525 us
  waiting for transfers between devices  166 us (31%)
  Pallas kernels  77.6 us (15%)
  starting transfers between devices  65.8 us (12%)
  local copies, waits for them, and re-layouts  63.5 us (12%)
  blocking collectives  48.6 us (9%)
  matrix products  42.5 us (8%)
  other arithmetic  42.3 us (8%)
  between operations  18.2 us (3%)
    all_to_all x2, blocking collectives, over_chips(): lax.all_to_all(x, 'ctx', 0, 0, axis_index_groups=SAME_CORE, tiled=True)  48.6 us
    unnamed x5, waiting for transfers between devices  44.9 us
    pallas_call x2, Pallas kernels, attention_back(): pl.pallas_call(backward_kernel, grid_spec=pltpu.PrefetchScalarGridSpec(nu...  44.6 us
    dot_general x18, matrix products, ein(): return jnp.einsum(spec, a, b, preferred_element_type=F32)  34.1 us
    pallas_call x2, Pallas kernels, attention(): pl.pallas_call(forward_kernel, grid_spec=pltpu.PrefetchScalarGridSpec(num...  30.9 us
    optimization_barrier x1, waiting for transfers between devices, local(): share1 = sum_chips(lax.optimization_barrier((share1, dkv))[0])  29.6 us
    ppermute x20, starting transfers between devices, to_partner(): return lax.ppermute(x, 'ctx', PARTNER)  27.9 us
    all_to_all x3, waiting for transfers between devices, over_fsdp(): return lax.all_to_all(x, 'fsdp', 0, 0, tiled=True)  27.8 us
  transfers between devices with their start and end apart: 38, of which 16 were waited for; matrix products, arithmetic and copies ran while one was open for 19% of the time, Pallas kernels for 10%

profile of v2, /device:TPU:1, one launch (start us, length us, event | category | flops | bytes accessed | tf_op | source)
XLA Modules:
  0.0 524.6 jit_solution(3823052754111185858)
XLA Ops:
  11.7 8.2 %all-to-all-start = ((bf16[8,72,772]{2,1,0:T(8,128)(2,1)}), bf16[8,72,772]{2,1,0:T(8,128)(2,1)S(1)}, u32[]{:S(2)}, u32[]{:S(2)}) async-start(bf16[8,72,772]{2,1,0:T(8,128)(2,1)} %broadcast_in_dim.16), calls=%async_computation | async-start | bytes 2064384 | tf_op jit(solution)/shard_map/all_to_all | solution.py:45
  28.9 8.2 %all-to-all-done = bf16[8,72,772]{2,1,0:T(8,128)(2,1)S(1)} async-done(((bf16[8,72,772]{2,1,0:T(8,128)(2,1)}), bf16[8,72,772]{2,1,0:T(8,128)(2,1)S(1)}, u32[]{:S(2)}, u32[]{:S(2)}) %all-to-all-start) | async-done | bytes 889376 | tf_op jit(solution)/shard_map/all_to_all | solution.py:45
  45.0 4.8 all-to-all-start.1
  50.6 22.7 %all-to-all-done.1.own_ref = bf16[8,2,3,64,256]{4,3,2,1,0:T(8,128)(2,1)S(1)} async-done(((bf16[8,2,3,64,256]{4,3,2,1,0:T(8,128)(2,1)}), bf16[8,2,3,64,256]{4,3,2,1,0:T(8,128)(2,1)S(1)}, u32[]{:S(2)}, u32[]{:S(2)}) %all-to-all-start.1) | async-done | bytes 1572896 | tf_op jit(solution)/shard_map/all_to_all | solution.py:41
  76.6 4.2 all-to-all-start.2
  88.8 15.5 %attention.2 = (f32[9,64,256]{2,1,0:T(8,128)S(1)}, f32[3,2,1,384]{3,2,1,0:T(1,128)S(1)}) custom-call(s32[39]{0:T(128)S(1)} %concatenate.93.sc, bf16[9,64,256]{2,1,0:T(8,128)(2,1)S(1)} %fusion.35.q_ref, bf16[8,2,3,64,256]{4,3,2,1,0:T(8,128)(2,1)S(1)} %all-to-all-done.1.own_ref, bf16[8,2,3,64,256]{4,3,2,1,0:T(8,128)(2,1)S(1)} %copy-done.11), custom_call_target="tpu_custom_call" | custom-call | flops 5435817984 | bytes 50000000 | tf_op jit(solution)/shard_map/attention/pallas_call | solution.py:225
  105.1 2.4 multiply_reduce_fusion.8
  110.3 2.1 slice.285
  112.4 2.7 reshape.312
  115.7 3.1 fusion.8
  129.2 24.3 %all_to_all.35.own_ref = bf16[8,2,3,64,256]{4,3,2,1,0:T(8,128)(2,1)S(1)} all-to-all(bf16[8,2,3,64,256]{4,3,2,1,0:T(8,128)(2,1)S(1)} %broadcast_in_dim.21), channel_id=1, replica_groups={{0,16,32,48,64,80,96,112},{8,24,40,56,72,88,104,120},{1,17,33,49,65,81,..., dimensions={0} | all-to-all | bytes 3145728 | tf_op jit(solution)/shard_map/all_to_all | solution.py:41
  155.4 3.0 collective-permute-done.5.other_ref
  158.3 15.5 %attention.3 = (f32[9,64,256]{2,1,0:T(8,128)S(1)}, f32[3,2,1,384]{3,2,1,0:T(1,128)S(1)}) custom-call(s32[39]{0:T(128)S(1)} %concatenate.93.sc, bf16[9,64,256]{2,1,0:T(8,128)(2,1)S(1)} %fusion.32.q_ref, bf16[8,2,3,64,256]{4,3,2,1,0:T(8,128)(2,1)S(1)} %all_to_all.35.own_ref, bf16[8,2,3,64,256]{4,3,2,1,0:T(8,128)(2,1)S(1)} %collective-permute-done.5.other_ref), custom_call_target="tpu_custom_call" | custom-call | flops 5435817984 | bytes 50000000 | tf_op jit(solution)/shard_map/attention/pallas_call | solution.py:225
  176.6 18.5 %all-gather.5.cloned.1.call-done = bf16[576,2304]{1,0:T(8,128)(2,1)} async-done(((bf16[72,2304]{1,0:T(8,128)(2,1)}), bf16[576,2304]{1,0:T(8,128)(2,1)}) %all-gather.5.cloned.1.call-update) | async-done | bytes 2654224 | tf_op jit(solution)/shard_map/all_gather | solution.py:381
  196.2 2.3 multiply_reduce_fusion.6
  201.9 2.1 slice.308
  204.0 3.4 reshape.314
  207.4 3.1 fusion.4
  210.6 2.6 multiply_convert_fusion.3
  215.7 2.7 convolution_convert_fusion.5
  225.0 3.3 convolution_convert_fusion.1
  228.3 2.2 copy.65
  230.5 3.2 reshape.317
  242.3 22.0 %attention_back.2 = (f32[9,64,256]{2,1,0:T(8,128)S(1)}, bf16[8,2,3,64,256]{4,3,2,1,0:T(8,128)(2,1)S(1)}, bf16[8,2,3,64,256]{4,3,2,1,0:T(8,128)(2,1)S(1)}) custom-call(s32[39]{0:T(128)S(1)} %concatenate.93.sc, bf16[9,64,256]{2,1,0:T(8,128)(2,1)S(1)} %copy-done.9, bf16[8,2,3,64,256]{4,3,2,1,0:T(8,128)(2,1)S(1)} %all_to_all.35.own_ref, ...), custom_call_target="tpu_custom_call" | custom-call | flops 13589544960 | bytes 75000000 | tf_op jit(solution)/shard_map/attention_back/pallas_call | solution.py:251
  264.4 3.4 collective-permute-done.11
  268.4 24.3 %all_to_all.36 = bf16[8,2,3,64,256]{4,3,2,1,0:T(8,128)(2,1)S(1)} all-to-all(bf16[8,2,3,64,256]{4,3,2,1,0:T(8,128)(2,1)S(1)} %add_convert_fusion.1), channel_id=1, replica_groups={{0,16,32,48,64,80,96,112},{8,24,40,56,72,88,104,120},{1,17,33,49,65,81,..., dimensions={0} | all-to-all | bytes 3145728 | tf_op jit(solution)/shard_map/all_to_all | solution.py:41
  299.6 3.1 multiply_convert_fusion.1
  304.6 2.6 convolution_convert_fusion.4
  310.5 3.4 convolution_convert_fusion
  313.9 2.2 copy.67
  316.1 3.2 reshape.319
  327.7 22.7 %attention_back.3 = (f32[9,64,256]{2,1,0:T(8,128)S(1)}, bf16[8,2,3,64,256]{4,3,2,1,0:T(8,128)(2,1)S(1)}, bf16[8,2,3,64,256]{4,3,2,1,0:T(8,128)(2,1)}) custom-call(s32[39]{0:T(128)S(1)} %concatenate.93.sc, bf16[9,64,256]{2,1,0:T(8,128)(2,1)S(1)} %copy-done.7, bf16[8,2,3,64,256]{4,3,2,1,0:T(8,128)(2,1)S(1)} %all-to-all-done.1.own_ref, ...), custom_call_target="tpu_custom_call" | custom-call | flops 13589544960 | bytes 75000000 | tf_op jit(solution)/shard_map/attention_back/pallas_call | solution.py:251
  351.6 3.2 collective-permute-done.15
  356.6 3.7 all-to-all-start.5
  360.4 29.6 %reduce-scatter.9.cloned.1.call-done = bf16[72,2592]{1,0:T(8,128)(2,1)} async-done(((bf16[576,2592]{1,0:T(8,128)(2,1)}), bf16[72,2592]{1,0:T(8,128)(2,1)}) %reduce-scatter.9.cloned.1.call-update) | async-done | bytes 373264 | tf_op jit(solution)/shard_map/optimization_barrier | solution.py:481
  393.4 2.9 collective-permute-start.16
  396.3 2.1 collective-permute-done.25
  399.5 2.2 collective-permute-start.26
  406.4 3.6 all-to-all-start.6
  411.1 2.2 collective-permute-start.27
  413.3 19.6 %all-to-all-done.6 = bf16[8,72,964]{2,1,0:T(8,128)(2,1)S(1)} async-done(((bf16[8,72,964]{2,1,0:T(8,128)(2,1)}), bf16[8,72,964]{2,1,0:T(8,128)(2,1)S(1)}, u32[]{:S(2)}, u32[]{:S(2)}) %all-to-all-start.6) | async-done | bytes 1110560 | tf_op jit(solution)/shard_map/all_to_all | solution.py:45
  433.5 44.8 %reduce-scatter.7.cloned.1.call-done = bf16[72,2592]{1,0:T(8,128)(2,1)} async-done(((bf16[576,2592]{1,0:T(8,128)(2,1)}), bf16[72,2592]{1,0:T(8,128)(2,1)}) %reduce-scatter.7.cloned.1.call-update) | async-done | bytes 373264
  480.0 6.5 %collective-permute-done.21 = bf16[72,2592]{1,0:T(8,128)(2,1)S(1)} collective-permute-done((bf16[72,2592]{1,0:T(8,128)(2,1)}, bf16[72,2592]{1,0:T(8,128)(2,1)S(1)}, u32[]{:S(2)}, u32[]{:S(2)}) %collective-permute-start.21) | collective-permute-done | bytes 373280 | tf_op jit(solution)/shard_map/ppermute | solution.py:63
  489.8 2.5 collective-permute-start.19
  492.3 2.4 collective-permute-done.22
  494.8 2.6 collective-permute-start.23
  498.5 8.4 %collective-permute-start.28 = (bf16[72,2592]{1,0:T(8,128)(2,1)S(1)}, bf16[72,2592]{1,0:T(8,128)(2,1)S(1)}, u32[]{:S(2)}, u32[]{:S(2)}) collective-permute-start(bf16[72,2592]{1,0:T(8,128)(2,1)S(1)} %add_convert_fusion.5.refs_2_), channel_id=1, source_target_pairs={{0,8},{8,0},{16,24},{24,16},{32,40},{40,32},{48,56},{56,48},{64,72... | collective-permute-start | bytes 1119752 | tf_op jit(solution)/shard_map/ppermute | solution.py:37
  508.5 4.2 collective-permute-start.24
  (359 shorter events, 119.0 us)
Async XLA Ops:
  11.7 25.3 %all-to-all-start = ((bf16[8,72,772]{2,1,0:T(8,128)(2,1)}), bf16[8,72,772]{2,1,0:T(8,128)(2,1)S(1)}, u32[]{:S(2)}, u32[]{:S(2)}) async-start(bf16[8,72,772]{2,1,0:T(8,128)(2,1)} %broadcast_in_dim.16), calls=%async_computation | async-start | bytes 2064384 | tf_op jit(solution)/shard_map/all_to_all | solution.py:45
  19.9 85.1 %all-gather.3.cloned.1.call-start = ((), (), s32[]{:S(2)}) async-start(), calls=%async_computation.9 | async-start | bytes 2985984 | tf_op jit(solution)/shard_map/all_gather | solution.py:380
  37.1 3.1 collective-permute-start
  45.0 28.3 %all-to-all-start.1 = ((bf16[8,2,3,64,256]{4,3,2,1,0:T(8,128)(2,1)}), bf16[8,2,3,64,256]{4,3,2,1,0:T(8,128)(2,1)S(1)}, u32[]{:S(2)}, u32[]{:S(2)}) async-start(bf16[8,2,3,64,256]{4,3,2,1,0:T(8,128)(2,1)} %broadcast_in_dim.19), calls=%async_computation.1 | async-start | bytes 3145728 | tf_op jit(solution)/shard_map/all_to_all | solution.py:41
  73.3 12.9 %collective-permute-start.1 = (bf16[8,2,3,64,256]{4,3,2,1,0:T(8,128)(2,1)S(1)}, bf16[8,2,3,64,256]{4,3,2,1,0:T(8,128)(2,1)S(1)}, u32[]{:S(2)}, u32[]{:S(2)}) collective-permute-start(bf16[8,2,3,64,256]{4,3,2,1,0:T(8,128)(2,1)S(1)} %all-to-all-done.1.own_ref), channel_id=1, source_target_pairs={{0,8},{8,0},{16,24},{24,16},{32,40},{40,32},{48,56},{56,48},{64,72... | collective-permute-start | bytes 4718600 | tf_op jit(solution)/shard_map/ppermute | solution.py:37
  76.6 28.4 %all-to-all-start.2 = ((bf16[8,72,768]{2,1,0:T(8,128)(2,1)}), bf16[8,72,768]{2,1,0:T(8,128)(2,1)}, u32[]{:S(2)}, u32[]{:S(2)}) async-start(bf16[8,72,768]{2,1,0:T(8,128)(2,1)} %broadcast_in_dim.20), calls=%async_computation.2 | async-start | bytes 1769472 | tf_op jit(solution)/shard_map/all_to_all | solution.py:45
  80.8 114.3 %all-gather.5.cloned.1.call-start = ((), (), s32[]{:S(2)}) async-start(), calls=%async_computation.10 | async-start | bytes 2985984 | tf_op jit(solution)/shard_map/all_gather | solution.py:381
  88.8 16.2 %copy-start.43 = (bf16[1,256,576]{1,2,0:T(8,128)(2,1)S(1)}, bf16[1,256,576]{1,2,0:T(8,128)(2,1)}, u32[]{:S(2)}) copy-start(bf16[1,256,576]{1,2,0:T(8,128)(2,1)} %param.9) | copy-start | bytes 884740
  107.5 16.4 %copy-start.20 = (f32[256,576]{0,1:T(8,128)}, f32[256,576]{0,1:T(8,128)S(1)}, u32[]{:S(2)}) copy-start(f32[256,576]{0,1:T(8,128)S(1)} %get-tuple-element.125) | copy-start | bytes 1769476
  108.4 7.2 %collective-permute-start.2 = (bf16[256,576]{0,1:T(8,128)(2,1)}, bf16[256,576]{0,1:T(8,128)(2,1)}, u32[]{:S(2)}, u32[]{:S(2)}) collective-permute-start(bf16[256,576]{0,1:T(8,128)(2,1)} %multiply_convert_fusion.8), channel_id=1, source_target_pairs={{0,8},{8,0},{16,24},{24,16},{32,40},{40,32},{48,56},{56,48},{64,72... | collective-permute-start | bytes 884744 | tf_op jit(solution)/shard_map/ppermute | solution.py:37
  115.1 10.0 %collective-permute-start.4 = (bf16[576,768]{1,0:T(8,128)(2,1)}, bf16[576,768]{1,0:T(8,128)(2,1)}, u32[]{:S(2)}, u32[]{:S(2)}) collective-permute-start(bf16[576,768]{1,0:T(8,128)(2,1)} %bitcast.17), channel_id=1, source_target_pairs={{0,8},{8,0},{16,24},{24,16},{32,40},{40,32},{48,56},{56,48},{64,72... | collective-permute-start | bytes 2654216 | tf_op jit(solution)/shard_map/ppermute | solution.py:37
  122.2 1.7 collective-permute-start.3
  123.3 266.7 %reduce-scatter.9.cloned.1.call-start = ((), (), s32[]{:S(2)}) async-start(), calls=%async_computation.12 | async-start | bytes 3483648
  125.1 168.6 %copy-start.76 = (f32[256]{0:T(256)}, f32[256]{0:T(256)S(1)}, u32[]{:S(2)}) copy-start(f32[256]{0:T(256)S(1)} %add_rsqrt_fusion.1) | copy-start | bytes 3076
  153.5 4.9 collective-permute-start.5
  200.1 7.3 %collective-permute-start.6 = (bf16[256,576]{0,1:T(8,128)(2,1)}, bf16[256,576]{0,1:T(8,128)(2,1)}, u32[]{:S(2)}, u32[]{:S(2)}) collective-permute-start(bf16[256,576]{0,1:T(8,128)(2,1)} %multiply_convert_fusion.6), channel_id=1, source_target_pairs={{0,8},{8,0},{16,24},{24,16},{32,40},{40,32},{48,56},{56,48},{64,72... | collective-permute-start | bytes 884744 | tf_op jit(solution)/shard_map/ppermute | solution.py:37
  201.4 9.2 %collective-permute-start.8 = (bf16[256,576]{0,1:T(8,128)(2,1)}, bf16[256,576]{0,1:T(8,128)(2,1)}, u32[]{:S(2)}, u32[]{:S(2)}) collective-permute-start(bf16[256,576]{0,1:T(8,128)(2,1)} %bitcast.24), channel_id=1, source_target_pairs={{0,8},{8,0},{16,24},{24,16},{32,40},{40,32},{48,56},{56,48},{64,72... | collective-permute-start | bytes 884744 | tf_op jit(solution)/shard_map/ppermute | solution.py:37
  214.3 4.1 collective-permute-start.9
  215.6 3.7 collective-permute-start.7
  224.4 11.3 %collective-permute-start.10 = (bf16[576,288]{1,0:T(8,128)(2,1)}, bf16[576,288]{1,0:T(8,128)(2,1)}, u32[]{:S(2)}, u32[]{:S(2)}) collective-permute-start(bf16[576,288]{1,0:T(8,128)(2,1)} %broadcast_select_fusion.6), channel_id=1, source_target_pairs={{0,8},{8,0},{16,24},{24,16},{32,40},{40,32},{48,56},{56,48},{64,72... | collective-permute-start | bytes 995336 | tf_op jit(solution)/shard_map/ppermute | solution.py:37
  264.2 3.5 collective-permute-start.11
  296.6 3.0 collective-permute-start.12
  298.2 180.1 %reduce-scatter.7.cloned.1.call-start = ((), (), s32[]{:S(2)}) async-start(), calls=%async_computation.11 | async-start | bytes 3483648
  303.9 3.3 collective-permute-start.13
  309.1 10.3 %copy-start.18 = (f32[256,576]{0,1:T(8,128)}, f32[256,576]{0,1:T(8,128)S(1)}, u32[]{:S(2)}) copy-start(f32[256,576]{0,1:T(8,128)S(1)} %multiply_add_fusion) | copy-start | bytes 1769476
  310.4 10.7 %collective-permute-start.14 = (bf16[576,288]{1,0:T(8,128)(2,1)}, bf16[576,288]{1,0:T(8,128)(2,1)}, u32[]{:S(2)}, u32[]{:S(2)}) collective-permute-start(bf16[576,288]{1,0:T(8,128)(2,1)} %broadcast_select_fusion.5), channel_id=1, source_target_pairs={{0,8},{8,0},{16,24},{24,16},{32,40},{40,32},{48,56},{56,48},{64,72... | collective-permute-start | bytes 995336 | tf_op jit(solution)/shard_map/ppermute | solution.py:37
  351.2 3.7 collective-permute-start.15
  356.6 33.4 %all-to-all-start.5 = ((bf16[8,2,3,64,256]{4,3,2,1,0:T(8,128)(2,1)}), bf16[8,2,3,64,256]{4,3,2,1,0:T(8,128)(2,1)S(1)}, u32[]{:S(2)}, u32[]{:S(2)}) async-start(bf16[8,2,3,64,256]{4,3,2,1,0:T(8,128)(2,1)} %add_convert_fusion), calls=%async_computation.5 | async-start | bytes 3145728 | tf_op jit(solution)/shard_map/all_to_all | solution.py:41
  360.3 30.0 %copy-start.5 = (f32[9,64,256]{2,1,0:T(8,128)S(1)}, f32[9,64,256]{2,1,0:T(8,128)}, u32[]{:S(2)}) copy-start(f32[9,64,256]{2,1,0:T(8,128)} %copy-done.4) | copy-start | bytes 1769476
  360.3 30.0 %copy-start.66 = (f32[32,256]{1,0:T(8,128)S(1)}, f32[32,256]{1,0:T(8,128)}, u32[]{:S(2)}) copy-start(f32[32,256]{1,0:T(8,128)} %get-tuple-element.121) | copy-start | bytes 98308
  390.0 8.3 %collective-permute-start.25 = (bf16[72,2592]{1,0:T(8,128)(2,1)}, bf16[72,2592]{1,0:T(8,128)(2,1)}, u32[]{:S(2)}, u32[]{:S(2)}) collective-permute-start(bf16[72,2592]{1,0:T(8,128)(2,1)} %reduce-scatter.9.cloned.1.call-done), channel_id=1, source_target_pairs={{0,16},{8,24},{16,0},{24,8},{32,48},{40,56},{48,32},{56,40},{64,80... | collective-permute-start | bytes 1119752 | tf_op jit(solution)/shard_map/ppermute | solution.py:63
  391.8 9.8 %copy-start.41 = (bf16[576,768]{1,0:T(8,128)(2,1)S(1)}, bf16[576,768]{1,0:T(8,128)(2,1)}, u32[]{:S(2)}) copy-start(bf16[576,768]{1,0:T(8,128)(2,1)} %copy-done.40) | copy-start | bytes 2654212
  391.8 9.8 %copy-start.54 = (bf16[576,768]{1,0:T(8,128)(2,1)S(1)}, bf16[576,768]{1,0:T(8,128)(2,1)}, u32[]{:S(2)}) copy-start(bf16[576,768]{1,0:T(8,128)(2,1)} %copy-done.53) | copy-start | bytes 2654212
  393.4 9.8 %collective-permute-start.16 = (bf16[576,960]{1,0:T(8,128)(2,1)}, bf16[576,960]{1,0:T(8,128)(2,1)}, u32[]{:S(2)}, u32[]{:S(2)}) collective-permute-start(bf16[576,960]{1,0:T(8,128)(2,1)} %get-tuple-element.130), channel_id=1, source_target_pairs={{0,8},{8,0},{16,24},{24,16},{32,40},{40,32},{48,56},{56,48},{64,72... | collective-permute-start | bytes 3317768 | tf_op jit(solution)/shard_map/ppermute | solution.py:37
  399.5 10.5 %collective-permute-start.26 = (bf16[72,2592]{1,0:T(8,128)(2,1)S(1)}, bf16[72,2592]{1,0:T(8,128)(2,1)}, u32[]{:S(2)}, u32[]{:S(2)}) collective-permute-start(bf16[72,2592]{1,0:T(8,128)(2,1)S(1)} %add_convert_fusion.7), channel_id=1, source_target_pairs={{0,32},{8,40},{16,48},{24,56},{32,0},{40,8},{48,16},{56,24},{64,96... | collective-permute-start | bytes 1119752 | tf_op jit(solution)/shard_map/ppermute | solution.py:63
  406.4 26.5 %all-to-all-start.6 = ((bf16[8,72,964]{2,1,0:T(8,128)(2,1)}), bf16[8,72,964]{2,1,0:T(8,128)(2,1)S(1)}, u32[]{:S(2)}, u32[]{:S(2)}) async-start(bf16[8,72,964]{2,1,0:T(8,128)(2,1)} %bitcast.38), calls=%async_computation.6 | async-start | bytes 2359296 | tf_op jit(solution)/shard_map/all_to_all | solution.py:45
  411.1 77.7 %copy-start.19 = (f32[256,576]{0,1:T(8,128)S(1)}, f32[256,576]{0,1:T(8,128)}, u32[]{:S(2)}) copy-start(f32[256,576]{0,1:T(8,128)} %copy-done.18) | copy-start | bytes 1769476
  411.1 77.6 %copy-start.59 = (f32[256,576]{0,1:T(8,128)S(1)}, f32[256,576]{0,1:T(8,128)}, u32[]{:S(2)}) copy-start(f32[256,576]{0,1:T(8,128)} %get-tuple-element.129) | copy-start | bytes 1769476
  411.1 86.3 %collective-permute-start.27 = (bf16[72,2592]{1,0:T(8,128)(2,1)S(1)}, bf16[72,2592]{1,0:T(8,128)(2,1)}, u32[]{:S(2)}, u32[]{:S(2)}) collective-permute-start(bf16[72,2592]{1,0:T(8,128)(2,1)S(1)} %add_convert_fusion.6), channel_id=1, source_target_pairs={{0,64},{8,72},{16,80},{24,88},{32,96},{40,104},{48,112},{56,120},{... | collective-permute-start | bytes 1119752 | tf_op jit(solution)/shard_map/ppermute | solution.py:63
  433.1 45.5 %collective-permute-start.17 = (bf16[72,964]{1,0:T(8,128)(2,1)S(1)}, bf16[72,964]{1,0:T(8,128)(2,1)S(1)}, u32[]{:S(2)}, u32[]{:S(2)}) collective-permute-start(bf16[72,964]{1,0:T(8,128)(2,1)S(1)} %reduce_sum.162), channel_id=1, source_target_pairs={{0,16},{8,24},{16,0},{24,8},{32,48},{40,56},{48,32},{56,40},{64,80... | collective-permute-start | bytes 416456 | tf_op jit(solution)/shard_map/ppermute | solution.py:63
  478.3 8.2 %collective-permute-start.21 = (bf16[72,2592]{1,0:T(8,128)(2,1)}, bf16[72,2592]{1,0:T(8,128)(2,1)S(1)}, u32[]{:S(2)}, u32[]{:S(2)}) collective-permute-start(bf16[72,2592]{1,0:T(8,128)(2,1)} %reduce-scatter.7.cloned.1.call-done), channel_id=1, source_target_pairs={{0,16},{8,24},{16,0},{24,8},{32,48},{40,56},{48,32},{56,40},{64,80... | collective-permute-start | bytes 1119752 | tf_op jit(solution)/shard_map/ppermute | solution.py:63
  478.7 11.0 %collective-permute-start.18 = (bf16[72,964]{1,0:T(8,128)(2,1)S(1)}, bf16[72,964]{1,0:T(8,128)(2,1)S(1)}, u32[]{:S(2)}, u32[]{:S(2)}) collective-permute-start(bf16[72,964]{1,0:T(8,128)(2,1)S(1)} %add_convert_fusion.14), channel_id=1, source_target_pairs={{0,32},{8,40},{16,48},{24,56},{32,0},{40,8},{48,16},{56,24},{64,96... | collective-permute-start | bytes 416456 | tf_op jit(solution)/shard_map/ppermute | solution.py:63
  487.6 7.1 %collective-permute-start.22 = (bf16[72,2592]{1,0:T(8,128)(2,1)S(1)}, bf16[72,2592]{1,0:T(8,128)(2,1)S(1)}, u32[]{:S(2)}, u32[]{:S(2)}) collective-permute-start(bf16[72,2592]{1,0:T(8,128)(2,1)S(1)} %add_convert_fusion.10), channel_id=1, source_target_pairs={{0,32},{8,40},{16,48},{24,56},{32,0},{40,8},{48,16},{56,24},{64,96... | collective-permute-start | bytes 1119752 | tf_op jit(solution)/shard_map/ppermute | solution.py:63
  489.8 17.1 %collective-permute-start.19 = (bf16[72,964]{1,0:T(8,128)(2,1)S(1)}, bf16[72,964]{1,0:T(8,128)(2,1)S(1)}, u32[]{:S(2)}, u32[]{:S(2)}) collective-permute-start(bf16[72,964]{1,0:T(8,128)(2,1)S(1)} %add_convert_fusion.13), channel_id=1, source_target_pairs={{0,64},{8,72},{16,80},{24,88},{32,96},{40,104},{48,112},{56,120},{... | collective-permute-start | bytes 416456 | tf_op jit(solution)/shard_map/ppermute | solution.py:63
  494.8 13.6 %collective-permute-start.23 = (bf16[72,2592]{1,0:T(8,128)(2,1)S(1)}, bf16[72,2592]{1,0:T(8,128)(2,1)S(1)}, u32[]{:S(2)}, u32[]{:S(2)}) collective-permute-start(bf16[72,2592]{1,0:T(8,128)(2,1)S(1)} %add_convert_fusion.9), channel_id=1, source_target_pairs={{0,64},{8,72},{16,80},{24,88},{32,96},{40,104},{48,112},{56,120},{... | collective-permute-start | bytes 1119752 | tf_op jit(solution)/shard_map/ppermute | solution.py:63
  498.5 14.2 %collective-permute-start.28 = (bf16[72,2592]{1,0:T(8,128)(2,1)S(1)}, bf16[72,2592]{1,0:T(8,128)(2,1)S(1)}, u32[]{:S(2)}, u32[]{:S(2)}) collective-permute-start(bf16[72,2592]{1,0:T(8,128)(2,1)S(1)} %add_convert_fusion.5.refs_2_), channel_id=1, source_target_pairs={{0,8},{8,0},{16,24},{24,16},{32,40},{40,32},{48,56},{56,48},{64,72... | collective-permute-start | bytes 1119752 | tf_op jit(solution)/shard_map/ppermute | solution.py:37
  507.0 6.3 %collective-permute-start.20 = (bf16[72,964]{1,0:T(8,128)(2,1)S(1)}, bf16[72,964]{1,0:T(8,128)(2,1)S(1)}, u32[]{:S(2)}, u32[]{:S(2)}) collective-permute-start(bf16[72,964]{1,0:T(8,128)(2,1)S(1)} %add_convert_fusion.12.refs_4_), channel_id=1, source_target_pairs={{0,8},{8,0},{16,24},{24,16},{32,40},{40,32},{48,56},{56,48},{64,72... | collective-permute-start | bytes 416456 | tf_op jit(solution)/shard_map/ppermute | solution.py:37
  508.5 5.6 %collective-permute-start.24 = (bf16[72,2592]{1,0:T(8,128)(2,1)S(1)}, bf16[72,2592]{1,0:T(8,128)(2,1)S(1)}, u32[]{:S(2)}, u32[]{:S(2)}) collective-permute-start(bf16[72,2592]{1,0:T(8,128)(2,1)S(1)} %add_convert_fusion.8.refs_0_), channel_id=1, source_target_pairs={{0,8},{8,0},{16,24},{24,16},{32,40},{40,32},{48,56},{56,48},{64,72... | collective-permute-start | bytes 1119752 | tf_op jit(solution)/shard_map/ppermute | solution.py:37
  (72 other events, 161.8 us)
Sparse Core Ops, SparseCore 0:
  27.0 71.9 all-gather.2
  123.4 71.6 all-gather.4
  298.4 91.6 reduce-scatter.8
  393.8 84.4 reduce-scatter.6

commit v3 on v2

--- a/solution.py
+++ b/solution.py
@@ -240,9 +240,6 @@
         ),
         out_shape=[HEAD_SHAPE, LSE_SHAPE],
         compiler_params=KERNEL_PARAMS,
-        cost_estimate=pl.CostEstimate(
-            flops=4 * 36 * BLK * HEADS * BLK * 256, transcendentals=36 * BLK * HEADS * BLK, bytes_accessed=50 * 10**6
-        ),
         name="attention",
     )(scalars, q_t, own, other)
 
@@ -267,9 +264,6 @@
         ),
         out_shape=[HEAD_SHAPE, KV_SHAPE, KV_SHAPE],
         compiler_params=KERNEL_PARAMS,
-        cost_estimate=pl.CostEstimate(
-            flops=10 * 36 * BLK * HEADS * BLK * 256, transcendentals=36 * BLK * HEADS * BLK, bytes_accessed=75 * 10**6
-        ),
         name="attention_back",
     )(scalars, q_t, own, other, o_t, do_t, lse)
 

time: 532 us -> 517 us (0.972)
  blocking collectives: 48.6 us -> 23.4 us
  waiting for transfers between devices: 166 us -> 174 us
  starting transfers between devices: 65.8 us -> 72.6 us
    all_to_all x2 -> x3, waiting for transfers between devices: 22.7 us -> 69 us  [over_chips(): lax.all_to_all(x, 'ctx', 0, 0, axis_index_groups=SAME_CORE, tiled=True)]
    optimization_barrier x1, waiting for transfers between devices: 29.6 us -> 0.02 us  [local(): share1 = sum_chips(lax.optimization_barrier((share1, dkv))[0])]
    all_to_all x2 -> x1, blocking collectives: 48.6 us -> 23.4 us  [over_chips(): lax.all_to_all(x, 'ctx', 0, 0, axis_index_groups=SAME_CORE, tiled=True)]
    unnamed x5, waiting for transfers between devices: 44.9 us -> 37.9 us
    all_to_all x2 -> x3, starting transfers between devices: 8.55 us -> 12.7 us  [over_chips(): lax.all_to_all(x, 'ctx', 0, 0, axis_index_groups=SAME_CORE, tiled=True)]
  transfers between devices with their start and end apart: 38 -> 39, of which waited for: 16 -> 17; matrix products, arithmetic and copies ran while one was open for 19% -> 19% of each run, Pallas kernels for 10% -> 11%
where the time goes in v3:
time: 517 us; the launch traced here: 510 us
  waiting for transfers between devices  174 us (34%)
  Pallas kernels  77.6 us (15%)
  starting transfers between devices  72.6 us (14%)
  local copies, waits for them, and re-layouts  61.2 us (12%)
  other arithmetic  42.4 us (8%)
  matrix products  41.1 us (8%)
  blocking collectives  23.4 us (5%)
  between operations  18.2 us (4%)
    all_to_all x3, waiting for transfers between devices, over_chips(): lax.all_to_all(x, 'ctx', 0, 0, axis_index_groups=SAME_CORE, tiled=True)  69 us
    pallas_call x2, Pallas kernels, attention_back(): pl.pallas_call(backward_kernel, grid_spec=pltpu.PrefetchScalarGridSpec(nu...  44.6 us
    unnamed x5, waiting for transfers between devices  37.9 us
    dot_general x18, matrix products, ein(): return jnp.einsum(spec, a, b, preferred_element_type=F32)  32.5 us
    pallas_call x2, Pallas kernels, attention(): pl.pallas_call(forward_kernel, grid_spec=pltpu.PrefetchScalarGridSpec(num...  30.9 us
    ppermute x20, starting transfers between devices, to_partner(): return lax.ppermute(x, 'ctx', PARTNER)  26.9 us
    unnamed x164, local copies, waits for them, and re-layouts  24.3 us
    all_to_all x1, blocking collectives, over_chips(): lax.all_to_all(x, 'ctx', 0, 0, axis_index_groups=SAME_CORE, tiled=True)  23.4 us
  transfers between devices with their start and end apart: 39, of which 17 were waited for; matrix products, arithmetic and copies ran while one was open for 19% of the time, Pallas kernels for 11%

profile of v3, /device:TPU:1, one launch (start us, length us, event | category | flops | bytes accessed | tf_op | source)
XLA Modules:
  0.0 510.1 jit_solution(14208982835131942936)
XLA Ops:
  11.1 8.2 %all-to-all-start = ((bf16[8,72,772]{2,1,0:T(8,128)(2,1)}), bf16[8,72,772]{2,1,0:T(8,128)(2,1)S(1)}, u32[]{:S(2)}, u32[]{:S(2)}) async-start(bf16[8,72,772]{2,1,0:T(8,128)(2,1)} %broadcast_in_dim.16), calls=%async_computation | async-start | bytes 2064384 | tf_op jit(solution)/shard_map/all_to_all | solution.py:45
  28.2 8.2 %all-to-all-done = bf16[8,72,772]{2,1,0:T(8,128)(2,1)S(1)} async-done(((bf16[8,72,772]{2,1,0:T(8,128)(2,1)}), bf16[8,72,772]{2,1,0:T(8,128)(2,1)S(1)}, u32[]{:S(2)}, u32[]{:S(2)}) %all-to-all-start) | async-done | bytes 889376 | tf_op jit(solution)/shard_map/all_to_all | solution.py:45
  44.5 4.7 all-to-all-start.1
  49.3 23.4 %all-to-all-done.1.own_ref = bf16[8,2,3,64,256]{4,3,2,1,0:T(8,128)(2,1)S(1)} async-done(((bf16[8,2,3,64,256]{4,3,2,1,0:T(8,128)(2,1)}), bf16[8,2,3,64,256]{4,3,2,1,0:T(8,128)(2,1)S(1)}, u32[]{:S(2)}, u32[]{:S(2)}) %all-to-all-start.1) | async-done | bytes 1572896 | tf_op jit(solution)/shard_map/all_to_all | solution.py:41
  75.0 4.2 all-to-all-start.2
  82.9 15.5 %attention.2 = (f32[9,64,256]{2,1,0:T(8,128)S(1)}, f32[3,2,1,384]{3,2,1,0:T(1,128)S(1)}) custom-call(s32[39]{0:T(128)S(1)} %concatenate.93.sc, bf16[9,64,256]{2,1,0:T(8,128)(2,1)S(1)} %fusion.35.q_ref, bf16[8,2,3,64,256]{4,3,2,1,0:T(8,128)(2,1)S(1)} %all-to-all-done.1.own_ref, bf16[8,2,3,64,256]{4,3,2,1,0:T(8,128)(2,1)S(1)} %collective-permute-done.1.other_ref), custom_call_target="tpu_custom_call" | custom-call | tf_op jit(solution)/shard_map/attention/pallas_call | solution.py:225
  101.0 2.2 multiply_reduce_fusion.8
  106.9 2.1 slice.285
  109.0 2.7 reshape.312
  111.8 3.3 fusion.8
  125.8 23.4 %all_to_all.35.own_ref = bf16[8,2,3,64,256]{4,3,2,1,0:T(8,128)(2,1)S(1)} all-to-all(bf16[8,2,3,64,256]{4,3,2,1,0:T(8,128)(2,1)S(1)} %broadcast_in_dim.21), channel_id=1, replica_groups={{0,16,32,48,64,80,96,112},{8,24,40,56,72,88,104,120},{1,17,33,49,65,81,..., dimensions={0} | all-to-all | bytes 3145728 | tf_op jit(solution)/shard_map/all_to_all | solution.py:41
  149.2 2.2 collective-permute-start.5
  151.5 3.0 collective-permute-done.5.other_ref
  154.5 15.5 %attention.3 = (f32[9,64,256]{2,1,0:T(8,128)S(1)}, f32[3,2,1,384]{3,2,1,0:T(1,128)S(1)}) custom-call(s32[39]{0:T(128)S(1)} %concatenate.93.sc, bf16[9,64,256]{2,1,0:T(8,128)(2,1)S(1)} %fusion.32.q_ref, bf16[8,2,3,64,256]{4,3,2,1,0:T(8,128)(2,1)S(1)} %all_to_all.35.own_ref, bf16[8,2,3,64,256]{4,3,2,1,0:T(8,128)(2,1)S(1)} %collective-permute-done.5.other_ref), custom_call_target="tpu_custom_call" | custom-call | tf_op jit(solution)/shard_map/attention/pallas_call | solution.py:225
  172.7 19.3 %all-gather.5.cloned.1.call-done = bf16[576,2304]{1,0:T(8,128)(2,1)} async-done(((bf16[72,2304]{1,0:T(8,128)(2,1)}), bf16[576,2304]{1,0:T(8,128)(2,1)}) %all-gather.5.cloned.1.call-update) | async-done | bytes 2654224 | tf_op jit(solution)/shard_map/all_gather | solution.py:375
  193.1 2.4 multiply_reduce_fusion.6
  198.9 2.1 slice.308
  201.1 3.4 reshape.314
  204.5 3.1 fusion.4
  207.7 2.6 multiply_convert_fusion.3
  212.8 2.6 convolution_convert_fusion.5
  222.0 3.3 convolution_convert_fusion.1
  225.4 2.2 copy.65
  227.6 3.2 reshape.317
  230.8 2.6 convolution_convert_fusion.9
  241.0 22.0 %attention_back.2 = (f32[9,64,256]{2,1,0:T(8,128)S(1)}, bf16[8,2,3,64,256]{4,3,2,1,0:T(8,128)(2,1)S(1)}, bf16[8,2,3,64,256]{4,3,2,1,0:T(8,128)(2,1)S(1)}) custom-call(s32[39]{0:T(128)S(1)} %concatenate.93.sc, bf16[9,64,256]{2,1,0:T(8,128)(2,1)S(1)} %copy-done.5, bf16[8,2,3,64,256]{4,3,2,1,0:T(8,128)(2,1)S(1)} %all_to_all.35.own_ref, ...), custom_call_target="tpu_custom_call" | custom-call | tf_op jit(solution)/shard_map/attention_back/pallas_call | solution.py:248
  263.9 3.3 collective-permute-done.11
  269.0 4.3 all-to-all-start.4
  274.1 23.2 %all-to-all-done.4 = bf16[8,2,3,64,256]{4,3,2,1,0:T(8,128)(2,1)} async-done(((bf16[8,2,3,64,256]{4,3,2,1,0:T(8,128)(2,1)}), bf16[8,2,3,64,256]{4,3,2,1,0:T(8,128)(2,1)}, u32[]{:S(2)}, u32[]{:S(2)}) %all-to-all-start.4) | async-done | bytes 1572896 | tf_op jit(solution)/shard_map/all_to_all | solution.py:41
  312.2 3.4 convolution_convert_fusion
  315.6 2.2 copy.67
  317.8 3.2 reshape.319
  321.0 2.5 convolution_convert_fusion.8
  329.1 22.7 %attention_back.3 = (f32[9,64,256]{2,1,0:T(8,128)S(1)}, bf16[8,2,3,64,256]{4,3,2,1,0:T(8,128)(2,1)S(1)}, bf16[8,2,3,64,256]{4,3,2,1,0:T(8,128)(2,1)}) custom-call(s32[39]{0:T(128)S(1)} %concatenate.93.sc, bf16[9,64,256]{2,1,0:T(8,128)(2,1)S(1)} %fusion.35.q_ref, bf16[8,2,3,64,256]{4,3,2,1,0:T(8,128)(2,1)S(1)} %all-to-all-done.1.own_ref, ...), custom_call_target="tpu_custom_call" | custom-call | tf_op jit(solution)/shard_map/attention_back/pallas_call | solution.py:248
  354.2 3.2 collective-permute-done.15
  359.2 3.7 all-to-all-start.5
  364.4 22.4 %all-to-all-done.5 = bf16[8,2,3,64,256]{4,3,2,1,0:T(8,128)(2,1)S(1)} async-done(((bf16[8,2,3,64,256]{4,3,2,1,0:T(8,128)(2,1)}), bf16[8,2,3,64,256]{4,3,2,1,0:T(8,128)(2,1)S(1)}, u32[]{:S(2)}, u32[]{:S(2)}) %all-to-all-start.5) | async-done | bytes 1572896 | tf_op jit(solution)/shard_map/all_to_all | solution.py:41
  391.3 3.0 collective-permute-done.25
  401.7 4.5 all-to-all-start.6
  407.4 3.2 collective-permute-start.27
  410.6 14.4 %all-to-all-done.6 = bf16[8,72,964]{2,1,0:T(8,128)(2,1)S(1)} async-done(((bf16[8,72,964]{2,1,0:T(8,128)(2,1)}), bf16[8,72,964]{2,1,0:T(8,128)(2,1)S(1)}, u32[]{:S(2)}, u32[]{:S(2)}) %all-to-all-start.6) | async-done | bytes 1110560 | tf_op jit(solution)/shard_map/all_to_all | solution.py:45
  426.5 37.2 %reduce-scatter.7.cloned.1.call-done = bf16[72,2592]{1,0:T(8,128)(2,1)} async-done(((bf16[576,2592]{1,0:T(8,128)(2,1)}), bf16[72,2592]{1,0:T(8,128)(2,1)}) %reduce-scatter.7.cloned.1.call-update) | async-done | bytes 373264
  465.4 6.5 %collective-permute-done.21 = bf16[72,2592]{1,0:T(8,128)(2,1)S(1)} collective-permute-done((bf16[72,2592]{1,0:T(8,128)(2,1)}, bf16[72,2592]{1,0:T(8,128)(2,1)S(1)}, u32[]{:S(2)}, u32[]{:S(2)}) %collective-permute-start.21) | collective-permute-done | bytes 373280 | tf_op jit(solution)/shard_map/ppermute | solution.py:63
  475.3 2.5 collective-permute-start.19
  477.8 2.3 collective-permute-done.22
  480.1 2.8 collective-permute-start.23
  484.0 8.3 %collective-permute-start.28 = (bf16[72,2592]{1,0:T(8,128)(2,1)S(1)}, bf16[72,2592]{1,0:T(8,128)(2,1)S(1)}, u32[]{:S(2)}, u32[]{:S(2)}) collective-permute-start(bf16[72,2592]{1,0:T(8,128)(2,1)S(1)} %add_convert_fusion.5.refs_2_), channel_id=1, source_target_pairs={{0,8},{8,0},{16,24},{24,16},{32,40},{40,32},{48,56},{56,48},{64,72... | collective-permute-start | bytes 1119752 | tf_op jit(solution)/shard_map/ppermute | solution.py:37
  494.0 4.2 collective-permute-start.24
  (360 shorter events, 121.6 us)
Async XLA Ops:
  10.1 9.3 %copy-start.65 = (bf16[2,192,576]{2,1,0:T(8,128)(2,1)S(1)}, bf16[2,192,576]{2,1,0:T(8,128)(2,1)}, u32[]{:S(2)}) copy-start(bf16[2,192,576]{2,1,0:T(8,128)(2,1)} %param.16) | copy-start | bytes 1327108
  11.1 25.3 %all-to-all-start = ((bf16[8,72,772]{2,1,0:T(8,128)(2,1)}), bf16[8,72,772]{2,1,0:T(8,128)(2,1)S(1)}, u32[]{:S(2)}, u32[]{:S(2)}) async-start(bf16[8,72,772]{2,1,0:T(8,128)(2,1)} %broadcast_in_dim.16), calls=%async_computation | async-start | bytes 2064384 | tf_op jit(solution)/shard_map/all_to_all | solution.py:45
  19.3 79.9 %all-gather.3.cloned.1.call-start = ((), (), s32[]{:S(2)}) async-start(), calls=%async_computation.9 | async-start | bytes 2985984 | tf_op jit(solution)/shard_map/all_gather | solution.py:374
  36.5 3.1 collective-permute-start
  44.5 28.2 %all-to-all-start.1 = ((bf16[8,2,3,64,256]{4,3,2,1,0:T(8,128)(2,1)}), bf16[8,2,3,64,256]{4,3,2,1,0:T(8,128)(2,1)S(1)}, u32[]{:S(2)}, u32[]{:S(2)}) async-start(bf16[8,2,3,64,256]{4,3,2,1,0:T(8,128)(2,1)} %broadcast_in_dim.19), calls=%async_computation.1 | async-start | bytes 3145728 | tf_op jit(solution)/shard_map/all_to_all | solution.py:41
  49.2 32.3 %copy-start.72 = (s32[1,4096]{1,0:T(1,128)S(1)}, s32[1,4096]{1,0:T(1,128)}, u32[]{:S(2)}) copy-start(s32[1,4096]{1,0:T(1,128)} %param.11) | copy-start | bytes 49156
  72.7 10.2 %collective-permute-start.1 = (bf16[8,2,3,64,256]{4,3,2,1,0:T(8,128)(2,1)S(1)}, bf16[8,2,3,64,256]{4,3,2,1,0:T(8,128)(2,1)S(1)}, u32[]{:S(2)}, u32[]{:S(2)}) collective-permute-start(bf16[8,2,3,64,256]{4,3,2,1,0:T(8,128)(2,1)S(1)} %all-to-all-done.1.own_ref), channel_id=1, source_target_pairs={{0,8},{8,0},{16,24},{24,16},{32,40},{40,32},{48,56},{56,48},{64,72... | collective-permute-start | bytes 4718600 | tf_op jit(solution)/shard_map/ppermute | solution.py:37
  75.0 24.2 %all-to-all-start.2 = ((bf16[8,72,768]{2,1,0:T(8,128)(2,1)}), bf16[8,72,768]{2,1,0:T(8,128)(2,1)}, u32[]{:S(2)}, u32[]{:S(2)}) async-start(bf16[8,72,768]{2,1,0:T(8,128)(2,1)} %broadcast_in_dim.20), calls=%async_computation.2 | async-start | bytes 1769472 | tf_op jit(solution)/shard_map/all_to_all | solution.py:45
  79.3 112.7 %all-gather.5.cloned.1.call-start = ((), (), s32[]{:S(2)}) async-start(), calls=%async_computation.10 | async-start | bytes 2985984 | tf_op jit(solution)/shard_map/all_gather | solution.py:375
  82.9 15.5 %copy-start = (bf16[8,2,3,64,256]{4,3,2,1,0:T(8,128)(2,1)}, bf16[8,2,3,64,256]{4,3,2,1,0:T(8,128)(2,1)S(1)}, u32[]{:S(2)}) copy-start(bf16[8,2,3,64,256]{4,3,2,1,0:T(8,128)(2,1)S(1)} %collective-permute-done.1.other_ref) | copy-start | bytes 4718596
  103.2 17.2 %copy-start.23 = (f32[256,576]{0,1:T(8,128)}, f32[256,576]{0,1:T(8,128)S(1)}, u32[]{:S(2)}) copy-start(f32[256,576]{0,1:T(8,128)S(1)} %get-tuple-element.125) | copy-start | bytes 1769476
  104.2 7.6 %collective-permute-start.2 = (bf16[256,576]{0,1:T(8,128)(2,1)}, bf16[256,576]{0,1:T(8,128)(2,1)}, u32[]{:S(2)}, u32[]{:S(2)}) collective-permute-start(bf16[256,576]{0,1:T(8,128)(2,1)} %multiply_convert_fusion.8), channel_id=1, source_target_pairs={{0,8},{8,0},{16,24},{24,16},{32,40},{40,32},{48,56},{56,48},{64,72... | collective-permute-start | bytes 884744 | tf_op jit(solution)/shard_map/ppermute | solution.py:37
  111.7 10.0 %collective-permute-start.4 = (bf16[576,768]{1,0:T(8,128)(2,1)}, bf16[576,768]{1,0:T(8,128)(2,1)}, u32[]{:S(2)}, u32[]{:S(2)}) collective-permute-start(bf16[576,768]{1,0:T(8,128)(2,1)} %bitcast.17), channel_id=1, source_target_pairs={{0,8},{8,0},{16,24},{24,16},{32,40},{40,32},{48,56},{56,48},{64,72... | collective-permute-start | bytes 2654216 | tf_op jit(solution)/shard_map/ppermute | solution.py:37
  118.5 1.9 collective-permute-start.3
  149.2 5.3 %collective-permute-start.5 = (bf16[8,2,3,64,256]{4,3,2,1,0:T(8,128)(2,1)S(1)}, bf16[8,2,3,64,256]{4,3,2,1,0:T(8,128)(2,1)S(1)}, u32[]{:S(2)}, u32[]{:S(2)}) collective-permute-start(bf16[8,2,3,64,256]{4,3,2,1,0:T(8,128)(2,1)S(1)} %all_to_all.35.own_ref), channel_id=1, source_target_pairs={{0,8},{8,0},{16,24},{24,16},{32,40},{40,32},{48,56},{56,48},{64,72... | collective-permute-start | bytes 4718600 | tf_op jit(solution)/shard_map/ppermute | solution.py:37
  197.1 7.4 %collective-permute-start.6 = (bf16[256,576]{0,1:T(8,128)(2,1)}, bf16[256,576]{0,1:T(8,128)(2,1)}, u32[]{:S(2)}, u32[]{:S(2)}) collective-permute-start(bf16[256,576]{0,1:T(8,128)(2,1)} %multiply_convert_fusion.6), channel_id=1, source_target_pairs={{0,8},{8,0},{16,24},{24,16},{32,40},{40,32},{48,56},{56,48},{64,72... | collective-permute-start | bytes 884744 | tf_op jit(solution)/shard_map/ppermute | solution.py:37
  198.4 9.3 %collective-permute-start.8 = (bf16[256,576]{0,1:T(8,128)(2,1)}, bf16[256,576]{0,1:T(8,128)(2,1)}, u32[]{:S(2)}, u32[]{:S(2)}) collective-permute-start(bf16[256,576]{0,1:T(8,128)(2,1)} %bitcast.24), channel_id=1, source_target_pairs={{0,8},{8,0},{16,24},{24,16},{32,40},{40,32},{48,56},{56,48},{64,72... | collective-permute-start | bytes 884744 | tf_op jit(solution)/shard_map/ppermute | solution.py:37
  211.4 4.1 collective-permute-start.9
  212.6 3.8 collective-permute-start.7
  221.5 12.0 %collective-permute-start.10 = (bf16[576,288]{1,0:T(8,128)(2,1)}, bf16[576,288]{1,0:T(8,128)(2,1)}, u32[]{:S(2)}, u32[]{:S(2)}) collective-permute-start(bf16[576,288]{1,0:T(8,128)(2,1)} %broadcast_select_fusion.6), channel_id=1, source_target_pairs={{0,8},{8,0},{16,24},{24,16},{32,40},{40,32},{48,56},{56,48},{64,72... | collective-permute-start | bytes 995336 | tf_op jit(solution)/shard_map/ppermute | solution.py:37
  263.8 3.4 collective-permute-start.11
  269.0 28.3 %all-to-all-start.4 = ((bf16[8,2,3,64,256]{4,3,2,1,0:T(8,128)(2,1)}), bf16[8,2,3,64,256]{4,3,2,1,0:T(8,128)(2,1)}, u32[]{:S(2)}, u32[]{:S(2)}) async-start(bf16[8,2,3,64,256]{4,3,2,1,0:T(8,128)(2,1)} %add_convert_fusion.1), calls=%async_computation.4 | async-start | bytes 3145728 | tf_op jit(solution)/shard_map/all_to_all | solution.py:41
  273.3 89.7 %reduce-scatter.9.cloned.1.call-start = ((), (), s32[]{:S(2)}) async-start(), calls=%async_computation.12 | async-start | bytes 3483648
  274.1 25.0 %copy-start.17 = (f32[9,64,256]{2,1,0:T(8,128)S(1)}, f32[9,64,256]{2,1,0:T(8,128)}, u32[]{:S(2)}) copy-start(f32[9,64,256]{2,1,0:T(8,128)} %copy-done.16) | copy-start | bytes 1769476
  274.1 189.6 %reduce-scatter.7.cloned.1.call-start = ((), (), s32[]{:S(2)}) async-start(), calls=%async_computation.11 | async-start | bytes 3483648
  302.2 2.5 collective-permute-start.12
  307.1 2.2 collective-permute-start.13
  310.7 10.3 %copy-start.21 = (f32[256,576]{0,1:T(8,128)}, f32[256,576]{0,1:T(8,128)S(1)}, u32[]{:S(2)}) copy-start(f32[256,576]{0,1:T(8,128)S(1)} %multiply_add_fusion) | copy-start | bytes 1769476
  312.1 11.4 %collective-permute-start.14 = (bf16[576,288]{1,0:T(8,128)(2,1)}, bf16[576,288]{1,0:T(8,128)(2,1)}, u32[]{:S(2)}, u32[]{:S(2)}) collective-permute-start(bf16[576,288]{1,0:T(8,128)(2,1)} %broadcast_select_fusion.5), channel_id=1, source_target_pairs={{0,8},{8,0},{16,24},{24,16},{32,40},{40,32},{48,56},{56,48},{64,72... | collective-permute-start | bytes 995336 | tf_op jit(solution)/shard_map/ppermute | solution.py:37
  353.8 3.6 collective-permute-start.15
  359.2 27.6 %all-to-all-start.5 = ((bf16[8,2,3,64,256]{4,3,2,1,0:T(8,128)(2,1)}), bf16[8,2,3,64,256]{4,3,2,1,0:T(8,128)(2,1)S(1)}, u32[]{:S(2)}, u32[]{:S(2)}) async-start(bf16[8,2,3,64,256]{4,3,2,1,0:T(8,128)(2,1)} %add_convert_fusion), calls=%async_computation.5 | async-start | bytes 3145728 | tf_op jit(solution)/shard_map/all_to_all | solution.py:41
  362.9 24.2 %copy-start.15 = (f32[9,64,256]{2,1,0:T(8,128)S(1)}, f32[9,64,256]{2,1,0:T(8,128)}, u32[]{:S(2)}) copy-start(f32[9,64,256]{2,1,0:T(8,128)} %copy-done.14) | copy-start | bytes 1769476
  363.0 31.3 %collective-permute-start.25 = (bf16[72,2592]{1,0:T(8,128)(2,1)}, bf16[72,2592]{1,0:T(8,128)(2,1)}, u32[]{:S(2)}, u32[]{:S(2)}) collective-permute-start(bf16[72,2592]{1,0:T(8,128)(2,1)} %reduce-scatter.9.cloned.1.call-done), channel_id=1, source_target_pairs={{0,16},{8,24},{16,0},{24,8},{32,48},{40,56},{48,32},{56,40},{64,80... | collective-permute-start | bytes 1119752 | tf_op jit(solution)/shard_map/ppermute | solution.py:63
  390.2 8.4 %collective-permute-start.16 = (bf16[576,960]{1,0:T(8,128)(2,1)}, bf16[576,960]{1,0:T(8,128)(2,1)}, u32[]{:S(2)}, u32[]{:S(2)}) collective-permute-start(bf16[576,960]{1,0:T(8,128)(2,1)} %get-tuple-element.130), channel_id=1, source_target_pairs={{0,8},{8,0},{16,24},{24,16},{32,40},{40,32},{48,56},{56,48},{64,72... | collective-permute-start | bytes 3317768 | tf_op jit(solution)/shard_map/ppermute | solution.py:37
  395.4 10.8 %collective-permute-start.26 = (bf16[72,2592]{1,0:T(8,128)(2,1)S(1)}, bf16[72,2592]{1,0:T(8,128)(2,1)}, u32[]{:S(2)}, u32[]{:S(2)}) collective-permute-start(bf16[72,2592]{1,0:T(8,128)(2,1)S(1)} %add_convert_fusion.7), channel_id=1, source_target_pairs={{0,32},{8,40},{16,48},{24,56},{32,0},{40,8},{48,16},{56,24},{64,96... | collective-permute-start | bytes 1119752 | tf_op jit(solution)/shard_map/ppermute | solution.py:63
  401.7 23.2 %all-to-all-start.6 = ((bf16[8,72,964]{2,1,0:T(8,128)(2,1)}), bf16[8,72,964]{2,1,0:T(8,128)(2,1)S(1)}, u32[]{:S(2)}, u32[]{:S(2)}) async-start(bf16[8,72,964]{2,1,0:T(8,128)(2,1)} %bitcast.38), calls=%async_computation.6 | async-start | bytes 2359296 | tf_op jit(solution)/shard_map/all_to_all | solution.py:45
  407.4 66.9 %copy-start.22 = (f32[256,576]{0,1:T(8,128)S(1)}, f32[256,576]{0,1:T(8,128)}, u32[]{:S(2)}) copy-start(f32[256,576]{0,1:T(8,128)} %copy-done.21) | copy-start | bytes 1769476
  407.4 66.9 %copy-start.63 = (f32[256,576]{0,1:T(8,128)S(1)}, f32[256,576]{0,1:T(8,128)}, u32[]{:S(2)}) copy-start(f32[256,576]{0,1:T(8,128)} %get-tuple-element.129) | copy-start | bytes 1769476
  407.4 75.6 %collective-permute-start.27 = (bf16[72,2592]{1,0:T(8,128)(2,1)S(1)}, bf16[72,2592]{1,0:T(8,128)(2,1)}, u32[]{:S(2)}, u32[]{:S(2)}) collective-permute-start(bf16[72,2592]{1,0:T(8,128)(2,1)S(1)} %add_convert_fusion.6), channel_id=1, source_target_pairs={{0,64},{8,72},{16,80},{24,88},{32,96},{40,104},{48,112},{56,120},{... | collective-permute-start | bytes 1119752 | tf_op jit(solution)/shard_map/ppermute | solution.py:63
  425.2 39.0 %collective-permute-start.17 = (bf16[72,964]{1,0:T(8,128)(2,1)S(1)}, bf16[72,964]{1,0:T(8,128)(2,1)S(1)}, u32[]{:S(2)}, u32[]{:S(2)}) collective-permute-start(bf16[72,964]{1,0:T(8,128)(2,1)S(1)} %reduce_sum.162), channel_id=1, source_target_pairs={{0,16},{8,24},{16,0},{24,8},{32,48},{40,56},{48,32},{56,40},{64,80... | collective-permute-start | bytes 416456 | tf_op jit(solution)/shard_map/ppermute | solution.py:63
  463.7 8.1 %collective-permute-start.21 = (bf16[72,2592]{1,0:T(8,128)(2,1)}, bf16[72,2592]{1,0:T(8,128)(2,1)S(1)}, u32[]{:S(2)}, u32[]{:S(2)}) collective-permute-start(bf16[72,2592]{1,0:T(8,128)(2,1)} %reduce-scatter.7.cloned.1.call-done), channel_id=1, source_target_pairs={{0,16},{8,24},{16,0},{24,8},{32,48},{40,56},{48,32},{56,40},{64,80... | collective-permute-start | bytes 1119752 | tf_op jit(solution)/shard_map/ppermute | solution.py:63
  464.2 11.0 %collective-permute-start.18 = (bf16[72,964]{1,0:T(8,128)(2,1)S(1)}, bf16[72,964]{1,0:T(8,128)(2,1)S(1)}, u32[]{:S(2)}, u32[]{:S(2)}) collective-permute-start(bf16[72,964]{1,0:T(8,128)(2,1)S(1)} %add_convert_fusion.14), channel_id=1, source_target_pairs={{0,32},{8,40},{16,48},{24,56},{32,0},{40,8},{48,16},{56,24},{64,96... | collective-permute-start | bytes 416456 | tf_op jit(solution)/shard_map/ppermute | solution.py:63
  472.9 7.1 %collective-permute-start.22 = (bf16[72,2592]{1,0:T(8,128)(2,1)S(1)}, bf16[72,2592]{1,0:T(8,128)(2,1)S(1)}, u32[]{:S(2)}, u32[]{:S(2)}) collective-permute-start(bf16[72,2592]{1,0:T(8,128)(2,1)S(1)} %add_convert_fusion.10), channel_id=1, source_target_pairs={{0,32},{8,40},{16,48},{24,56},{32,0},{40,8},{48,16},{56,24},{64,96... | collective-permute-start | bytes 1119752 | tf_op jit(solution)/shard_map/ppermute | solution.py:63
  475.3 17.0 %collective-permute-start.19 = (bf16[72,964]{1,0:T(8,128)(2,1)S(1)}, bf16[72,964]{1,0:T(8,128)(2,1)S(1)}, u32[]{:S(2)}, u32[]{:S(2)}) collective-permute-start(bf16[72,964]{1,0:T(8,128)(2,1)S(1)} %add_convert_fusion.13), channel_id=1, source_target_pairs={{0,64},{8,72},{16,80},{24,88},{32,96},{40,104},{48,112},{56,120},{... | collective-permute-start | bytes 416456 | tf_op jit(solution)/shard_map/ppermute | solution.py:63
  480.1 13.7 %collective-permute-start.23 = (bf16[72,2592]{1,0:T(8,128)(2,1)S(1)}, bf16[72,2592]{1,0:T(8,128)(2,1)S(1)}, u32[]{:S(2)}, u32[]{:S(2)}) collective-permute-start(bf16[72,2592]{1,0:T(8,128)(2,1)S(1)} %add_convert_fusion.9), channel_id=1, source_target_pairs={{0,64},{8,72},{16,80},{24,88},{32,96},{40,104},{48,112},{56,120},{... | collective-permute-start | bytes 1119752 | tf_op jit(solution)/shard_map/ppermute | solution.py:63
  484.0 14.2 %collective-permute-start.28 = (bf16[72,2592]{1,0:T(8,128)(2,1)S(1)}, bf16[72,2592]{1,0:T(8,128)(2,1)S(1)}, u32[]{:S(2)}, u32[]{:S(2)}) collective-permute-start(bf16[72,2592]{1,0:T(8,128)(2,1)S(1)} %add_convert_fusion.5.refs_2_), channel_id=1, source_target_pairs={{0,8},{8,0},{16,24},{24,16},{32,40},{40,32},{48,56},{56,48},{64,72... | collective-permute-start | bytes 1119752 | tf_op jit(solution)/shard_map/ppermute | solution.py:37
  492.4 6.4 %collective-permute-start.20 = (bf16[72,964]{1,0:T(8,128)(2,1)S(1)}, bf16[72,964]{1,0:T(8,128)(2,1)S(1)}, u32[]{:S(2)}, u32[]{:S(2)}) collective-permute-start(bf16[72,964]{1,0:T(8,128)(2,1)S(1)} %add_convert_fusion.12.refs_4_), channel_id=1, source_target_pairs={{0,8},{8,0},{16,24},{24,16},{32,40},{40,32},{48,56},{56,48},{64,72... | collective-permute-start | bytes 416456 | tf_op jit(solution)/shard_map/ppermute | solution.py:37
  494.0 5.6 %collective-permute-start.24 = (bf16[72,2592]{1,0:T(8,128)(2,1)S(1)}, bf16[72,2592]{1,0:T(8,128)(2,1)S(1)}, u32[]{:S(2)}, u32[]{:S(2)}) collective-permute-start(bf16[72,2592]{1,0:T(8,128)(2,1)S(1)} %add_convert_fusion.8.refs_0_), channel_id=1, source_target_pairs={{0,8},{8,0},{16,24},{24,16},{32,40},{40,32},{48,56},{56,48},{64,72... | collective-permute-start | bytes 1119752 | tf_op jit(solution)/shard_map/ppermute | solution.py:37
  (73 other events, 168.2 us)
Sparse Core Ops, SparseCore 0:
  26.3 71.7 all-gather.2
  120.0 71.8 all-gather.4
  278.1 79.8 reduce-scatter.8
  361.8 101.8 reduce-scatter.6

commit v4 on v3

--- a/solution.py
+++ b/solution.py
@@ -271,6 +271,39 @@
 VMEM_SPEC = pl.BlockSpec(memory_space=pltpu.VMEM)
 
 
+def dispatch_kernel(me, x_ref, *outs):
+    for dx, out in enumerate(outs):
+        for dz in range(2):
+            out[dz] = x_ref[jnp.bitwise_xor(me[0], 4 * dz + dx)]
+
+
+def dispatch(me, x):
+    return pl.pallas_call(
+        dispatch_kernel,
+        grid_spec=pltpu.PrefetchScalarGridSpec(
+            num_scalar_prefetch=1,
+            grid=(),
+            in_specs=[VMEM_SPEC],
+            out_specs=[VMEM_SPEC] * 4,
+        ),
+        out_shape=[jax.ShapeDtypeStruct((2,) + x.shape[1:], BF16)] * 4,
+        compiler_params=pltpu.CompilerParams(vmem_limit_bytes=40 * 2**20),
+        name="dispatch",
+    )(me, x)
+
+
+def across(x, d):
+    return lax.ppermute(x, "fsdp", [(i, i ^ d) for i in range(FSDP)])
+
+
+def scatter_by_permutes(me, x):
+    parts = dispatch(me, x.reshape(FSDP, -1, x.shape[1]))
+    total = parts[0].astype(F32)
+    for dx in range(1, 4):
+        total = total + across(parts[dx], dx).astype(F32)
+    return (total[0] + across(total[1].astype(BF16), 4).astype(F32)).astype(BF16)
+
+
 UNITS = FF // FSDP // 2
 
 
@@ -347,6 +380,7 @@
     place = lax.axis_index("ctx")
     core = jnp.bitwise_and(place, 1)
     first_core = core == 0
+    me = lax.axis_index("fsdp").reshape(1)
 
     def my_half(left, right):
         return jnp.where(first_core, left, right)
@@ -451,27 +485,25 @@
         d_gu = jnp.concatenate([d_gate, d_up], 1).astype(BF16)
         part = ein("tf,df->td", d_gu, wgu)
         d_norm = part[:ROWS] + to_partner(part[ROWS:].astype(BF16)).astype(F32)
-        d_wdown = ein("tf,td->fd", inner, both_grad).astype(BF16)
-        d_wgu = ein("td,tf->df", both_in, d_gu).astype(BF16)
         d_gain_m = jnp.sum(d_norm * unit_m, 0)
         d_hidden = d_hidden + norm_back(d_norm * gains[layer, 1], unit_m, rms_m)
         grad_b = d_hidden.astype(BF16)
-        d_wout = mm(attn_out, grad_b)
         do_t = ein("ad,td->at", wout, grad_b).astype(BF16).reshape(HEADS, HEAD_DIM, ROWS)
+        dq_t, dkv_own, dkv_other = attention_back(scalars, q_t, kv_own, kv_other, o_t, do_t, lse)
+        dkv = (dkv_own.astype(F32) + to_partner(dkv_other).astype(F32)).astype(BF16)
+        d_gu, late_in, late_grad, _ = lax.optimization_barrier((d_gu, both_in, grad_b, dkv))
+        d_wgu = ein("td,tf->df", late_in, d_gu).astype(BF16)
+        d_wdown = ein("tf,td->fd", inner, both_grad).astype(BF16)
+        d_wout = mm(attn_out, late_grad).astype(BF16)
         wout_half = D // 2
-        d_wout = d_wout.astype(BF16)
         wout_mine = my_half(d_wout[:, :wout_half], d_wout[:, wout_half:])
         wout_theirs = my_half(d_wout[:, wout_half:], d_wout[:, :wout_half])
         d_mlp = [d_wgu, d_wdown.reshape(D, HALF), sum_pair(wout_mine, to_partner(wout_theirs))]
-        do_t, d_mlp = lax.optimization_barrier((do_t, jnp.concatenate(d_mlp, 1)))
-        share = lax.psum_scatter(d_mlp, "fsdp", scatter_dimension=0, tiled=True)
+        d_mlp = jnp.concatenate(d_mlp, 1)
         if layer == 1:
-            share1 = share
+            share1 = lax.psum_scatter(d_mlp, "fsdp", scatter_dimension=0, tiled=True)
         else:
-            share0 = share
-        dq_t, dkv_own, dkv_other = attention_back(scalars, q_t, kv_own, kv_other, o_t, do_t, lse)
-        dkv = (dkv_own.astype(F32) + to_partner(dkv_other).astype(F32)).astype(BF16)
-        if layer == 0:
+            share0 = scatter_by_permutes(me, d_mlp)
             share1 = sum_chips(lax.optimization_barrier((share1, dkv))[0])
         dkv = jnp.sum(over_chips(dkv).astype(F32), 0)
         turned = jnp.concatenate([dq_t, dkv[0]], 0)

time: 517 us -> 523 us (1.012)
  blocking collectives: 23.4 us -> 47.7 us
  waiting for transfers between devices: 174 us -> 155 us
  other arithmetic: 42.4 us -> 53 us
  local copies, waits for them, and re-layouts: 61.2 us -> 50.9 us
    all_to_all x3 -> x2, waiting for transfers between devices: 69 us -> 23.4 us  [over_chips(): lax.all_to_all(x, 'ctx', 0, 0, axis_index_groups=SAME_CORE, tiled=True)]
    optimization_barrier x1, waiting for transfers between devices: 0.02 us -> 45.3 us  [local(): share1 = sum_chips(lax.optimization_barrier((share1, dkv))[0])]
    unnamed x5 -> x3, waiting for transfers between devices: 37.9 us -> 0.05 us
    ppermute x0 -> x4, waiting for transfers between devices: none -> 31.7 us  [across(): return lax.ppermute(x, 'fsdp', [(i, i ^ d) for i in range(FSDP)])]
    all_to_all x1 -> x2, blocking collectives: 23.4 us -> 47.7 us  [over_chips(): lax.all_to_all(x, 'ctx', 0, 0, axis_index_groups=SAME_CORE, tiled=True)]
    all_to_all x3, waiting for transfers between devices: 22.6 us -> 8.16 us  [over_fsdp(): return lax.all_to_all(x, 'fsdp', 0, 0, tiled=True)]
    concatenate x2 -> x6, other arithmetic: 3.54 us -> 11.3 us  [the longest x2 4.05 us: local(): d_gu = jnp.concatenate([d_gate, d_up], 1).astype(BF16)]
    unnamed x164 -> x162, local copies, waits for them, and re-layouts: 24.3 us -> 17.3 us
  transfers between devices with their start and end apart: 39 -> 41, of which waited for: 17 -> 18; matrix products, arithmetic and copies ran while one was open for 19% -> 17% of each run, Pallas kernels for 11% -> 6%
where the time goes in v4:
time: 523 us; the launch traced here: 516 us
  waiting for transfers between devices  155 us (30%)
  Pallas kernels  77.8 us (15%)
  starting transfers between devices  73.2 us (14%)
  other arithmetic  53 us (10%)
  local copies, waits for them, and re-layouts  50.9 us (10%)
  blocking collectives  47.7 us (9%)
  matrix products  40.4 us (8%)
  between operations  17.9 us (3%)
    all_to_all x2, blocking collectives, over_chips(): lax.all_to_all(x, 'ctx', 0, 0, axis_index_groups=SAME_CORE, tiled=True)  47.7 us
    optimization_barrier x1, waiting for transfers between devices, local(): share1 = sum_chips(lax.optimization_barrier((share1, dkv))[0])  45.3 us
    pallas_call x2, Pallas kernels, attention_back(): pl.pallas_call(backward_kernel, grid_spec=pltpu.PrefetchScalarGridSpec(nu...  44.6 us
    dot_general x18, matrix products, ein(): return jnp.einsum(spec, a, b, preferred_element_type=F32)  31.7 us
    ppermute x4, waiting for transfers between devices, across(): return lax.ppermute(x, 'fsdp', [(i, i ^ d) for i in range(FSDP)])  31.7 us
    pallas_call x2, Pallas kernels, attention(): pl.pallas_call(forward_kernel, grid_spec=pltpu.PrefetchScalarGridSpec(num...  30.9 us
    ppermute x20, starting transfers between devices, to_partner(): return lax.ppermute(x, 'ctx', PARTNER)  28.6 us
    all_to_all x2, waiting for transfers between devices, over_chips(): lax.all_to_all(x, 'ctx', 0, 0, axis_index_groups=SAME_CORE, tiled=True)  23.4 us
  transfers between devices with their start and end apart: 41, of which 18 were waited for; matrix products, arithmetic and copies ran while one was open for 17% of the time, Pallas kernels for 6%

profile of v4, /device:TPU:1, one launch (start us, length us, event | category | flops | bytes accessed | tf_op | source)
XLA Modules:
  0.0 516.0 jit_solution(5216862973508022518)
XLA Ops:
  11.1 8.2 %all-to-all-start = ((bf16[8,72,772]{2,1,0:T(8,128)(2,1)}), bf16[8,72,772]{2,1,0:T(8,128)(2,1)S(1)}, u32[]{:S(2)}, u32[]{:S(2)}) async-start(bf16[8,72,772]{2,1,0:T(8,128)(2,1)} %broadcast_in_dim.16), calls=%async_computation | async-start | bytes 2064384 | tf_op jit(solution)/shard_map/all_to_all | solution.py:45
  28.3 8.2 %all-to-all-done = bf16[8,72,772]{2,1,0:T(8,128)(2,1)S(1)} async-done(((bf16[8,72,772]{2,1,0:T(8,128)(2,1)}), bf16[8,72,772]{2,1,0:T(8,128)(2,1)S(1)}, u32[]{:S(2)}, u32[]{:S(2)}) %all-to-all-start) | async-done | bytes 889376 | tf_op jit(solution)/shard_map/all_to_all | solution.py:45
  44.6 4.7 all-to-all-start.1
  49.4 23.4 %all-to-all-done.1.own_ref = bf16[8,2,3,64,256]{4,3,2,1,0:T(8,128)(2,1)S(1)} async-done(((bf16[8,2,3,64,256]{4,3,2,1,0:T(8,128)(2,1)}), bf16[8,2,3,64,256]{4,3,2,1,0:T(8,128)(2,1)S(1)}, u32[]{:S(2)}, u32[]{:S(2)}) %all-to-all-start.1) | async-done | bytes 1572896 | tf_op jit(solution)/shard_map/all_to_all | solution.py:41
  75.0 4.2 all-to-all-start.2
  83.0 15.5 %attention.2 = (f32[9,64,256]{2,1,0:T(8,128)S(1)}, f32[3,2,1,384]{3,2,1,0:T(1,128)S(1)}) custom-call(s32[39]{0:T(128)S(1)} %concatenate.100.sc, bf16[9,64,256]{2,1,0:T(8,128)(2,1)S(1)} %fusion.37.q_ref, bf16[8,2,3,64,256]{4,3,2,1,0:T(8,128)(2,1)S(1)} %all-to-all-done.1.own_ref, bf16[8,2,3,64,256]{4,3,2,1,0:T(8,128)(2,1)S(1)} %collective-permute-done.1.other_ref), custom_call_target="tpu_custom_call" | custom-call | tf_op jit(solution)/shard_map/attention/pallas_call | solution.py:225
  101.1 2.2 multiply_reduce_fusion.8
  106.9 2.1 slice.292
  109.0 2.7 reshape.319
  111.8 3.3 fusion.8
  125.5 23.4 %all_to_all.35.own_ref = bf16[8,2,3,64,256]{4,3,2,1,0:T(8,128)(2,1)S(1)} all-to-all(bf16[8,2,3,64,256]{4,3,2,1,0:T(8,128)(2,1)S(1)} %broadcast_in_dim.21), channel_id=1, replica_groups={{0,16,32,48,64,80,96,112},{8,24,40,56,72,88,104,120},{1,17,33,49,65,81,..., dimensions={0} | all-to-all | bytes 3145728 | tf_op jit(solution)/shard_map/all_to_all | solution.py:41
  148.9 2.2 collective-permute-start.5
  151.2 3.0 collective-permute-done.5.other_ref
  154.2 15.5 %attention.3 = (f32[9,64,256]{2,1,0:T(8,128)S(1)}, f32[3,2,1,384]{3,2,1,0:T(1,128)S(1)}) custom-call(s32[39]{0:T(128)S(1)} %concatenate.100.sc, bf16[9,64,256]{2,1,0:T(8,128)(2,1)S(1)} %fusion.34.q_ref, bf16[8,2,3,64,256]{4,3,2,1,0:T(8,128)(2,1)S(1)} %all_to_all.35.own_ref, bf16[8,2,3,64,256]{4,3,2,1,0:T(8,128)(2,1)S(1)} %collective-permute-done.5.other_ref), custom_call_target="tpu_custom_call" | custom-call | tf_op jit(solution)/shard_map/attention/pallas_call | solution.py:225
  172.3 19.2 %all-gather.5.cloned.1.call-done = bf16[576,2304]{1,0:T(8,128)(2,1)} async-done(((bf16[72,2304]{1,0:T(8,128)(2,1)}), bf16[576,2304]{1,0:T(8,128)(2,1)}) %all-gather.5.cloned.1.call-update) | async-done | bytes 2654224 | tf_op jit(solution)/shard_map/all_gather | solution.py:409
  192.7 2.4 multiply_reduce_fusion.6
  198.3 2.1 slice.315
  200.4 3.4 reshape.321
  203.8 3.1 fusion.4
  207.0 2.5 multiply_convert_fusion.3
  213.6 2.1 fusion.77
  217.2 22.0 %attention_back.2 = (f32[9,64,256]{2,1,0:T(8,128)S(1)}, bf16[8,2,3,64,256]{4,3,2,1,0:T(8,128)(2,1)S(1)}, bf16[8,2,3,64,256]{4,3,2,1,0:T(8,128)(2,1)S(1)}) custom-call(s32[39]{0:T(128)S(1)} %concatenate.100.sc, bf16[9,64,256]{2,1,0:T(8,128)(2,1)S(1)} %copy-done.5, bf16[8,2,3,64,256]{4,3,2,1,0:T(8,128)(2,1)S(1)} %all_to_all.35.own_ref, ...), custom_call_target="tpu_custom_call" | custom-call | tf_op jit(solution)/shard_map/attention_back/pallas_call | solution.py:248
  239.4 3.2 collective-permute-done.10
  243.4 24.3 %all_to_all.36 = bf16[8,2,3,64,256]{4,3,2,1,0:T(8,128)(2,1)S(1)} all-to-all(bf16[8,2,3,64,256]{4,3,2,1,0:T(8,128)(2,1)S(1)} %add_convert_fusion.1), channel_id=1, replica_groups={{0,16,32,48,64,80,96,112},{8,24,40,56,72,88,104,120},{1,17,33,49,65,81,..., dimensions={0} | all-to-all | bytes 3145728 | tf_op jit(solution)/shard_map/all_to_all | solution.py:41
  275.1 3.4 multiply_convert_fusion.1
  286.7 22.7 %attention_back.3 = (f32[9,64,256]{2,1,0:T(8,128)S(1)}, bf16[8,2,3,64,256]{4,3,2,1,0:T(8,128)(2,1)S(1)}, bf16[8,2,3,64,256]{4,3,2,1,0:T(8,128)(2,1)}) custom-call(s32[39]{0:T(128)S(1)} %concatenate.100.sc, bf16[9,64,256]{2,1,0:T(8,128)(2,1)S(1)} %fusion.37.q_ref, bf16[8,2,3,64,256]{4,3,2,1,0:T(8,128)(2,1)S(1)} %all-to-all-done.1.own_ref, ...), custom_call_target="tpu_custom_call" | custom-call | tf_op jit(solution)/shard_map/attention_back/pallas_call | solution.py:248
  311.9 2.6 convolution_convert_fusion.4
  316.1 2.2 reshape.329
  318.3 3.9 convolution_convert_fusion
  324.3 2.7 pad_maximum_fusion.3
  327.0 3.3 add_convert_fusion
  336.0 3.7 convolution_convert_fusion.1
  343.9 2.4 collective-permute-start.21
  349.4 4.3 all-to-all-start.5
  353.7 10.3 %collective-permute-done.20 = bf16[2,72,2592]{2,1,0:T(8,128)(2,1)} collective-permute-done((bf16[2,72,2592]{2,1,0:T(8,128)(2,1)S(1)}, bf16[2,72,2592]{2,1,0:T(8,128)(2,1)}, u32[]{:S(2)}, u32[]{:S(2)}) %collective-permute-start.20) | collective-permute-done | bytes 746528 | tf_op jit(solution)/shard_map/ppermute | solution.py:296
  364.0 21.3 %collective-permute-done.21 = bf16[2,72,2592]{2,1,0:T(8,128)(2,1)} collective-permute-done((bf16[2,72,2592]{2,1,0:T(8,128)(2,1)S(1)}, bf16[2,72,2592]{2,1,0:T(8,128)(2,1)}, u32[]{:S(2)}, u32[]{:S(2)}) %collective-permute-start.21) | collective-permute-done | bytes 746528 | tf_op jit(solution)/shard_map/ppermute | solution.py:296
  397.5 3.9 collective-permute-start.14
  401.6 2.3 fusion.27
  408.8 3.8 all-to-all-start.6
  412.6 45.3 %reduce-scatter.4.cloned.1.call-done = bf16[72,2592]{1,0:T(8,128)(2,1)} async-done(((bf16[576,2592]{1,0:T(8,128)(2,1)}), bf16[72,2592]{1,0:T(8,128)(2,1)}) %reduce-scatter.4.cloned.1.call-update) | async-done | bytes 373264 | tf_op jit(solution)/shard_map/optimization_barrier | solution.py:507
  459.7 6.3 %collective-permute-done.29 = bf16[72,2592]{1,0:T(8,128)(2,1)S(1)} collective-permute-done((bf16[72,2592]{1,0:T(8,128)(2,1)}, bf16[72,2592]{1,0:T(8,128)(2,1)S(1)}, u32[]{:S(2)}, u32[]{:S(2)}) %collective-permute-start.29) | collective-permute-done | bytes 373280 | tf_op jit(solution)/shard_map/ppermute | solution.py:63
  469.3 2.6 collective-permute-start.26
  474.3 3.1 collective-permute-start.31
  477.4 8.3 %collective-permute-done.16 = bf16[72,964]{1,0:T(8,128)(2,1)S(1)} collective-permute-done((bf16[72,964]{1,0:T(8,128)(2,1)S(1)}, bf16[72,964]{1,0:T(8,128)(2,1)S(1)}, u32[]{:S(2)}, u32[]{:S(2)}) %collective-permute-start.16) | collective-permute-done | bytes 138848 | tf_op jit(solution)/shard_map/ppermute | solution.py:63
  485.7 2.9 collective-permute-start.17
  488.7 8.7 %collective-permute-start.27 = (bf16[72,2592]{1,0:T(8,128)(2,1)S(1)}, bf16[72,2592]{1,0:T(8,128)(2,1)S(1)}, u32[]{:S(2)}, u32[]{:S(2)}) collective-permute-start(bf16[72,2592]{1,0:T(8,128)(2,1)S(1)} %add_convert_fusion.6.refs_0_), channel_id=1, source_target_pairs={{0,8},{8,0},{16,24},{24,16},{32,40},{40,32},{48,56},{56,48},{64,72... | collective-permute-start | bytes 1119752 | tf_op jit(solution)/shard_map/ppermute | solution.py:37
  499.3 4.5 collective-permute-start.18
  507.3 2.0 unpack.1
  (372 shorter events, 118.8 us)
Async XLA Ops:
  10.1 9.3 %copy-start.65 = (bf16[2,192,576]{2,1,0:T(8,128)(2,1)S(1)}, bf16[2,192,576]{2,1,0:T(8,128)(2,1)}, u32[]{:S(2)}) copy-start(bf16[2,192,576]{2,1,0:T(8,128)(2,1)} %param.16) | copy-start | bytes 1327108
  11.1 25.3 %all-to-all-start = ((bf16[8,72,772]{2,1,0:T(8,128)(2,1)}), bf16[8,72,772]{2,1,0:T(8,128)(2,1)S(1)}, u32[]{:S(2)}, u32[]{:S(2)}) async-start(bf16[8,72,772]{2,1,0:T(8,128)(2,1)} %broadcast_in_dim.16), calls=%async_computation | async-start | bytes 2064384 | tf_op jit(solution)/shard_map/all_to_all | solution.py:45
  19.3 80.0 %all-gather.3.cloned.1.call-start = ((), (), s32[]{:S(2)}) async-start(), calls=%async_computation.8 | async-start | bytes 2985984 | tf_op jit(solution)/shard_map/all_gather | solution.py:408
  36.5 3.1 collective-permute-start
  44.6 28.2 %all-to-all-start.1 = ((bf16[8,2,3,64,256]{4,3,2,1,0:T(8,128)(2,1)}), bf16[8,2,3,64,256]{4,3,2,1,0:T(8,128)(2,1)S(1)}, u32[]{:S(2)}, u32[]{:S(2)}) async-start(bf16[8,2,3,64,256]{4,3,2,1,0:T(8,128)(2,1)} %broadcast_in_dim.19), calls=%async_computation.1 | async-start | bytes 3145728 | tf_op jit(solution)/shard_map/all_to_all | solution.py:41
  49.2 32.3 %copy-start.71 = (s32[1,4096]{1,0:T(1,128)S(1)}, s32[1,4096]{1,0:T(1,128)}, u32[]{:S(2)}) copy-start(s32[1,4096]{1,0:T(1,128)} %param.11) | copy-start | bytes 49156
  72.7 10.3 %collective-permute-start.1 = (bf16[8,2,3,64,256]{4,3,2,1,0:T(8,128)(2,1)S(1)}, bf16[8,2,3,64,256]{4,3,2,1,0:T(8,128)(2,1)S(1)}, u32[]{:S(2)}, u32[]{:S(2)}) collective-permute-start(bf16[8,2,3,64,256]{4,3,2,1,0:T(8,128)(2,1)S(1)} %all-to-all-done.1.own_ref), channel_id=1, source_target_pairs={{0,8},{8,0},{16,24},{24,16},{32,40},{40,32},{48,56},{56,48},{64,72... | collective-permute-start | bytes 4718600 | tf_op jit(solution)/shard_map/ppermute | solution.py:37
  75.0 24.3 %all-to-all-start.2 = ((bf16[8,72,768]{2,1,0:T(8,128)(2,1)}), bf16[8,72,768]{2,1,0:T(8,128)(2,1)}, u32[]{:S(2)}, u32[]{:S(2)}) async-start(bf16[8,72,768]{2,1,0:T(8,128)(2,1)} %broadcast_in_dim.20), calls=%async_computation.2 | async-start | bytes 1769472 | tf_op jit(solution)/shard_map/all_to_all | solution.py:45
  79.3 112.3 %all-gather.5.cloned.1.call-start = ((), (), s32[]{:S(2)}) async-start(), calls=%async_computation.9 | async-start | bytes 2985984 | tf_op jit(solution)/shard_map/all_gather | solution.py:409
  83.0 15.5 %copy-start = (bf16[8,2,3,64,256]{4,3,2,1,0:T(8,128)(2,1)}, bf16[8,2,3,64,256]{4,3,2,1,0:T(8,128)(2,1)S(1)}, u32[]{:S(2)}) copy-start(bf16[8,2,3,64,256]{4,3,2,1,0:T(8,128)(2,1)S(1)} %collective-permute-done.1.other_ref) | copy-start | bytes 4718596
  101.1 4.8 copy-start.40
  103.3 16.9 %copy-start.15 = (f32[256,576]{0,1:T(8,128)}, f32[256,576]{0,1:T(8,128)S(1)}, u32[]{:S(2)}) copy-start(f32[256,576]{0,1:T(8,128)S(1)} %get-tuple-element.140) | copy-start | bytes 1769476
  104.2 7.6 %collective-permute-start.2 = (bf16[256,576]{0,1:T(8,128)(2,1)}, bf16[256,576]{0,1:T(8,128)(2,1)}, u32[]{:S(2)}, u32[]{:S(2)}) collective-permute-start(bf16[256,576]{0,1:T(8,128)(2,1)} %multiply_convert_fusion.8), channel_id=1, source_target_pairs={{0,8},{8,0},{16,24},{24,16},{32,40},{40,32},{48,56},{56,48},{64,72... | collective-permute-start | bytes 884744 | tf_op jit(solution)/shard_map/ppermute | solution.py:37
  111.7 9.8 %collective-permute-start.4 = (bf16[576,768]{1,0:T(8,128)(2,1)}, bf16[576,768]{1,0:T(8,128)(2,1)}, u32[]{:S(2)}, u32[]{:S(2)}) collective-permute-start(bf16[576,768]{1,0:T(8,128)(2,1)} %bitcast.17), channel_id=1, source_target_pairs={{0,8},{8,0},{16,24},{24,16},{32,40},{40,32},{48,56},{56,48},{64,72... | collective-permute-start | bytes 2654216 | tf_op jit(solution)/shard_map/ppermute | solution.py:37
  118.5 1.7 collective-permute-start.3
  119.7 338.3 %reduce-scatter.4.cloned.1.call-start = ((), (), s32[]{:S(2)}) async-start(), calls=%async_computation.10 | async-start | bytes 3483648
  148.9 5.2 %collective-permute-start.5 = (bf16[8,2,3,64,256]{4,3,2,1,0:T(8,128)(2,1)S(1)}, bf16[8,2,3,64,256]{4,3,2,1,0:T(8,128)(2,1)S(1)}, u32[]{:S(2)}, u32[]{:S(2)}) collective-permute-start(bf16[8,2,3,64,256]{4,3,2,1,0:T(8,128)(2,1)S(1)} %all_to_all.35.own_ref), channel_id=1, source_target_pairs={{0,8},{8,0},{16,24},{24,16},{32,40},{40,32},{48,56},{56,48},{64,72... | collective-permute-start | bytes 4718600 | tf_op jit(solution)/shard_map/ppermute | solution.py:37
  196.7 7.1 %collective-permute-start.6 = (bf16[256,576]{0,1:T(8,128)(2,1)}, bf16[256,576]{0,1:T(8,128)(2,1)}, u32[]{:S(2)}, u32[]{:S(2)}) collective-permute-start(bf16[256,576]{0,1:T(8,128)(2,1)} %multiply_convert_fusion.6), channel_id=1, source_target_pairs={{0,8},{8,0},{16,24},{24,16},{32,40},{40,32},{48,56},{56,48},{64,72... | collective-permute-start | bytes 884744 | tf_op jit(solution)/shard_map/ppermute | solution.py:37
  198.0 9.0 %collective-permute-start.8 = (bf16[256,576]{0,1:T(8,128)(2,1)}, bf16[256,576]{0,1:T(8,128)(2,1)}, u32[]{:S(2)}, u32[]{:S(2)}) collective-permute-start(bf16[256,576]{0,1:T(8,128)(2,1)} %bitcast.24), channel_id=1, source_target_pairs={{0,8},{8,0},{16,24},{24,16},{32,40},{40,32},{48,56},{56,48},{64,72... | collective-permute-start | bytes 884744 | tf_op jit(solution)/shard_map/ppermute | solution.py:37
  210.7 1.7 collective-permute-start.9
  212.0 1.7 collective-permute-start.7
  239.2 3.5 collective-permute-start.10
  271.5 3.7 collective-permute-start.11
  280.9 3.5 collective-permute-start.12
  286.7 23.9 %copy-start.35 = (bf16[9,64,256]{2,1,0:T(8,128)(2,1)S(1)}, bf16[9,64,256]{2,1,0:T(8,128)(2,1)}, u32[]{:S(2)}) copy-start(bf16[9,64,256]{2,1,0:T(8,128)(2,1)} %copy-done.34) | copy-start | bytes 884740
  286.7 23.9 %copy-start.42 = (bf16[256,576]{0,1:T(8,128)(2,1)S(1)}, bf16[256,576]{0,1:T(8,128)(2,1)}, u32[]{:S(2)}) copy-start(bf16[256,576]{0,1:T(8,128)(2,1)} %copy-done.41) | copy-start | bytes 884740
  310.2 16.8 %collective-permute-start.13 = (bf16[8,2,3,64,256]{4,3,2,1,0:T(8,128)(2,1)}, bf16[8,2,3,64,256]{4,3,2,1,0:T(8,128)(2,1)}, u32[]{:S(2)}, u32[]{:S(2)}) collective-permute-start(bf16[8,2,3,64,256]{4,3,2,1,0:T(8,128)(2,1)} %get-tuple-element.60), channel_id=1, source_target_pairs={{0,8},{8,0},{16,24},{24,16},{32,40},{40,32},{48,56},{56,48},{64,72... | collective-permute-start | bytes 4718600 | tf_op jit(solution)/shard_map/ppermute | solution.py:37
  311.9 10.4 %collective-permute-start.28 = (bf16[576,288]{0,1:T(8,128)(2,1)}, bf16[576,288]{0,1:T(8,128)(2,1)}, u32[]{:S(2)}, u32[]{:S(2)}) collective-permute-start(bf16[576,288]{0,1:T(8,128)(2,1)} %broadcast_select_fusion.5), channel_id=1, source_target_pairs={{0,8},{8,0},{16,24},{24,16},{32,40},{40,32},{48,56},{56,48},{64,72... | collective-permute-start | bytes 995336 | tf_op jit(solution)/shard_map/ppermute | solution.py:37
  331.6 8.2 %collective-permute-start.19 = (bf16[576,288]{0,1:T(8,128)(2,1)}, bf16[576,288]{0,1:T(8,128)(2,1)}, u32[]{:S(2)}, u32[]{:S(2)}) collective-permute-start(bf16[576,288]{0,1:T(8,128)(2,1)} %broadcast_select_fusion.6), channel_id=1, source_target_pairs={{0,8},{8,0},{16,24},{24,16},{32,40},{40,32},{48,56},{56,48},{64,72... | collective-permute-start | bytes 995336 | tf_op jit(solution)/shard_map/ppermute | solution.py:37
  342.9 21.1 %collective-permute-start.20 = (bf16[2,72,2592]{2,1,0:T(8,128)(2,1)S(1)}, bf16[2,72,2592]{2,1,0:T(8,128)(2,1)}, u32[]{:S(2)}, u32[]{:S(2)}) collective-permute-start(bf16[2,72,2592]{2,1,0:T(8,128)(2,1)S(1)} %get-tuple-element.65), channel_id=1, source_target_pairs={{0,1},{1,0},{2,3},{3,2},{4,5},{5,4},{6,7},{7,6},{8,9},{9,8},{10,11... | collective-permute-start | bytes 2239496 | tf_op jit(solution)/shard_map/ppermute | solution.py:296
  343.9 41.4 %collective-permute-start.21 = (bf16[2,72,2592]{2,1,0:T(8,128)(2,1)S(1)}, bf16[2,72,2592]{2,1,0:T(8,128)(2,1)}, u32[]{:S(2)}, u32[]{:S(2)}) collective-permute-start(bf16[2,72,2592]{2,1,0:T(8,128)(2,1)S(1)} %get-tuple-element.66), channel_id=1, source_target_pairs={{0,2},{1,3},{2,0},{3,1},{4,6},{5,7},{6,4},{7,5},{8,10},{9,11},{10,... | collective-permute-start | bytes 2239496 | tf_op jit(solution)/shard_map/ppermute | solution.py:296
  346.4 39.0 %collective-permute-start.22 = (bf16[2,72,2592]{2,1,0:T(8,128)(2,1)S(1)}, bf16[2,72,2592]{2,1,0:T(8,128)(2,1)}, u32[]{:S(2)}, u32[]{:S(2)}) collective-permute-start(bf16[2,72,2592]{2,1,0:T(8,128)(2,1)S(1)} %get-tuple-element.67), channel_id=1, source_target_pairs={{0,3},{1,2},{2,1},{3,0},{4,7},{5,6},{6,5},{7,4},{8,11},{9,10},{10,... | collective-permute-start | bytes 2239496 | tf_op jit(solution)/shard_map/ppermute | solution.py:296
  349.4 40.3 %all-to-all-start.5 = ((bf16[8,2,3,64,256]{4,3,2,1,0:T(8,128)(2,1)}), bf16[8,2,3,64,256]{4,3,2,1,0:T(8,128)(2,1)}, u32[]{:S(2)}, u32[]{:S(2)}) async-start(bf16[8,2,3,64,256]{4,3,2,1,0:T(8,128)(2,1)} %add_convert_fusion), calls=%async_computation.5 | async-start | bytes 3145728 | tf_op jit(solution)/shard_map/all_to_all | solution.py:41
  388.1 15.9 %collective-permute-start.23 = (bf16[72,2592]{1,0:T(8,128)(2,1)}, bf16[72,2592]{1,0:T(8,128)(2,1)}, u32[]{:S(2)}, u32[]{:S(2)}) collective-permute-start(bf16[72,2592]{1,0:T(8,128)(2,1)} %fusion.47), channel_id=1, source_target_pairs={{0,4},{1,5},{2,6},{3,7},{4,0},{5,1},{6,2},{7,3},{8,12},{9,13},{10,... | collective-permute-start | bytes 1119752 | tf_op jit(solution)/shard_map/ppermute | solution.py:296
  397.5 8.1 %collective-permute-start.14 = (bf16[576,960]{1,0:T(8,128)(2,1)}, bf16[576,960]{1,0:T(8,128)(2,1)}, u32[]{:S(2)}, u32[]{:S(2)}) collective-permute-start(bf16[576,960]{1,0:T(8,128)(2,1)} %get-tuple-element.145), channel_id=1, source_target_pairs={{0,8},{8,0},{16,24},{24,16},{32,40},{40,32},{48,56},{56,48},{64,72... | collective-permute-start | bytes 3317768 | tf_op jit(solution)/shard_map/ppermute | solution.py:37
  405.0 53.3 %collective-permute-start.24 = (bf16[72,2592]{1,0:T(8,128)(2,1)S(1)}, bf16[72,2592]{1,0:T(8,128)(2,1)S(1)}, u32[]{:S(2)}, u32[]{:S(2)}) collective-permute-start(bf16[72,2592]{1,0:T(8,128)(2,1)S(1)} %fusion.11), channel_id=1, source_target_pairs={{0,16},{8,24},{16,0},{24,8},{32,48},{40,56},{48,32},{56,40},{64,80... | collective-permute-start | bytes 1119752 | tf_op jit(solution)/shard_map/ppermute | solution.py:63
  408.8 59.6 %all-to-all-start.6 = ((bf16[8,72,964]{2,1,0:T(8,128)(2,1)}), bf16[8,72,964]{2,1,0:T(8,128)(2,1)S(1)}, u32[]{:S(2)}, u32[]{:S(2)}) async-start(bf16[8,72,964]{2,1,0:T(8,128)(2,1)} %bitcast.38), calls=%async_computation.6 | async-start | bytes 2359296 | tf_op jit(solution)/shard_map/all_to_all | solution.py:45
  457.9 8.1 %collective-permute-start.29 = (bf16[72,2592]{1,0:T(8,128)(2,1)}, bf16[72,2592]{1,0:T(8,128)(2,1)S(1)}, u32[]{:S(2)}, u32[]{:S(2)}) collective-permute-start(bf16[72,2592]{1,0:T(8,128)(2,1)} %reduce-scatter.4.cloned.1.call-done), channel_id=1, source_target_pairs={{0,16},{8,24},{16,0},{24,8},{32,48},{40,56},{48,32},{56,40},{64,80... | collective-permute-start | bytes 1119752 | tf_op jit(solution)/shard_map/ppermute | solution.py:63
  458.5 10.7 %collective-permute-start.25 = (bf16[72,2592]{1,0:T(8,128)(2,1)S(1)}, bf16[72,2592]{1,0:T(8,128)(2,1)S(1)}, u32[]{:S(2)}, u32[]{:S(2)}) collective-permute-start(bf16[72,2592]{1,0:T(8,128)(2,1)S(1)} %add_convert_fusion.8), channel_id=1, source_target_pairs={{0,32},{8,40},{16,48},{24,56},{32,0},{40,8},{48,16},{56,24},{64,96... | collective-permute-start | bytes 1119752 | tf_op jit(solution)/shard_map/ppermute | solution.py:63
  467.1 7.1 %collective-permute-start.30 = (bf16[72,2592]{1,0:T(8,128)(2,1)S(1)}, bf16[72,2592]{1,0:T(8,128)(2,1)S(1)}, u32[]{:S(2)}, u32[]{:S(2)}) collective-permute-start(bf16[72,2592]{1,0:T(8,128)(2,1)S(1)} %add_convert_fusion.5), channel_id=1, source_target_pairs={{0,32},{8,40},{16,48},{24,56},{32,0},{40,8},{48,16},{56,24},{64,96... | collective-permute-start | bytes 1119752 | tf_op jit(solution)/shard_map/ppermute | solution.py:63
  468.6 4.1 collective-permute-start.15
  469.3 19.3 %collective-permute-start.26 = (bf16[72,2592]{1,0:T(8,128)(2,1)S(1)}, bf16[72,2592]{1,0:T(8,128)(2,1)S(1)}, u32[]{:S(2)}, u32[]{:S(2)}) collective-permute-start(bf16[72,2592]{1,0:T(8,128)(2,1)S(1)} %add_convert_fusion.7), channel_id=1, source_target_pairs={{0,64},{8,72},{16,80},{24,88},{32,96},{40,104},{48,112},{56,120},{... | collective-permute-start | bytes 1119752 | tf_op jit(solution)/shard_map/ppermute | solution.py:63
  472.7 12.9 %collective-permute-start.16 = (bf16[72,964]{1,0:T(8,128)(2,1)S(1)}, bf16[72,964]{1,0:T(8,128)(2,1)S(1)}, u32[]{:S(2)}, u32[]{:S(2)}) collective-permute-start(bf16[72,964]{1,0:T(8,128)(2,1)S(1)} %add_convert_fusion.14), channel_id=1, source_target_pairs={{0,32},{8,40},{16,48},{24,56},{32,0},{40,8},{48,16},{56,24},{64,96... | collective-permute-start | bytes 416456 | tf_op jit(solution)/shard_map/ppermute | solution.py:63
  474.3 29.5 %collective-permute-start.31 = (bf16[72,2592]{1,0:T(8,128)(2,1)S(1)}, bf16[72,2592]{1,0:T(8,128)(2,1)S(1)}, u32[]{:S(2)}, u32[]{:S(2)}) collective-permute-start(bf16[72,2592]{1,0:T(8,128)(2,1)S(1)} %add_convert_fusion.4), channel_id=1, source_target_pairs={{0,64},{8,72},{16,80},{24,88},{32,96},{40,104},{48,112},{56,120},{... | collective-permute-start | bytes 1119752 | tf_op jit(solution)/shard_map/ppermute | solution.py:63
  485.7 13.6 %collective-permute-start.17 = (bf16[72,964]{1,0:T(8,128)(2,1)S(1)}, bf16[72,964]{1,0:T(8,128)(2,1)S(1)}, u32[]{:S(2)}, u32[]{:S(2)}) collective-permute-start(bf16[72,964]{1,0:T(8,128)(2,1)S(1)} %add_convert_fusion.13), channel_id=1, source_target_pairs={{0,64},{8,72},{16,80},{24,88},{32,96},{40,104},{48,112},{56,120},{... | collective-permute-start | bytes 416456 | tf_op jit(solution)/shard_map/ppermute | solution.py:63
  488.7 15.4 %collective-permute-start.27 = (bf16[72,2592]{1,0:T(8,128)(2,1)S(1)}, bf16[72,2592]{1,0:T(8,128)(2,1)S(1)}, u32[]{:S(2)}, u32[]{:S(2)}) collective-permute-start(bf16[72,2592]{1,0:T(8,128)(2,1)S(1)} %add_convert_fusion.6.refs_0_), channel_id=1, source_target_pairs={{0,8},{8,0},{16,24},{24,16},{32,40},{40,32},{48,56},{56,48},{64,72... | collective-permute-start | bytes 1119752 | tf_op jit(solution)/shard_map/ppermute | solution.py:37
  499.3 5.5 %collective-permute-start.18 = (bf16[72,964]{1,0:T(8,128)(2,1)S(1)}, bf16[72,964]{1,0:T(8,128)(2,1)S(1)}, u32[]{:S(2)}, u32[]{:S(2)}) collective-permute-start(bf16[72,964]{1,0:T(8,128)(2,1)S(1)} %add_convert_fusion.12.refs_4_), channel_id=1, source_target_pairs={{0,8},{8,0},{16,24},{24,16},{32,40},{40,32},{48,56},{56,48},{64,72... | collective-permute-start | bytes 416456 | tf_op jit(solution)/shard_map/ppermute | solution.py:37
  504.0 1.8 collective-permute-start.32
  (74 other events, 147.8 us)
Sparse Core Ops, SparseCore 0:
  26.3 71.7 all-gather.2
  119.8 71.7 all-gather.4
  348.8 109.0 reduce-scatter.3

commit v5 on v4

--- a/solution.py
+++ b/solution.py
@@ -391,11 +391,12 @@
     gain_cols = jnp.transpose(norm_gains.reshape(2 * LAYERS, SHARD))
     cut = (Q_ROWS + KV_ROWS + D) // 2
 
-    def mlp_pack(layer):
+    def wgu_pack(layer):
         wgu = w_gate_up[layer].reshape(SHARD, 2, FSDP, 2, UNITS)
-        wgu = my_half(wgu[..., 0, :], wgu[..., 1, :]).reshape(SHARD, FF)
-        wdown = my_half(w_down[layer, :UNITS], w_down[layer, UNITS:]).reshape(SHARD, HALF)
-        return jnp.concatenate([wgu, wdown], 1)
+        return my_half(wgu[..., 0, :], wgu[..., 1, :]).reshape(SHARD, FF)
+
+    def wd_pack(layer):
+        return my_half(w_down[layer, :UNITS], w_down[layer, UNITS:]).reshape(SHARD, HALF)
 
     def proj_pack(layer):
         proj = jnp.concatenate([w_qkv[layer], w_out[layer]], 1)
@@ -405,15 +406,13 @@
     first = jnp.broadcast_to(first[None], (FSDP,) + first.shape)
     first, w_gate_up, w_down = lax.optimization_barrier((first, w_gate_up, w_down))
     first = over_fsdp(first).reshape(D, -1)
-    pack0 = lax.all_gather(mlp_pack(0), "fsdp", axis=0, tiled=True)
-    pack1 = lax.all_gather(mlp_pack(1), "fsdp", axis=0, tiled=True)
+    pack0 = jnp.concatenate([wgu_pack(0), wd_pack(0), wd_pack(1)], 1)
+    pack0 = lax.all_gather(pack0, "fsdp", axis=0, tiled=True)
+    pack1 = lax.all_gather(wgu_pack(1), "fsdp", axis=0, tiled=True)
     gains = jnp.transpose(first[:, cut:].astype(F32)).reshape(LAYERS, 2, D)
 
     def whole_proj(own):
         return jnp.concatenate(in_order(own, to_partner(own)), 1)
-
-    def mlp_weights(pack):
-        return pack[:, :FF], pack[:, FF:].reshape(HALF, D)
 
     projs, mlps = [whole_proj(first[:, :cut])], []
 
@@ -449,11 +448,11 @@
         o_t, lse = attention(scalars, q_t, kv_own, kv_other)
         if layer == 0:
             o_t, pack0, late = lax.optimization_barrier((o_t, pack0, late))
-            mlps.append(mlp_weights(pack0))
+            mlps.append((pack0[:, :FF], pack0[:, FF : FF + HALF].reshape(HALF, D)))
             projs.append(whole_proj(late))
         else:
             o_t, pack1 = lax.optimization_barrier((o_t, pack1))
-            mlps.append(mlp_weights(pack1))
+            mlps.append((pack1, pack0[:, FF + HALF :].reshape(HALF, D)))
         attn_out = o_t.astype(BF16).reshape(Q_ROWS, ROWS)
         mid = hidden + ein("at,ad->td", attn_out, wout)
         unit_m, rms_m = normed(mid)
@@ -500,12 +499,14 @@
         wout_theirs = my_half(d_wout[:, wout_half:], d_wout[:, :wout_half])
         d_mlp = [d_wgu, d_wdown.reshape(D, HALF), sum_pair(wout_mine, to_partner(wout_theirs))]
         d_mlp = jnp.concatenate(d_mlp, 1)
+        if layer == 0:
+            share1 = sum_chips(lax.optimization_barrier((share1, dkv))[0])
+        dkv = jnp.sum(over_chips(dkv).astype(F32), 0)
+        dkv, d_mlp = lax.optimization_barrier((dkv, d_mlp))
         if layer == 1:
             share1 = lax.psum_scatter(d_mlp, "fsdp", scatter_dimension=0, tiled=True)
         else:
             share0 = scatter_by_permutes(me, d_mlp)
-            share1 = sum_chips(lax.optimization_barrier((share1, dkv))[0])
-        dkv = jnp.sum(over_chips(dkv).astype(F32), 0)
         turned = jnp.concatenate([dq_t, dkv[0]], 0)
         d_qkv = jnp.concatenate([rotate(turned, cosine, -sine), dkv[1]], 0)
         d_qkv = d_qkv.astype(BF16).reshape(Q_ROWS + KV_ROWS, ROWS)

time: 523 us -> 500 us (0.956)
  blocking collectives: 47.7 us -> 26.2 us
  waiting for transfers between devices: 155 us -> 166 us
  matrix products: 40.4 us -> 33.3 us
  starting transfers between devices: 73.2 us -> 67.4 us
    optimization_barrier x1, waiting for transfers between devices: 45.3 us -> 0.02 us  [local(): share1 = sum_chips(lax.optimization_barrier((share1, dkv))[0])]
    all_to_all x3, waiting for transfers between devices: 8.16 us -> 32 us  [over_fsdp(): return lax.all_to_all(x, 'fsdp', 0, 0, tiled=True)]
    all_to_all x2 -> x3, waiting for transfers between devices: 23.4 us -> 47 us  [over_chips(): lax.all_to_all(x, 'ctx', 0, 0, axis_index_groups=SAME_CORE, tiled=True)]
    all_to_all x2 -> x1, blocking collectives: 47.7 us -> 26.2 us  [over_chips(): lax.all_to_all(x, 'ctx', 0, 0, axis_index_groups=SAME_CORE, tiled=True)]
    ppermute x9, waiting for transfers between devices: 18.4 us -> 28.6 us  [sum_chips(): x = sum_pair(x, lax.ppermute(x, 'ctx', [(i, i ^ bit) for i in range(CTX)]))]
    dot_general x18, matrix products: 31.7 us -> 24.9 us  [ein(): return jnp.einsum(spec, a, b, preferred_element_type=F32)]
    ppermute x20, starting transfers between devices: 28.6 us -> 22.8 us  [to_partner(): return lax.ppermute(x, 'ctx', PARTNER)]
    all_to_all x2 -> x3, starting transfers between devices: 8.99 us -> 13.6 us  [over_chips(): lax.all_to_all(x, 'ctx', 0, 0, axis_index_groups=SAME_CORE, tiled=True)]
  transfers between devices with their start and end apart: 41 -> 42, of which waited for: 18 -> 24; matrix products, arithmetic and copies ran while one was open for 17% -> 17% of each run, Pallas kernels for 6% -> 7%
where the time goes in v5:
time: 500 us; the launch traced here: 490 us
  waiting for transfers between devices  166 us (33%)
  Pallas kernels  79.2 us (16%)
  starting transfers between devices  67.4 us (13%)
  local copies, waits for them, and re-layouts  51 us (10%)
  other arithmetic  49 us (10%)
  matrix products  33.3 us (7%)
  blocking collectives  26.2 us (5%)
  between operations  18.4 us (4%)
    all_to_all x3, waiting for transfers between devices, over_chips(): lax.all_to_all(x, 'ctx', 0, 0, axis_index_groups=SAME_CORE, tiled=True)  47 us
    pallas_call x2, Pallas kernels, attention_back(): pl.pallas_call(backward_kernel, grid_spec=pltpu.PrefetchScalarGridSpec(nu...  44.6 us
    ppermute x4, waiting for transfers between devices, across(): return lax.ppermute(x, 'fsdp', [(i, i ^ d) for i in range(FSDP)])  34.8 us
    all_to_all x3, waiting for transfers between devices, over_fsdp(): return lax.all_to_all(x, 'fsdp', 0, 0, tiled=True)  32 us
    pallas_call x2, Pallas kernels, attention(): pl.pallas_call(forward_kernel, grid_spec=pltpu.PrefetchScalarGridSpec(num...  30.9 us
    ppermute x9, waiting for transfers between devices, sum_chips(): x = sum_pair(x, lax.ppermute(x, 'ctx', [(i, i ^ bit) for i in range(CTX)]))  28.6 us
    all_to_all x1, blocking collectives, over_chips(): lax.all_to_all(x, 'ctx', 0, 0, axis_index_groups=SAME_CORE, tiled=True)  26.2 us
    dot_general x18, matrix products, ein(): return jnp.einsum(spec, a, b, preferred_element_type=F32)  24.9 us
  transfers between devices with their start and end apart: 42, of which 24 were waited for; matrix products, arithmetic and copies ran while one was open for 17% of the time, Pallas kernels for 7%

profile of v5, /device:TPU:1, one launch (start us, length us, event | category | flops | bytes accessed | tf_op | source)
XLA Modules:
  0.0 490.3 jit_solution(5781884128618400294)
XLA Ops:
  15.8 8.2 %all-to-all-start = ((bf16[8,72,772]{2,1,0:T(8,128)(2,1)}), bf16[8,72,772]{2,1,0:T(8,128)(2,1)S(1)}, u32[]{:S(2)}, u32[]{:S(2)}) async-start(bf16[8,72,772]{2,1,0:T(8,128)(2,1)} %broadcast_in_dim.16), calls=%async_computation | async-start | bytes 2064384 | tf_op jit(solution)/shard_map/all_to_all | solution.py:45
  25.9 19.1 %all-to-all-done = bf16[8,72,772]{2,1,0:T(8,128)(2,1)S(1)} async-done(((bf16[8,72,772]{2,1,0:T(8,128)(2,1)}), bf16[8,72,772]{2,1,0:T(8,128)(2,1)S(1)}, u32[]{:S(2)}, u32[]{:S(2)}) %all-to-all-start) | async-done | bytes 889376 | tf_op jit(solution)/shard_map/all_to_all | solution.py:45
  52.7 4.8 all-to-all-start.1
  57.6 23.4 %all-to-all-done.1.own_ref = bf16[8,2,3,64,256]{4,3,2,1,0:T(8,128)(2,1)S(1)} async-done(((bf16[8,2,3,64,256]{4,3,2,1,0:T(8,128)(2,1)}), bf16[8,2,3,64,256]{4,3,2,1,0:T(8,128)(2,1)S(1)}, u32[]{:S(2)}, u32[]{:S(2)}) %all-to-all-start.1) | async-done | bytes 1572896 | tf_op jit(solution)/shard_map/all_to_all | solution.py:41
  83.3 4.2 all-to-all-start.2
  91.0 15.5 %attention.2 = (f32[9,64,256]{2,1,0:T(8,128)S(1)}, f32[3,2,1,384]{3,2,1,0:T(1,128)S(1)}) custom-call(s32[39]{0:T(128)S(1)} %concatenate.90.sc, bf16[9,64,256]{2,1,0:T(8,128)(2,1)S(1)} %fusion.33.q_ref, bf16[8,2,3,64,256]{4,3,2,1,0:T(8,128)(2,1)S(1)} %all-to-all-done.1.own_ref, bf16[8,2,3,64,256]{4,3,2,1,0:T(8,128)(2,1)S(1)} %collective-permute-done.1.other_ref), custom_call_target="tpu_custom_call" | custom-call | tf_op jit(solution)/shard_map/attention/pallas_call | solution.py:225
  107.3 6.7 %all-gather.3.cloned.1.call-done = bf16[576,3072]{1,0:T(8,128)(2,1)} async-done(((bf16[72,3072]{1,0:T(8,128)(2,1)}), bf16[576,3072]{1,0:T(8,128)(2,1)}) %all-gather.3.cloned.1.call-update) | async-done | bytes 3538960 | tf_op jit(solution)/shard_map/all_gather | solution.py:410
  115.2 2.3 multiply_reduce_fusion.8
  120.1 2.8 fusion.77
  122.8 3.4 reshape.319
  126.2 3.1 fusion.4
  141.5 26.2 %all_to_all.35.own_ref = bf16[8,2,3,64,256]{4,3,2,1,0:T(8,128)(2,1)S(1)} all-to-all(bf16[8,2,3,64,256]{4,3,2,1,0:T(8,128)(2,1)S(1)} %broadcast_in_dim.21), channel_id=1, replica_groups={{0,16,32,48,64,80,96,112},{8,24,40,56,72,88,104,120},{1,17,33,49,65,81,..., dimensions={0} | all-to-all | bytes 3145728 | tf_op jit(solution)/shard_map/all_to_all | solution.py:41
  168.6 3.0 collective-permute-done.5.other_ref
  171.6 15.5 %attention.3 = (f32[9,64,256]{2,1,0:T(8,128)S(1)}, f32[3,2,1,384]{3,2,1,0:T(1,128)S(1)}) custom-call(s32[39]{0:T(128)S(1)} %concatenate.90.sc, bf16[9,64,256]{2,1,0:T(8,128)(2,1)S(1)} %fusion.30.q_ref, bf16[8,2,3,64,256]{4,3,2,1,0:T(8,128)(2,1)S(1)} %all_to_all.35.own_ref, bf16[8,2,3,64,256]{4,3,2,1,0:T(8,128)(2,1)S(1)} %collective-permute-done.5.other_ref), custom_call_target="tpu_custom_call" | custom-call | tf_op jit(solution)/shard_map/attention/pallas_call | solution.py:225
  189.7 10.1 %all-gather.5.cloned.1.call-done = bf16[576,1536]{1,0:T(8,128)(2,1)} async-done(((bf16[72,1536]{1,0:T(8,128)(2,1)}), bf16[576,1536]{1,0:T(8,128)(2,1)}) %all-gather.5.cloned.1.call-update) | async-done | bytes 1769488 | tf_op jit(solution)/shard_map/all_gather | solution.py:411
  200.9 2.4 multiply_reduce_fusion.6
  205.0 2.3 collective-permute-start.6
  207.3 3.4 reshape.321
  210.7 3.1 fusion.71
  213.9 2.5 multiply_convert_fusion.3
  220.7 2.3 fusion.75
  224.5 22.0 %attention_back.2 = (f32[9,64,256]{2,1,0:T(8,128)S(1)}, bf16[8,2,3,64,256]{4,3,2,1,0:T(8,128)(2,1)S(1)}, bf16[8,2,3,64,256]{4,3,2,1,0:T(8,128)(2,1)S(1)}) custom-call(s32[39]{0:T(128)S(1)} %concatenate.90.sc, bf16[9,64,256]{2,1,0:T(8,128)(2,1)S(1)} %copy-done.5, bf16[8,2,3,64,256]{4,3,2,1,0:T(8,128)(2,1)S(1)} %all_to_all.35.own_ref, ...), custom_call_target="tpu_custom_call" | custom-call | tf_op jit(solution)/shard_map/attention_back/pallas_call | solution.py:248
  251.8 4.4 all-to-all-start.4
  261.1 2.5 reshape.324
  263.6 2.7 convolution_convert_fusion.1
  269.5 10.3 %all-to-all-done.4 = bf16[8,2,3,64,256]{4,3,2,1,0:T(8,128)(2,1)} async-done(((bf16[8,2,3,64,256]{4,3,2,1,0:T(8,128)(2,1)}), bf16[8,2,3,64,256]{4,3,2,1,0:T(8,128)(2,1)}, u32[]{:S(2)}, u32[]{:S(2)}) %all-to-all-start.4) | async-done | bytes 1572896 | tf_op jit(solution)/shard_map/all_to_all | solution.py:41
  294.0 22.7 %attention_back.3 = (f32[9,64,256]{2,1,0:T(8,128)S(1)}, bf16[8,2,3,64,256]{4,3,2,1,0:T(8,128)(2,1)S(1)}, bf16[8,2,3,64,256]{4,3,2,1,0:T(8,128)(2,1)}) custom-call(s32[39]{0:T(128)S(1)} %concatenate.90.sc, bf16[9,64,256]{2,1,0:T(8,128)(2,1)S(1)} %fusion.33.q_ref, bf16[8,2,3,64,256]{4,3,2,1,0:T(8,128)(2,1)S(1)} %all-to-all-done.1.own_ref, ...), custom_call_target="tpu_custom_call" | custom-call | tf_op jit(solution)/shard_map/attention_back/pallas_call | solution.py:248
  319.9 2.6 pad_maximum_fusion.3
  324.3 4.4 all-to-all-start.5
  333.7 2.2 reshape.326
  336.0 2.1 convolution_convert_fusion
  339.8 13.3 %all-to-all-done.5 = bf16[8,2,3,64,256]{4,3,2,1,0:T(8,128)(2,1)} async-done(((bf16[8,2,3,64,256]{4,3,2,1,0:T(8,128)(2,1)}), bf16[8,2,3,64,256]{4,3,2,1,0:T(8,128)(2,1)}, u32[]{:S(2)}, u32[]{:S(2)}) %all-to-all-start.5) | async-done | bytes 1572896 | tf_op jit(solution)/shard_map/all_to_all | solution.py:41
  361.4 2.4 collective-permute-start.22
  368.5 12.1 %collective-permute-done.21 = bf16[2,72,2592]{2,1,0:T(8,128)(2,1)} collective-permute-done((bf16[2,72,2592]{2,1,0:T(8,128)(2,1)}, bf16[2,72,2592]{2,1,0:T(8,128)(2,1)}, u32[]{:S(2)}, u32[]{:S(2)}) %collective-permute-start.21) | collective-permute-done | bytes 746528 | tf_op jit(solution)/shard_map/ppermute | solution.py:296
  380.6 19.1 %collective-permute-done.22 = bf16[2,72,2592]{2,1,0:T(8,128)(2,1)} collective-permute-done((bf16[2,72,2592]{2,1,0:T(8,128)(2,1)}, bf16[2,72,2592]{2,1,0:T(8,128)(2,1)}, u32[]{:S(2)}, u32[]{:S(2)}) %collective-permute-start.22) | collective-permute-done | bytes 746528 | tf_op jit(solution)/shard_map/ppermute | solution.py:296
  405.9 4.4 all-to-all-start.6
  410.3 2.3 collective-permute-done.24
  415.3 12.9 %all-to-all-done.6 = bf16[8,72,964]{2,1,0:T(8,128)(2,1)S(1)} async-done(((bf16[8,72,964]{2,1,0:T(8,128)(2,1)}), bf16[8,72,964]{2,1,0:T(8,128)(2,1)S(1)}, u32[]{:S(2)}, u32[]{:S(2)}) %all-to-all-start.6) | async-done | bytes 1110560 | tf_op jit(solution)/shard_map/all_to_all | solution.py:45
  430.0 2.4 collective-permute-done.25
  436.5 7.3 %collective-permute-done.29 = bf16[72,2592]{1,0:T(8,128)(2,1)S(1)} collective-permute-done((bf16[72,2592]{1,0:T(8,128)(2,1)}, bf16[72,2592]{1,0:T(8,128)(2,1)S(1)}, u32[]{:S(2)}, u32[]{:S(2)}) %collective-permute-start.29) | collective-permute-done | bytes 373280 | tf_op jit(solution)/shard_map/ppermute | solution.py:63
  445.0 2.7 collective-permute-start.27
  448.2 5.9 %collective-permute-done.30 = bf16[72,2592]{1,0:T(8,128)(2,1)S(1)} collective-permute-done((bf16[72,2592]{1,0:T(8,128)(2,1)S(1)}, bf16[72,2592]{1,0:T(8,128)(2,1)S(1)}, u32[]{:S(2)}, u32[]{:S(2)}) %collective-permute-start.30) | collective-permute-done | bytes 373280 | tf_op jit(solution)/shard_map/ppermute | solution.py:63
  454.1 2.5 collective-permute-start.31
  456.6 7.9 %collective-permute-done.27 = bf16[72,2592]{1,0:T(8,128)(2,1)S(1)} collective-permute-done((bf16[72,2592]{1,0:T(8,128)(2,1)S(1)}, bf16[72,2592]{1,0:T(8,128)(2,1)S(1)}, u32[]{:S(2)}, u32[]{:S(2)}) %collective-permute-start.27) | collective-permute-done | bytes 373280 | tf_op jit(solution)/shard_map/ppermute | solution.py:63
  464.6 4.2 collective-permute-start.28
  468.8 3.0 collective-permute-start.20
  471.8 4.1 collective-permute-done.31
  476.0 2.3 collective-permute-start.32
  (389 shorter events, 123.2 us)
Async XLA Ops:
  7.2 106.9 %all-gather.3.cloned.1.call-start = ((), (), s32[]{:S(2)}) async-start(), calls=%async_computation.8 | async-start | bytes 3981312 | tf_op jit(solution)/shard_map/all_gather | solution.py:410
  15.8 29.3 %all-to-all-start = ((bf16[8,72,772]{2,1,0:T(8,128)(2,1)}), bf16[8,72,772]{2,1,0:T(8,128)(2,1)S(1)}, u32[]{:S(2)}, u32[]{:S(2)}) async-start(bf16[8,72,772]{2,1,0:T(8,128)(2,1)} %broadcast_in_dim.16), calls=%async_computation | async-start | bytes 2064384 | tf_op jit(solution)/shard_map/all_to_all | solution.py:45
  45.2 3.1 collective-permute-start
  52.7 28.3 %all-to-all-start.1 = ((bf16[8,2,3,64,256]{4,3,2,1,0:T(8,128)(2,1)}), bf16[8,2,3,64,256]{4,3,2,1,0:T(8,128)(2,1)S(1)}, u32[]{:S(2)}, u32[]{:S(2)}) async-start(bf16[8,2,3,64,256]{4,3,2,1,0:T(8,128)(2,1)} %broadcast_in_dim.19), calls=%async_computation.1 | async-start | bytes 3145728 | tf_op jit(solution)/shard_map/all_to_all | solution.py:41
  57.5 32.1 %copy-start.80 = (s32[1,4096]{1,0:T(1,128)S(1)}, s32[1,4096]{1,0:T(1,128)}, u32[]{:S(2)}) copy-start(s32[1,4096]{1,0:T(1,128)} %param.11) | copy-start | bytes 49156
  57.5 32.3 %copy-start.87 = (s32[32]{0:T(128)S(1)}, s32[32]{0:T(128)}, u32[]{:S(2)}) copy-start(s32[32]{0:T(128)} %param.10) | copy-start | bytes 388
  81.0 10.0 %collective-permute-start.1 = (bf16[8,2,3,64,256]{4,3,2,1,0:T(8,128)(2,1)S(1)}, bf16[8,2,3,64,256]{4,3,2,1,0:T(8,128)(2,1)S(1)}, u32[]{:S(2)}, u32[]{:S(2)}) collective-permute-start(bf16[8,2,3,64,256]{4,3,2,1,0:T(8,128)(2,1)S(1)} %all-to-all-done.1.own_ref), channel_id=1, source_target_pairs={{0,8},{8,0},{16,24},{24,16},{32,40},{40,32},{48,56},{56,48},{64,72... | collective-permute-start | bytes 4718600 | tf_op jit(solution)/shard_map/ppermute | solution.py:37
  83.3 24.0 %all-to-all-start.2 = ((bf16[8,72,768]{2,1,0:T(8,128)(2,1)}), bf16[8,72,768]{2,1,0:T(8,128)(2,1)}, u32[]{:S(2)}, u32[]{:S(2)}) async-start(bf16[8,72,768]{2,1,0:T(8,128)(2,1)} %broadcast_in_dim.20), calls=%async_computation.2 | async-start | bytes 1769472 | tf_op jit(solution)/shard_map/all_to_all | solution.py:45
  87.6 112.2 %all-gather.5.cloned.1.call-start = ((), (), s32[]{:S(2)}) async-start(), calls=%async_computation.9 | async-start | bytes 1990656 | tf_op jit(solution)/shard_map/all_gather | solution.py:411
  91.0 15.5 %copy-start = (bf16[8,2,3,64,256]{4,3,2,1,0:T(8,128)(2,1)}, bf16[8,2,3,64,256]{4,3,2,1,0:T(8,128)(2,1)S(1)}, u32[]{:S(2)}) copy-start(bf16[8,2,3,64,256]{4,3,2,1,0:T(8,128)(2,1)S(1)} %collective-permute-done.1.other_ref) | copy-start | bytes 4718596
  117.4 18.7 %copy-start.19 = (f32[256,576]{0,1:T(8,128)}, f32[256,576]{0,1:T(8,128)S(1)}, u32[]{:S(2)}) copy-start(f32[256,576]{0,1:T(8,128)S(1)} %get-tuple-element.150) | copy-start | bytes 1769476
  118.3 7.9 %collective-permute-start.2 = (bf16[256,576]{0,1:T(8,128)(2,1)}, bf16[256,576]{0,1:T(8,128)(2,1)}, u32[]{:S(2)}, u32[]{:S(2)}) collective-permute-start(bf16[256,576]{0,1:T(8,128)(2,1)} %multiply_convert_fusion.8), channel_id=1, source_target_pairs={{0,8},{8,0},{16,24},{24,16},{32,40},{40,32},{48,56},{56,48},{64,72... | collective-permute-start | bytes 884744 | tf_op jit(solution)/shard_map/ppermute | solution.py:37
  120.0 17.4 %collective-permute-start.4 = (bf16[576,768]{1,0:T(8,128)(2,1)}, bf16[576,768]{1,0:T(8,128)(2,1)}, u32[]{:S(2)}, u32[]{:S(2)}) collective-permute-start(bf16[576,768]{1,0:T(8,128)(2,1)} %bitcast.17), channel_id=1, source_target_pairs={{0,8},{8,0},{16,24},{24,16},{32,40},{40,32},{48,56},{56,48},{64,72... | collective-permute-start | bytes 2654216 | tf_op jit(solution)/shard_map/ppermute | solution.py:37
  133.7 2.4 collective-permute-start.3
  167.7 3.9 collective-permute-start.5
  205.0 5.7 %collective-permute-start.6 = (bf16[256,576]{0,1:T(8,128)(2,1)}, bf16[256,576]{0,1:T(8,128)(2,1)}, u32[]{:S(2)}, u32[]{:S(2)}) collective-permute-start(bf16[256,576]{0,1:T(8,128)(2,1)} %multiply_convert_fusion.6), channel_id=1, source_target_pairs={{0,8},{8,0},{16,24},{24,16},{32,40},{40,32},{48,56},{56,48},{64,72... | collective-permute-start | bytes 884744 | tf_op jit(solution)/shard_map/ppermute | solution.py:37
  207.3 6.6 %collective-permute-start.8 = (bf16[256,576]{0,1:T(8,128)(2,1)}, bf16[256,576]{0,1:T(8,128)(2,1)}, u32[]{:S(2)}, u32[]{:S(2)}) collective-permute-start(bf16[256,576]{0,1:T(8,128)(2,1)} %bitcast.24), channel_id=1, source_target_pairs={{0,8},{8,0},{16,24},{24,16},{32,40},{40,32},{48,56},{56,48},{64,72... | collective-permute-start | bytes 884744 | tf_op jit(solution)/shard_map/ppermute | solution.py:37
  217.5 1.8 collective-permute-start.9
  218.8 1.8 collective-permute-start.7
  246.5 3.5 collective-permute-start.10
  251.8 28.0 %all-to-all-start.4 = ((bf16[8,2,3,64,256]{4,3,2,1,0:T(8,128)(2,1)}), bf16[8,2,3,64,256]{4,3,2,1,0:T(8,128)(2,1)}, u32[]{:S(2)}, u32[]{:S(2)}) async-start(bf16[8,2,3,64,256]{4,3,2,1,0:T(8,128)(2,1)} %add_convert_fusion.1), calls=%async_computation.4 | async-start | bytes 3145728 | tf_op jit(solution)/shard_map/all_to_all | solution.py:41
  256.2 172.3 %reduce-scatter.4.cloned.1.call-start = ((), (), s32[]{:S(2)}) async-start(), calls=%async_computation.10 | async-start | bytes 3483648
  257.7 8.6 %collective-permute-start.11 = (bf16[576,288]{1,0:T(8,128)(2,1)}, bf16[576,288]{1,0:T(8,128)(2,1)}, u32[]{:S(2)}, u32[]{:S(2)}) collective-permute-start(bf16[576,288]{1,0:T(8,128)(2,1)} %broadcast_select_fusion.6), channel_id=1, source_target_pairs={{0,8},{8,0},{16,24},{24,16},{32,40},{40,32},{48,56},{56,48},{64,72... | collective-permute-start | bytes 995336 | tf_op jit(solution)/shard_map/ppermute | solution.py:37
  284.5 2.9 collective-permute-start.12
  289.9 1.7 collective-permute-start.13
  294.0 25.8 %copy-start.85 = (bf16[576]{0:T(1024)(128)(2,1)S(1)}, bf16[576]{0:T(1024)(128)(2,1)}, u32[]{:S(2)}) copy-start(bf16[576]{0:T(1024)(128)(2,1)} %get-tuple-element.92) | copy-start | bytes 3460
  317.5 5.0 %collective-permute-start.14 = (bf16[8,2,3,64,256]{4,3,2,1,0:T(8,128)(2,1)}, bf16[8,2,3,64,256]{4,3,2,1,0:T(8,128)(2,1)S(1)}, u32[]{:S(2)}, u32[]{:S(2)}) collective-permute-start(bf16[8,2,3,64,256]{4,3,2,1,0:T(8,128)(2,1)} %get-tuple-element.68), channel_id=1, source_target_pairs={{0,8},{8,0},{16,24},{24,16},{32,40},{40,32},{48,56},{56,48},{64,72... | collective-permute-start | bytes 4718600 | tf_op jit(solution)/shard_map/ppermute | solution.py:37
  324.3 28.9 %all-to-all-start.5 = ((bf16[8,2,3,64,256]{4,3,2,1,0:T(8,128)(2,1)}), bf16[8,2,3,64,256]{4,3,2,1,0:T(8,128)(2,1)}, u32[]{:S(2)}, u32[]{:S(2)}) async-start(bf16[8,2,3,64,256]{4,3,2,1,0:T(8,128)(2,1)} %add_convert_fusion), calls=%async_computation.5 | async-start | bytes 3145728 | tf_op jit(solution)/shard_map/all_to_all | solution.py:41
  330.2 8.0 %collective-permute-start.15 = (bf16[576,288]{1,0:T(8,128)(2,1)}, bf16[576,288]{1,0:T(8,128)(2,1)}, u32[]{:S(2)}, u32[]{:S(2)}) collective-permute-start(bf16[576,288]{1,0:T(8,128)(2,1)} %broadcast_select_fusion.5), channel_id=1, source_target_pairs={{0,8},{8,0},{16,24},{24,16},{32,40},{40,32},{48,56},{56,48},{64,72... | collective-permute-start | bytes 995336 | tf_op jit(solution)/shard_map/ppermute | solution.py:37
  360.3 20.2 %collective-permute-start.21 = (bf16[2,72,2592]{2,1,0:T(8,128)(2,1)}, bf16[2,72,2592]{2,1,0:T(8,128)(2,1)}, u32[]{:S(2)}, u32[]{:S(2)}) collective-permute-start(bf16[2,72,2592]{2,1,0:T(8,128)(2,1)} %get-tuple-element.75), channel_id=1, source_target_pairs={{0,1},{1,0},{2,3},{3,2},{4,5},{5,4},{6,7},{7,6},{8,9},{9,8},{10,11... | collective-permute-start | bytes 2239496 | tf_op jit(solution)/shard_map/ppermute | solution.py:296
  361.4 38.3 %collective-permute-start.22 = (bf16[2,72,2592]{2,1,0:T(8,128)(2,1)}, bf16[2,72,2592]{2,1,0:T(8,128)(2,1)}, u32[]{:S(2)}, u32[]{:S(2)}) collective-permute-start(bf16[2,72,2592]{2,1,0:T(8,128)(2,1)} %get-tuple-element.76), channel_id=1, source_target_pairs={{0,2},{1,3},{2,0},{3,1},{4,6},{5,7},{6,4},{7,5},{8,10},{9,11},{10,... | collective-permute-start | bytes 2239496 | tf_op jit(solution)/shard_map/ppermute | solution.py:296
  363.8 37.2 %collective-permute-start.23 = (bf16[2,72,2592]{2,1,0:T(8,128)(2,1)}, bf16[2,72,2592]{2,1,0:T(8,128)(2,1)}, u32[]{:S(2)}, u32[]{:S(2)}) collective-permute-start(bf16[2,72,2592]{2,1,0:T(8,128)(2,1)} %get-tuple-element.77), channel_id=1, source_target_pairs={{0,3},{1,2},{2,1},{3,0},{4,7},{5,6},{6,5},{7,4},{8,11},{9,10},{10,... | collective-permute-start | bytes 2239496 | tf_op jit(solution)/shard_map/ppermute | solution.py:296
  366.1 34.9 %copy-start.11 = (bf16[2,72,2592]{2,1,0:T(8,128)(2,1)S(1)}, bf16[2,72,2592]{2,1,0:T(8,128)(2,1)}, u32[]{:S(2)}) copy-start(bf16[2,72,2592]{2,1,0:T(8,128)(2,1)} %copy-done.10) | copy-start | bytes 2239492
  366.6 37.3 %collective-permute-start.16 = (bf16[576,960]{1,0:T(8,128)(2,1)S(1)}, bf16[576,960]{1,0:T(8,128)(2,1)S(1)}, u32[]{:S(2)}, u32[]{:S(2)}) collective-permute-start(bf16[576,960]{1,0:T(8,128)(2,1)S(1)} %get-tuple-element.155), channel_id=1, source_target_pairs={{0,8},{8,0},{16,24},{24,16},{32,40},{40,32},{48,56},{56,48},{64,72... | collective-permute-start | bytes 3317768 | tf_op jit(solution)/shard_map/ppermute | solution.py:37
  403.8 8.8 %collective-permute-start.24 = (bf16[72,2592]{1,0:T(8,128)(2,1)}, bf16[72,2592]{1,0:T(8,128)(2,1)}, u32[]{:S(2)}, u32[]{:S(2)}) collective-permute-start(bf16[72,2592]{1,0:T(8,128)(2,1)} %fusion.43), channel_id=1, source_target_pairs={{0,4},{1,5},{2,6},{3,7},{4,0},{5,1},{6,2},{7,3},{8,12},{9,13},{10,... | collective-permute-start | bytes 1119752 | tf_op jit(solution)/shard_map/ppermute | solution.py:296
  405.9 22.3 %all-to-all-start.6 = ((bf16[8,72,964]{2,1,0:T(8,128)(2,1)}), bf16[8,72,964]{2,1,0:T(8,128)(2,1)S(1)}, u32[]{:S(2)}, u32[]{:S(2)}) async-start(bf16[8,72,964]{2,1,0:T(8,128)(2,1)} %bitcast.38), calls=%async_computation.6 | async-start | bytes 2359296 | tf_op jit(solution)/shard_map/all_to_all | solution.py:45
  414.3 18.0 %collective-permute-start.25 = (bf16[72,2592]{1,0:T(8,128)(2,1)}, bf16[72,2592]{1,0:T(8,128)(2,1)S(1)}, u32[]{:S(2)}, u32[]{:S(2)}) collective-permute-start(bf16[72,2592]{1,0:T(8,128)(2,1)} %fusion.7), channel_id=1, source_target_pairs={{0,16},{8,24},{16,0},{24,8},{32,48},{40,56},{48,32},{56,40},{64,80... | collective-permute-start | bytes 1119752 | tf_op jit(solution)/shard_map/ppermute | solution.py:63
  428.4 7.1 %collective-permute-start.17 = (bf16[72,964]{1,0:T(8,128)(2,1)S(1)}, bf16[72,964]{1,0:T(8,128)(2,1)S(1)}, u32[]{:S(2)}, u32[]{:S(2)}) collective-permute-start(bf16[72,964]{1,0:T(8,128)(2,1)S(1)} %reduce_sum.162), channel_id=1, source_target_pairs={{0,16},{8,24},{16,0},{24,8},{32,48},{40,56},{48,32},{56,40},{64,80... | collective-permute-start | bytes 416456 | tf_op jit(solution)/shard_map/ppermute | solution.py:63
  428.6 15.2 %collective-permute-start.29 = (bf16[72,2592]{1,0:T(8,128)(2,1)}, bf16[72,2592]{1,0:T(8,128)(2,1)S(1)}, u32[]{:S(2)}, u32[]{:S(2)}) collective-permute-start(bf16[72,2592]{1,0:T(8,128)(2,1)} %reduce-scatter.4.cloned.1.call-done), channel_id=1, source_target_pairs={{0,16},{8,24},{16,0},{24,8},{32,48},{40,56},{48,32},{56,40},{64,80... | collective-permute-start | bytes 1119752 | tf_op jit(solution)/shard_map/ppermute | solution.py:63
  433.4 11.5 %collective-permute-start.26 = (bf16[72,2592]{1,0:T(8,128)(2,1)S(1)}, bf16[72,2592]{1,0:T(8,128)(2,1)S(1)}, u32[]{:S(2)}, u32[]{:S(2)}) collective-permute-start(bf16[72,2592]{1,0:T(8,128)(2,1)S(1)} %add_convert_fusion.10), channel_id=1, source_target_pairs={{0,32},{8,40},{16,48},{24,56},{32,0},{40,8},{48,16},{56,24},{64,96... | collective-permute-start | bytes 1119752 | tf_op jit(solution)/shard_map/ppermute | solution.py:63
  435.5 12.2 %collective-permute-start.18 = (bf16[72,964]{1,0:T(8,128)(2,1)S(1)}, bf16[72,964]{1,0:T(8,128)(2,1)S(1)}, u32[]{:S(2)}, u32[]{:S(2)}) collective-permute-start(bf16[72,964]{1,0:T(8,128)(2,1)S(1)} %add_convert_fusion.14), channel_id=1, source_target_pairs={{0,32},{8,40},{16,48},{24,56},{32,0},{40,8},{48,16},{56,24},{64,96... | collective-permute-start | bytes 416456 | tf_op jit(solution)/shard_map/ppermute | solution.py:63
  443.9 10.1 %collective-permute-start.30 = (bf16[72,2592]{1,0:T(8,128)(2,1)S(1)}, bf16[72,2592]{1,0:T(8,128)(2,1)S(1)}, u32[]{:S(2)}, u32[]{:S(2)}) collective-permute-start(bf16[72,2592]{1,0:T(8,128)(2,1)S(1)} %add_convert_fusion.7), channel_id=1, source_target_pairs={{0,32},{8,40},{16,48},{24,56},{32,0},{40,8},{48,16},{56,24},{64,96... | collective-permute-start | bytes 1119752 | tf_op jit(solution)/shard_map/ppermute | solution.py:63
  445.0 19.5 %collective-permute-start.27 = (bf16[72,2592]{1,0:T(8,128)(2,1)S(1)}, bf16[72,2592]{1,0:T(8,128)(2,1)S(1)}, u32[]{:S(2)}, u32[]{:S(2)}) collective-permute-start(bf16[72,2592]{1,0:T(8,128)(2,1)S(1)} %add_convert_fusion.9), channel_id=1, source_target_pairs={{0,64},{8,72},{16,80},{24,88},{32,96},{40,104},{48,112},{56,120},{... | collective-permute-start | bytes 1119752 | tf_op jit(solution)/shard_map/ppermute | solution.py:63
  447.7 21.0 %collective-permute-start.19 = (bf16[72,964]{1,0:T(8,128)(2,1)S(1)}, bf16[72,964]{1,0:T(8,128)(2,1)S(1)}, u32[]{:S(2)}, u32[]{:S(2)}) collective-permute-start(bf16[72,964]{1,0:T(8,128)(2,1)S(1)} %add_convert_fusion.13), channel_id=1, source_target_pairs={{0,64},{8,72},{16,80},{24,88},{32,96},{40,104},{48,112},{56,120},{... | collective-permute-start | bytes 416456 | tf_op jit(solution)/shard_map/ppermute | solution.py:63
  454.1 21.8 %collective-permute-start.31 = (bf16[72,2592]{1,0:T(8,128)(2,1)S(1)}, bf16[72,2592]{1,0:T(8,128)(2,1)S(1)}, u32[]{:S(2)}, u32[]{:S(2)}) collective-permute-start(bf16[72,2592]{1,0:T(8,128)(2,1)S(1)} %add_convert_fusion.6), channel_id=1, source_target_pairs={{0,64},{8,72},{16,80},{24,88},{32,96},{40,104},{48,112},{56,120},{... | collective-permute-start | bytes 1119752 | tf_op jit(solution)/shard_map/ppermute | solution.py:63
  464.6 13.8 %collective-permute-start.28 = (bf16[72,2592]{1,0:T(8,128)(2,1)S(1)}, bf16[72,2592]{1,0:T(8,128)(2,1)S(1)}, u32[]{:S(2)}, u32[]{:S(2)}) collective-permute-start(bf16[72,2592]{1,0:T(8,128)(2,1)S(1)} %add_convert_fusion.8.refs_0_), channel_id=1, source_target_pairs={{0,8},{8,0},{16,24},{24,16},{32,40},{40,32},{48,56},{56,48},{64,72... | collective-permute-start | bytes 1119752 | tf_op jit(solution)/shard_map/ppermute | solution.py:37
  468.8 10.1 %collective-permute-start.20 = (bf16[72,964]{1,0:T(8,128)(2,1)S(1)}, bf16[72,964]{1,0:T(8,128)(2,1)S(1)}, u32[]{:S(2)}, u32[]{:S(2)}) collective-permute-start(bf16[72,964]{1,0:T(8,128)(2,1)S(1)} %add_convert_fusion.12.refs_4_), channel_id=1, source_target_pairs={{0,8},{8,0},{16,24},{24,16},{32,40},{40,32},{48,56},{56,48},{64,72... | collective-permute-start | bytes 416456 | tf_op jit(solution)/shard_map/ppermute | solution.py:37
  476.0 3.7 collective-permute-start.32
  (85 other events, 236.4 us)
Sparse Core Ops, SparseCore 0:
  15.9 98.1 all-gather.2
  136.2 63.5 all-gather.4
  320.0 91.2 reduce-scatter.3

commit v6 on v5

--- a/solution.py
+++ b/solution.py
@@ -296,11 +296,13 @@
     return lax.ppermute(x, "fsdp", [(i, i ^ d) for i in range(FSDP)])
 
 
-def scatter_by_permutes(me, x):
+def send_parts(me, x):
     parts = dispatch(me, x.reshape(FSDP, -1, x.shape[1]))
-    total = parts[0].astype(F32)
-    for dx in range(1, 4):
-        total = total + across(parts[dx], dx).astype(F32)
+    return [parts[0]] + [across(parts[dx], dx) for dx in range(1, 4)]
+
+
+def sum_parts(parts):
+    total = sum(p.astype(F32) for p in parts)
     return (total[0] + across(total[1].astype(BF16), 4).astype(F32)).astype(BF16)
 
 
@@ -406,7 +408,7 @@
     first = jnp.broadcast_to(first[None], (FSDP,) + first.shape)
     first, w_gate_up, w_down = lax.optimization_barrier((first, w_gate_up, w_down))
     first = over_fsdp(first).reshape(D, -1)
-    pack0 = jnp.concatenate([wgu_pack(0), wd_pack(0), wd_pack(1)], 1)
+    pack0 = jnp.concatenate([wgu_pack(0), wd_pack(0)], 1)
     pack0 = lax.all_gather(pack0, "fsdp", axis=0, tiled=True)
     pack1 = lax.all_gather(wgu_pack(1), "fsdp", axis=0, tiled=True)
     gains = jnp.transpose(first[:, cut:].astype(F32)).reshape(LAYERS, 2, D)
@@ -442,17 +444,18 @@
         kv_t = kv_t.reshape(1, 2, KV_HEADS, HEAD_DIM, ROWS)
         kv_own = over_chips(jnp.broadcast_to(kv_t, (CTX // 2,) + kv_t.shape[1:]))
         if layer == 0:
-            kv_own, late = lax.optimization_barrier((kv_own, proj_pack(1)))
+            late = jnp.concatenate([proj_pack(1), wd_pack(1)], 1)
+            kv_own, late = lax.optimization_barrier((kv_own, late))
             late = gather_fsdp(late)
         kv_other = to_partner(kv_own)
         o_t, lse = attention(scalars, q_t, kv_own, kv_other)
         if layer == 0:
-            o_t, pack0, late = lax.optimization_barrier((o_t, pack0, late))
-            mlps.append((pack0[:, :FF], pack0[:, FF : FF + HALF].reshape(HALF, D)))
-            projs.append(whole_proj(late))
+            o_t, pack0 = lax.optimization_barrier((o_t, pack0))
+            mlps.append((pack0[:, :FF], pack0[:, FF:].reshape(HALF, D)))
+            projs.append(whole_proj(late[:, :cut]))
         else:
             o_t, pack1 = lax.optimization_barrier((o_t, pack1))
-            mlps.append((pack1, pack0[:, FF + HALF :].reshape(HALF, D)))
+            mlps.append((pack1, late[:, cut:].reshape(HALF, D)))
         attn_out = o_t.astype(BF16).reshape(Q_ROWS, ROWS)
         mid = hidden + ein("at,ad->td", attn_out, wout)
         unit_m, rms_m = normed(mid)
@@ -499,14 +502,14 @@
         wout_theirs = my_half(d_wout[:, wout_half:], d_wout[:, :wout_half])
         d_mlp = [d_wgu, d_wdown.reshape(D, HALF), sum_pair(wout_mine, to_partner(wout_theirs))]
         d_mlp = jnp.concatenate(d_mlp, 1)
-        if layer == 0:
-            share1 = sum_chips(lax.optimization_barrier((share1, dkv))[0])
         dkv = jnp.sum(over_chips(dkv).astype(F32), 0)
-        dkv, d_mlp = lax.optimization_barrier((dkv, d_mlp))
         if layer == 1:
+            dkv, d_mlp = lax.optimization_barrier((dkv, d_mlp))
             share1 = lax.psum_scatter(d_mlp, "fsdp", scatter_dimension=0, tiled=True)
         else:
-            share0 = scatter_by_permutes(me, d_mlp)
+            dkv, d_mlp, share1 = lax.optimization_barrier((dkv, d_mlp, share1))
+            parts = send_parts(me, d_mlp)
+            share1 = sum_chips(share1)
         turned = jnp.concatenate([dq_t, dkv[0]], 0)
         d_qkv = jnp.concatenate([rotate(turned, cosine, -sine), dkv[1]], 0)
         d_qkv = d_qkv.astype(BF16).reshape(Q_ROWS + KV_ROWS, ROWS)
@@ -521,6 +524,7 @@
     mine, theirs = in_order(*qkv_grads)
     d_gains = jnp.transpose(jnp.stack(gain_grads).reshape(2 * LAYERS, D)).astype(BF16)
     d_wqkv = jnp.concatenate([sum_pair(mine, to_partner(theirs)), d_gains], 1)
+    share0 = sum_parts(lax.optimization_barrier((parts, d_wqkv))[0])
     qkv = sum_chips(scatter_fsdp(d_wqkv))
     qkv_p = to_partner(qkv)
 

time: 500 us -> 520 us (1.040)
  waiting for transfers between devices: 166 us -> 177 us
    optimization_barrier x1, waiting for transfers between devices: 0.02 us -> 22 us  [local(): dkv, d_mlp, share1 = lax.optimization_barrier((dkv, d_mlp, share1))]
    all_to_all x3, waiting for transfers between devices: 32 us -> 12.4 us  [over_fsdp(): return lax.all_to_all(x, 'fsdp', 0, 0, tiled=True)]
    ppermute x9, waiting for transfers between devices: 28.6 us -> 39.4 us  [sum_chips(): x = sum_pair(x, lax.ppermute(x, 'ctx', [(i, i ^ bit) for i in range(CTX)]))]
    unnamed x182 -> x164, local copies, waits for them, and re-layouts: 17 us -> 13.7 us
  transfers between devices with their start and end apart: 42 -> 42, of which waited for: 24 -> 28; matrix products, arithmetic and copies ran while one was open for 17% -> 19% of each run, Pallas kernels for 7% -> 11%
where the time goes in v6:
time: 520 us; the launch traced here: 510 us
  waiting for transfers between devices  177 us (34%)
  Pallas kernels  78.6 us (15%)
  starting transfers between devices  71.5 us (14%)
  local copies, waits for them, and re-layouts  51.4 us (10%)
  other arithmetic  51.4 us (10%)
  matrix products  36.6 us (7%)
  blocking collectives  25 us (5%)
  between operations  18.3 us (4%)
    all_to_all x3, waiting for transfers between devices, over_chips(): lax.all_to_all(x, 'ctx', 0, 0, axis_index_groups=SAME_CORE, tiled=True)  45.3 us
    pallas_call x2, Pallas kernels, attention_back(): pl.pallas_call(backward_kernel, grid_spec=pltpu.PrefetchScalarGridSpec(nu...  44 us
    ppermute x9, waiting for transfers between devices, sum_chips(): x = sum_pair(x, lax.ppermute(x, 'ctx', [(i, i ^ bit) for i in range(CTX)]))  39.4 us
    ppermute x4, waiting for transfers between devices, across(): return lax.ppermute(x, 'fsdp', [(i, i ^ d) for i in range(FSDP)])  35.9 us
    pallas_call x2, Pallas kernels, attention(): pl.pallas_call(forward_kernel, grid_spec=pltpu.PrefetchScalarGridSpec(num...  30.9 us
    dot_general x18, matrix products, ein(): return jnp.einsum(spec, a, b, preferred_element_type=F32)  28.1 us
    all_to_all x1, blocking collectives, over_chips(): lax.all_to_all(x, 'ctx', 0, 0, axis_index_groups=SAME_CORE, tiled=True)  25 us
    ppermute x20, starting transfers between devices, to_partner(): return lax.ppermute(x, 'ctx', PARTNER)  23.7 us
  transfers between devices with their start and end apart: 42, of which 28 were waited for; matrix products, arithmetic and copies ran while one was open for 19% of the time, Pallas kernels for 11%

profile of v6, /device:TPU:1, one launch (start us, length us, event | category | flops | bytes accessed | tf_op | source)
XLA Modules:
  0.0 510.0 jit_solution(14979485896618508071)
XLA Ops:
  11.7 8.3 %all-to-all-start = ((bf16[8,72,772]{2,1,0:T(8,128)(2,1)}), bf16[8,72,772]{2,1,0:T(8,128)(2,1)S(1)}, u32[]{:S(2)}, u32[]{:S(2)}) async-start(bf16[8,72,772]{2,1,0:T(8,128)(2,1)} %broadcast_in_dim.16), calls=%async_computation | async-start | bytes 2064384 | tf_op jit(solution)/shard_map/all_to_all | solution.py:45
  25.8 11.4 %all-to-all-done = bf16[8,72,772]{2,1,0:T(8,128)(2,1)S(1)} async-done(((bf16[8,72,772]{2,1,0:T(8,128)(2,1)}), bf16[8,72,772]{2,1,0:T(8,128)(2,1)S(1)}, u32[]{:S(2)}, u32[]{:S(2)}) %all-to-all-start) | async-done | bytes 889376 | tf_op jit(solution)/shard_map/all_to_all | solution.py:45
  45.3 4.8 all-to-all-start.1
  50.4 23.2 %all-to-all-done.1.own_ref = bf16[8,2,3,64,256]{4,3,2,1,0:T(8,128)(2,1)S(1)} async-done(((bf16[8,2,3,64,256]{4,3,2,1,0:T(8,128)(2,1)}), bf16[8,2,3,64,256]{4,3,2,1,0:T(8,128)(2,1)S(1)}, u32[]{:S(2)}, u32[]{:S(2)}) %all-to-all-start.1) | async-done | bytes 1572896 | tf_op jit(solution)/shard_map/all_to_all | solution.py:41
  76.2 4.5 all-to-all-start.2
  84.1 15.5 %attention.2 = (f32[9,64,256]{2,1,0:T(8,128)S(1)}, f32[3,2,1,384]{3,2,1,0:T(1,128)S(1)}) custom-call(s32[39]{0:T(128)S(1)} %concatenate.93.sc, bf16[9,64,256]{2,1,0:T(8,128)(2,1)S(1)} %fusion.33.q_ref, bf16[8,2,3,64,256]{4,3,2,1,0:T(8,128)(2,1)S(1)} %all-to-all-done.1.own_ref, bf16[8,2,3,64,256]{4,3,2,1,0:T(8,128)(2,1)S(1)} %collective-permute-done.1.other_ref), custom_call_target="tpu_custom_call" | custom-call | tf_op jit(solution)/shard_map/attention/pallas_call | solution.py:225
  100.5 3.5 all-gather.3.cloned.1.call-done
  105.1 2.3 multiply_reduce_fusion.8
  115.3 3.4 reshape.318
  118.8 3.1 fusion.4
  129.5 3.0 broadcast_select_fusion.2
  134.8 25.0 %all_to_all.35.own_ref = bf16[8,2,3,64,256]{4,3,2,1,0:T(8,128)(2,1)S(1)} all-to-all(bf16[8,2,3,64,256]{4,3,2,1,0:T(8,128)(2,1)S(1)} %broadcast_in_dim.21), channel_id=1, replica_groups={{0,16,32,48,64,80,96,112},{8,24,40,56,72,88,104,120},{1,17,33,49,65,81,..., dimensions={0} | all-to-all | bytes 3145728 | tf_op jit(solution)/shard_map/all_to_all | solution.py:41
  161.0 3.0 collective-permute-done.5.other_ref
  164.0 15.5 %attention.3 = (f32[9,64,256]{2,1,0:T(8,128)S(1)}, f32[3,2,1,384]{3,2,1,0:T(1,128)S(1)}) custom-call(s32[39]{0:T(128)S(1)} %concatenate.93.sc, bf16[9,64,256]{2,1,0:T(8,128)(2,1)S(1)} %fusion.30.q_ref, bf16[8,2,3,64,256]{4,3,2,1,0:T(8,128)(2,1)S(1)} %all_to_all.35.own_ref, bf16[8,2,3,64,256]{4,3,2,1,0:T(8,128)(2,1)S(1)} %collective-permute-done.5.other_ref), custom_call_target="tpu_custom_call" | custom-call | tf_op jit(solution)/shard_map/attention/pallas_call | solution.py:225
  182.2 9.8 %all-gather.5.cloned.1.call-done = bf16[576,1536]{1,0:T(8,128)(2,1)} async-done(((bf16[72,1536]{1,0:T(8,128)(2,1)}), bf16[576,1536]{1,0:T(8,128)(2,1)}) %all-gather.5.cloned.1.call-update) | async-done | bytes 1769488 | tf_op jit(solution)/shard_map/all_gather | solution.py:413
  193.1 2.4 multiply_reduce_fusion.6
  199.2 3.4 reshape.321
  202.6 3.1 fusion.71
  205.8 2.4 multiply_convert_fusion.3
  212.6 2.2 fusion.75
  216.4 22.0 %attention_back.2 = (f32[9,64,256]{2,1,0:T(8,128)S(1)}, bf16[8,2,3,64,256]{4,3,2,1,0:T(8,128)(2,1)S(1)}, bf16[8,2,3,64,256]{4,3,2,1,0:T(8,128)(2,1)S(1)}) custom-call(s32[39]{0:T(128)S(1)} %concatenate.93.sc, bf16[9,64,256]{2,1,0:T(8,128)(2,1)S(1)} %copy-done.5, bf16[8,2,3,64,256]{4,3,2,1,0:T(8,128)(2,1)S(1)} %all_to_all.35.own_ref, ...), custom_call_target="tpu_custom_call" | custom-call | tf_op jit(solution)/shard_map/attention_back/pallas_call | solution.py:248
  243.7 4.4 all-to-all-start.4
  253.0 2.5 reshape.324
  255.5 2.7 convolution_convert_fusion.1
  261.3 10.4 %all-to-all-done.4 = bf16[8,2,3,64,256]{4,3,2,1,0:T(8,128)(2,1)} async-done(((bf16[8,2,3,64,256]{4,3,2,1,0:T(8,128)(2,1)}), bf16[8,2,3,64,256]{4,3,2,1,0:T(8,128)(2,1)}, u32[]{:S(2)}, u32[]{:S(2)}) %all-to-all-start.4) | async-done | bytes 1572896 | tf_op jit(solution)/shard_map/all_to_all | solution.py:41
  280.4 3.2 multiply_convert_fusion.1
  289.0 22.0 %attention_back.3 = (f32[9,64,256]{2,1,0:T(8,128)S(1)}, bf16[8,2,3,64,256]{4,3,2,1,0:T(8,128)(2,1)S(1)}, bf16[8,2,3,64,256]{4,3,2,1,0:T(8,128)(2,1)S(1)}) custom-call(s32[39]{0:T(128)S(1)} %concatenate.93.sc, bf16[9,64,256]{2,1,0:T(8,128)(2,1)S(1)} %fusion.33.q_ref, bf16[8,2,3,64,256]{4,3,2,1,0:T(8,128)(2,1)S(1)} %all-to-all-done.1.own_ref, ...), custom_call_target="tpu_custom_call" | custom-call | tf_op jit(solution)/shard_map/attention_back/pallas_call | solution.py:248
  316.3 4.4 all-to-all-start.5
  322.7 2.6 convolution_convert_fusion.4
  326.9 2.2 reshape.326
  333.0 11.7 %all-to-all-done.5 = bf16[8,2,3,64,256]{4,3,2,1,0:T(8,128)(2,1)} async-done(((bf16[8,2,3,64,256]{4,3,2,1,0:T(8,128)(2,1)}), bf16[8,2,3,64,256]{4,3,2,1,0:T(8,128)(2,1)}, u32[]{:S(2)}, u32[]{:S(2)}) %all-to-all-start.5) | async-done | bytes 1572896 | tf_op jit(solution)/shard_map/all_to_all | solution.py:41
  344.7 2.4 convert_reduce_fusion
  347.1 22.0 %reduce-scatter.4.cloned.1.call-done = bf16[72,2592]{1,0:T(8,128)(2,1)} async-done(((bf16[576,2592]{1,0:T(8,128)(2,1)}), bf16[72,2592]{1,0:T(8,128)(2,1)}) %reduce-scatter.4.cloned.1.call-update) | async-done | bytes 373264 | tf_op jit(solution)/shard_map/optimization_barrier | solution.py:510
  375.6 2.6 collective-permute-start.16
  380.8 2.4 collective-permute-start.22
  388.0 11.1 %collective-permute-done.21 = bf16[2,72,2592]{2,1,0:T(8,128)(2,1)} collective-permute-done((bf16[2,72,2592]{2,1,0:T(8,128)(2,1)}, bf16[2,72,2592]{2,1,0:T(8,128)(2,1)}, u32[]{:S(2)}, u32[]{:S(2)}) %collective-permute-start.21) | collective-permute-done | bytes 746528 | tf_op jit(solution)/shard_map/ppermute | solution.py:296
  399.1 18.5 %collective-permute-done.22 = bf16[2,72,2592]{2,1,0:T(8,128)(2,1)} collective-permute-done((bf16[2,72,2592]{2,1,0:T(8,128)(2,1)}, bf16[2,72,2592]{2,1,0:T(8,128)(2,1)}, u32[]{:S(2)}, u32[]{:S(2)}) %collective-permute-start.22) | collective-permute-done | bytes 746528 | tf_op jit(solution)/shard_map/ppermute | solution.py:296
  424.7 4.1 all-to-all-start.6
  428.9 4.4 collective-permute-done.24
  434.7 14.6 %collective-permute-done.29 = bf16[72,2592]{1,0:T(8,128)(2,1)} collective-permute-done((bf16[72,2592]{1,0:T(8,128)(2,1)}, bf16[72,2592]{1,0:T(8,128)(2,1)}, u32[]{:S(2)}, u32[]{:S(2)}) %collective-permute-start.29) | collective-permute-done | bytes 373280 | tf_op jit(solution)/shard_map/ppermute | solution.py:63
  451.9 8.8 %collective-permute-done.25 = bf16[72,2592]{1,0:T(8,128)(2,1)S(1)} collective-permute-done((bf16[72,2592]{1,0:T(8,128)(2,1)S(1)}, bf16[72,2592]{1,0:T(8,128)(2,1)S(1)}, u32[]{:S(2)}, u32[]{:S(2)}) %collective-permute-start.25) | collective-permute-done | bytes 373280 | tf_op jit(solution)/shard_map/ppermute | solution.py:63
  462.9 2.5 collective-permute-start.31
  469.1 2.8 collective-permute-start.27
  471.9 8.5 %collective-permute-done.18 = bf16[72,964]{1,0:T(8,128)(2,1)S(1)} collective-permute-done((bf16[72,964]{1,0:T(8,128)(2,1)S(1)}, bf16[72,964]{1,0:T(8,128)(2,1)S(1)}, u32[]{:S(2)}, u32[]{:S(2)}) %collective-permute-start.18) | collective-permute-done | bytes 138848 | tf_op jit(solution)/shard_map/ppermute | solution.py:63
  480.5 3.1 collective-permute-start.19
  483.7 6.5 %collective-permute-start.32 = (bf16[72,2592]{1,0:T(8,128)(2,1)S(1)}, bf16[72,2592]{1,0:T(8,128)(2,1)S(1)}, u32[]{:S(2)}, u32[]{:S(2)}) collective-permute-start(bf16[72,2592]{1,0:T(8,128)(2,1)S(1)} %add_convert_fusion.5.refs_2_), channel_id=1, source_target_pairs={{0,8},{8,0},{16,24},{24,16},{32,40},{40,32},{48,56},{56,48},{64,72... | collective-permute-start | bytes 1119752 | tf_op jit(solution)/shard_map/ppermute | solution.py:37
  490.3 3.9 collective-permute-done.19
  494.2 3.4 collective-permute-start.20
  (373 shorter events, 132.2 us)
Async XLA Ops:
  11.7 25.4 %all-to-all-start = ((bf16[8,72,772]{2,1,0:T(8,128)(2,1)}), bf16[8,72,772]{2,1,0:T(8,128)(2,1)S(1)}, u32[]{:S(2)}, u32[]{:S(2)}) async-start(bf16[8,72,772]{2,1,0:T(8,128)(2,1)} %broadcast_in_dim.16), calls=%async_computation | async-start | bytes 2064384 | tf_op jit(solution)/shard_map/all_to_all | solution.py:45
  20.0 83.9 %all-gather.3.cloned.1.call-start = ((), (), s32[]{:S(2)}) async-start(), calls=%async_computation.8 | async-start | bytes 2985984 | tf_op jit(solution)/shard_map/all_gather | solution.py:412
  37.2 3.1 collective-permute-start
  45.3 28.3 %all-to-all-start.1 = ((bf16[8,2,3,64,256]{4,3,2,1,0:T(8,128)(2,1)}), bf16[8,2,3,64,256]{4,3,2,1,0:T(8,128)(2,1)S(1)}, u32[]{:S(2)}, u32[]{:S(2)}) async-start(bf16[8,2,3,64,256]{4,3,2,1,0:T(8,128)(2,1)} %broadcast_in_dim.19), calls=%async_computation.1 | async-start | bytes 3145728 | tf_op jit(solution)/shard_map/all_to_all | solution.py:41
  73.6 10.6 %collective-permute-start.1 = (bf16[8,2,3,64,256]{4,3,2,1,0:T(8,128)(2,1)S(1)}, bf16[8,2,3,64,256]{4,3,2,1,0:T(8,128)(2,1)S(1)}, u32[]{:S(2)}, u32[]{:S(2)}) collective-permute-start(bf16[8,2,3,64,256]{4,3,2,1,0:T(8,128)(2,1)S(1)} %all-to-all-done.1.own_ref), channel_id=1, source_target_pairs={{0,8},{8,0},{16,24},{24,16},{32,40},{40,32},{48,56},{56,48},{64,72... | collective-permute-start | bytes 4718600 | tf_op jit(solution)/shard_map/ppermute | solution.py:37
  76.2 34.4 %all-to-all-start.2 = ((bf16[8,72,1536]{2,1,0:T(8,128)(2,1)}), bf16[8,72,1536]{2,1,0:T(8,128)(2,1)}, u32[]{:S(2)}, u32[]{:S(2)}) async-start(bf16[8,72,1536]{2,1,0:T(8,128)(2,1)} %broadcast_in_dim.20), calls=%async_computation.2 | async-start | bytes 3538944 | tf_op jit(solution)/shard_map/all_to_all | solution.py:45
  80.7 111.3 %all-gather.5.cloned.1.call-start = ((), (), s32[]{:S(2)}) async-start(), calls=%async_computation.9 | async-start | bytes 1990656 | tf_op jit(solution)/shard_map/all_gather | solution.py:413
  84.1 15.5 %copy-start = (bf16[8,2,3,64,256]{4,3,2,1,0:T(8,128)(2,1)}, bf16[8,2,3,64,256]{4,3,2,1,0:T(8,128)(2,1)S(1)}, u32[]{:S(2)}) copy-start(bf16[8,2,3,64,256]{4,3,2,1,0:T(8,128)(2,1)S(1)} %collective-permute-done.1.other_ref) | copy-start | bytes 4718596
  107.4 20.9 %copy-start.20 = (f32[256,576]{0,1:T(8,128)}, f32[256,576]{0,1:T(8,128)S(1)}, u32[]{:S(2)}) copy-start(f32[256,576]{0,1:T(8,128)S(1)} %get-tuple-element.155) | copy-start | bytes 1769476
  108.3 10.5 %collective-permute-start.2 = (bf16[256,576]{0,1:T(8,128)(2,1)}, bf16[256,576]{0,1:T(8,128)(2,1)}, u32[]{:S(2)}, u32[]{:S(2)}) collective-permute-start(bf16[256,576]{0,1:T(8,128)(2,1)} %multiply_convert_fusion.8), channel_id=1, source_target_pairs={{0,8},{8,0},{16,24},{24,16},{32,40},{40,32},{48,56},{56,48},{64,72... | collective-permute-start | bytes 884744 | tf_op jit(solution)/shard_map/ppermute | solution.py:37
  112.8 16.7 %collective-permute-start.4 = (bf16[576,768]{1,0:T(8,128)(2,1)}, bf16[576,768]{1,0:T(8,128)(2,1)}, u32[]{:S(2)}, u32[]{:S(2)}) collective-permute-start(bf16[576,768]{1,0:T(8,128)(2,1)} %slice.361), channel_id=1, source_target_pairs={{0,8},{8,0},{16,24},{24,16},{32,40},{40,32},{48,56},{56,48},{64,72... | collective-permute-start | bytes 2654216 | tf_op jit(solution)/shard_map/ppermute | solution.py:37
  126.2 2.0 collective-permute-start.3
  159.8 4.2 collective-permute-start.5
  197.1 5.5 %collective-permute-start.6 = (bf16[256,576]{0,1:T(8,128)(2,1)}, bf16[256,576]{0,1:T(8,128)(2,1)}, u32[]{:S(2)}, u32[]{:S(2)}) collective-permute-start(bf16[256,576]{0,1:T(8,128)(2,1)} %multiply_convert_fusion.6), channel_id=1, source_target_pairs={{0,8},{8,0},{16,24},{24,16},{32,40},{40,32},{48,56},{56,48},{64,72... | collective-permute-start | bytes 884744 | tf_op jit(solution)/shard_map/ppermute | solution.py:37
  199.2 6.6 %collective-permute-start.8 = (bf16[256,576]{0,1:T(8,128)(2,1)}, bf16[256,576]{0,1:T(8,128)(2,1)}, u32[]{:S(2)}, u32[]{:S(2)}) collective-permute-start(bf16[256,576]{0,1:T(8,128)(2,1)} %bitcast.24), channel_id=1, source_target_pairs={{0,8},{8,0},{16,24},{24,16},{32,40},{40,32},{48,56},{56,48},{64,72... | collective-permute-start | bytes 884744 | tf_op jit(solution)/shard_map/ppermute | solution.py:37
  209.5 1.8 collective-permute-start.9
  210.8 1.8 collective-permute-start.7
  214.8 23.5 %copy-start.49 = (bf16[256,576]{0,1:T(8,128)(2,1)}, bf16[256,576]{0,1:T(8,128)(2,1)S(1)}, u32[]{:S(2)}) copy-start(bf16[256,576]{0,1:T(8,128)(2,1)S(1)} %get-tuple-element.65) | copy-start | bytes 884740
  238.4 3.5 collective-permute-start.10
  243.7 28.0 %all-to-all-start.4 = ((bf16[8,2,3,64,256]{4,3,2,1,0:T(8,128)(2,1)}), bf16[8,2,3,64,256]{4,3,2,1,0:T(8,128)(2,1)}, u32[]{:S(2)}, u32[]{:S(2)}) async-start(bf16[8,2,3,64,256]{4,3,2,1,0:T(8,128)(2,1)} %add_convert_fusion.1), calls=%async_computation.4 | async-start | bytes 3145728 | tf_op jit(solution)/shard_map/all_to_all | solution.py:41
  248.1 121.0 %reduce-scatter.4.cloned.1.call-start = ((), (), s32[]{:S(2)}) async-start(), calls=%async_computation.10 | async-start | bytes 3483648
  249.6 8.6 %collective-permute-start.11 = (bf16[576,288]{1,0:T(8,128)(2,1)}, bf16[576,288]{1,0:T(8,128)(2,1)}, u32[]{:S(2)}, u32[]{:S(2)}) collective-permute-start(bf16[576,288]{1,0:T(8,128)(2,1)} %broadcast_select_fusion.6), channel_id=1, source_target_pairs={{0,8},{8,0},{16,24},{24,16},{32,40},{40,32},{48,56},{56,48},{64,72... | collective-permute-start | bytes 995336 | tf_op jit(solution)/shard_map/ppermute | solution.py:37
  277.3 3.1 collective-permute-start.12
  284.9 1.7 collective-permute-start.13
  311.0 3.5 collective-permute-start.14
  316.3 28.4 %all-to-all-start.5 = ((bf16[8,2,3,64,256]{4,3,2,1,0:T(8,128)(2,1)}), bf16[8,2,3,64,256]{4,3,2,1,0:T(8,128)(2,1)}, u32[]{:S(2)}, u32[]{:S(2)}) async-start(bf16[8,2,3,64,256]{4,3,2,1,0:T(8,128)(2,1)} %add_convert_fusion), calls=%async_computation.5 | async-start | bytes 3145728 | tf_op jit(solution)/shard_map/all_to_all | solution.py:41
  322.2 9.1 %collective-permute-start.15 = (bf16[576,288]{1,0:T(8,128)(2,1)}, bf16[576,288]{1,0:T(8,128)(2,1)}, u32[]{:S(2)}, u32[]{:S(2)}) collective-permute-start(bf16[576,288]{1,0:T(8,128)(2,1)} %broadcast_select_fusion.5), channel_id=1, source_target_pairs={{0,8},{8,0},{16,24},{24,16},{32,40},{40,32},{48,56},{56,48},{64,72... | collective-permute-start | bytes 995336 | tf_op jit(solution)/shard_map/ppermute | solution.py:37
  347.1 26.0 %copy-start.39 = (bf16[1,256,576]{1,2,0:T(8,128)(2,1)S(1)}, bf16[1,256,576]{1,2,0:T(8,128)(2,1)}, u32[]{:S(2)}) copy-start(bf16[1,256,576]{1,2,0:T(8,128)(2,1)} %param.9) | copy-start | bytes 884740
  347.1 26.0 %copy-start.75 = (f32[256]{0:T(256)S(1)}, f32[256]{0:T(256)}, u32[]{:S(2)}) copy-start(f32[256]{0:T(256)} %copy-done.74) | copy-start | bytes 3076
  375.6 9.0 %collective-permute-start.16 = (bf16[576,960]{1,0:T(8,128)(2,1)}, bf16[576,960]{1,0:T(8,128)(2,1)}, u32[]{:S(2)}, u32[]{:S(2)}) collective-permute-start(bf16[576,960]{1,0:T(8,128)(2,1)} %get-tuple-element.160), channel_id=1, source_target_pairs={{0,8},{8,0},{16,24},{24,16},{32,40},{40,32},{48,56},{56,48},{64,72... | collective-permute-start | bytes 3317768 | tf_op jit(solution)/shard_map/ppermute | solution.py:37
  379.9 19.2 %collective-permute-start.21 = (bf16[2,72,2592]{2,1,0:T(8,128)(2,1)}, bf16[2,72,2592]{2,1,0:T(8,128)(2,1)}, u32[]{:S(2)}, u32[]{:S(2)}) collective-permute-start(bf16[2,72,2592]{2,1,0:T(8,128)(2,1)} %get-tuple-element.78), channel_id=1, source_target_pairs={{0,1},{1,0},{2,3},{3,2},{4,5},{5,4},{6,7},{7,6},{8,9},{9,8},{10,11... | collective-permute-start | bytes 2239496 | tf_op jit(solution)/shard_map/ppermute | solution.py:296
  380.8 36.8 %collective-permute-start.22 = (bf16[2,72,2592]{2,1,0:T(8,128)(2,1)}, bf16[2,72,2592]{2,1,0:T(8,128)(2,1)}, u32[]{:S(2)}, u32[]{:S(2)}) collective-permute-start(bf16[2,72,2592]{2,1,0:T(8,128)(2,1)} %get-tuple-element.79), channel_id=1, source_target_pairs={{0,2},{1,3},{2,0},{3,1},{4,6},{5,7},{6,4},{7,5},{8,10},{9,11},{10,... | collective-permute-start | bytes 2239496 | tf_op jit(solution)/shard_map/ppermute | solution.py:296
  383.2 36.4 %collective-permute-start.23 = (bf16[2,72,2592]{2,1,0:T(8,128)(2,1)}, bf16[2,72,2592]{2,1,0:T(8,128)(2,1)}, u32[]{:S(2)}, u32[]{:S(2)}) collective-permute-start(bf16[2,72,2592]{2,1,0:T(8,128)(2,1)} %get-tuple-element.80), channel_id=1, source_target_pairs={{0,3},{1,2},{2,1},{3,0},{4,7},{5,6},{6,5},{7,4},{8,11},{9,10},{10,... | collective-permute-start | bytes 2239496 | tf_op jit(solution)/shard_map/ppermute | solution.py:296
  386.8 32.7 %copy-start.11 = (bf16[2,72,2592]{2,1,0:T(8,128)(2,1)S(1)}, bf16[2,72,2592]{2,1,0:T(8,128)(2,1)}, u32[]{:S(2)}) copy-start(bf16[2,72,2592]{2,1,0:T(8,128)(2,1)} %copy-done.10) | copy-start | bytes 2239492
  422.4 10.8 %collective-permute-start.24 = (bf16[72,2592]{1,0:T(8,128)(2,1)}, bf16[72,2592]{1,0:T(8,128)(2,1)}, u32[]{:S(2)}, u32[]{:S(2)}) collective-permute-start(bf16[72,2592]{1,0:T(8,128)(2,1)} %fusion.43), channel_id=1, source_target_pairs={{0,4},{1,5},{2,6},{3,7},{4,0},{5,1},{6,2},{7,3},{8,12},{9,13},{10,... | collective-permute-start | bytes 1119752 | tf_op jit(solution)/shard_map/ppermute | solution.py:296
  422.4 27.0 %collective-permute-start.29 = (bf16[72,2592]{1,0:T(8,128)(2,1)}, bf16[72,2592]{1,0:T(8,128)(2,1)}, u32[]{:S(2)}, u32[]{:S(2)}) collective-permute-start(bf16[72,2592]{1,0:T(8,128)(2,1)} %reduce-scatter.4.cloned.1.call-done), channel_id=1, source_target_pairs={{0,16},{8,24},{16,0},{24,8},{32,48},{40,56},{48,32},{56,40},{64,80... | collective-permute-start | bytes 1119752 | tf_op jit(solution)/shard_map/ppermute | solution.py:63
  424.7 37.4 %all-to-all-start.6 = ((bf16[8,72,964]{2,1,0:T(8,128)(2,1)}), bf16[8,72,964]{2,1,0:T(8,128)(2,1)S(1)}, u32[]{:S(2)}, u32[]{:S(2)}) async-start(bf16[8,72,964]{2,1,0:T(8,128)(2,1)} %bitcast.38), calls=%async_computation.6 | async-start | bytes 2359296 | tf_op jit(solution)/shard_map/all_to_all | solution.py:45
  434.3 26.4 %collective-permute-start.25 = (bf16[72,2592]{1,0:T(8,128)(2,1)S(1)}, bf16[72,2592]{1,0:T(8,128)(2,1)S(1)}, u32[]{:S(2)}, u32[]{:S(2)}) collective-permute-start(bf16[72,2592]{1,0:T(8,128)(2,1)S(1)} %fusion.7), channel_id=1, source_target_pairs={{0,16},{8,24},{16,0},{24,8},{32,48},{40,56},{48,32},{56,40},{64,80... | collective-permute-start | bytes 1119752 | tf_op jit(solution)/shard_map/ppermute | solution.py:63
  450.6 12.2 %collective-permute-start.30 = (bf16[72,2592]{1,0:T(8,128)(2,1)S(1)}, bf16[72,2592]{1,0:T(8,128)(2,1)S(1)}, u32[]{:S(2)}, u32[]{:S(2)}) collective-permute-start(bf16[72,2592]{1,0:T(8,128)(2,1)S(1)} %add_convert_fusion.7), channel_id=1, source_target_pairs={{0,32},{8,40},{16,48},{24,56},{32,0},{40,8},{48,16},{56,24},{64,96... | collective-permute-start | bytes 1119752 | tf_op jit(solution)/shard_map/ppermute | solution.py:63
  460.8 8.2 %collective-permute-start.26 = (bf16[72,2592]{1,0:T(8,128)(2,1)S(1)}, bf16[72,2592]{1,0:T(8,128)(2,1)S(1)}, u32[]{:S(2)}, u32[]{:S(2)}) collective-permute-start(bf16[72,2592]{1,0:T(8,128)(2,1)S(1)} %add_convert_fusion.10), channel_id=1, source_target_pairs={{0,32},{8,40},{16,48},{24,56},{32,0},{40,8},{48,16},{56,24},{64,96... | collective-permute-start | bytes 1119752 | tf_op jit(solution)/shard_map/ppermute | solution.py:63
  462.4 4.4 collective-permute-start.17
  462.9 20.7 %collective-permute-start.31 = (bf16[72,2592]{1,0:T(8,128)(2,1)S(1)}, bf16[72,2592]{1,0:T(8,128)(2,1)S(1)}, u32[]{:S(2)}, u32[]{:S(2)}) collective-permute-start(bf16[72,2592]{1,0:T(8,128)(2,1)S(1)} %add_convert_fusion.6), channel_id=1, source_target_pairs={{0,64},{8,72},{16,80},{24,88},{32,96},{40,104},{48,112},{56,120},{... | collective-permute-start | bytes 1119752 | tf_op jit(solution)/shard_map/ppermute | solution.py:63
  466.8 13.7 %collective-permute-start.18 = (bf16[72,964]{1,0:T(8,128)(2,1)S(1)}, bf16[72,964]{1,0:T(8,128)(2,1)S(1)}, u32[]{:S(2)}, u32[]{:S(2)}) collective-permute-start(bf16[72,964]{1,0:T(8,128)(2,1)S(1)} %add_convert_fusion.14), channel_id=1, source_target_pairs={{0,32},{8,40},{16,48},{24,56},{32,0},{40,8},{48,16},{56,24},{64,96... | collective-permute-start | bytes 416456 | tf_op jit(solution)/shard_map/ppermute | solution.py:63
  469.1 28.4 %collective-permute-start.27 = (bf16[72,2592]{1,0:T(8,128)(2,1)S(1)}, bf16[72,2592]{1,0:T(8,128)(2,1)S(1)}, u32[]{:S(2)}, u32[]{:S(2)}) collective-permute-start(bf16[72,2592]{1,0:T(8,128)(2,1)S(1)} %add_convert_fusion.9), channel_id=1, source_target_pairs={{0,64},{8,72},{16,80},{24,88},{32,96},{40,104},{48,112},{56,120},{... | collective-permute-start | bytes 1119752 | tf_op jit(solution)/shard_map/ppermute | solution.py:63
  480.5 13.6 %collective-permute-start.19 = (bf16[72,964]{1,0:T(8,128)(2,1)S(1)}, bf16[72,964]{1,0:T(8,128)(2,1)S(1)}, u32[]{:S(2)}, u32[]{:S(2)}) collective-permute-start(bf16[72,964]{1,0:T(8,128)(2,1)S(1)} %add_convert_fusion.13), channel_id=1, source_target_pairs={{0,64},{8,72},{16,80},{24,88},{32,96},{40,104},{48,112},{56,120},{... | collective-permute-start | bytes 416456 | tf_op jit(solution)/shard_map/ppermute | solution.py:63
  483.7 14.0 %collective-permute-start.32 = (bf16[72,2592]{1,0:T(8,128)(2,1)S(1)}, bf16[72,2592]{1,0:T(8,128)(2,1)S(1)}, u32[]{:S(2)}, u32[]{:S(2)}) collective-permute-start(bf16[72,2592]{1,0:T(8,128)(2,1)S(1)} %add_convert_fusion.5.refs_2_), channel_id=1, source_target_pairs={{0,8},{8,0},{16,24},{24,16},{32,40},{40,32},{48,56},{56,48},{64,72... | collective-permute-start | bytes 1119752 | tf_op jit(solution)/shard_map/ppermute | solution.py:37
  494.2 4.4 collective-permute-start.20
  497.7 1.8 collective-permute-start.28
  (76 other events, 222.8 us)
Sparse Core Ops, SparseCore 0:
  23.9 80.0 all-gather.2
  128.4 63.5 all-gather.4
  279.0 90.0 reduce-scatter.3
